TPU v7x, 128 devices: a whole 4x4x4 slice. The times are simulated.
128 devices in a mesh: pipe: 2 (over core), ctx: 16 (over y, x), dp: 4 (over z).
Axes of the slice: x: 4, y: 4, z: 4, core: 2. Of those that a mesh axis runs over, the one named last changes fastest.
Arguments:
- queries: bfloat16 [2, 4, 2048, 2048], P('pipe', 'dp', 'ctx'), may hold values from -16 to 16
- key_rows: bfloat16 [2, 4, 2048, 512], P('pipe', 'dp', 'ctx'), may hold values from -8 to 8
- layer_value_rows: bfloat16 [2, 4, 2048, 512], P('pipe', 'dp', 'ctx'), may hold values from -6 to 6
- prior_output: bfloat16 [2, 4, 2048, 2048], P('pipe', 'dp', 'ctx'), may hold values from -3 to 3
- later_grad: bfloat16 [2, 4, 2048, 2048], P('pipe', 'dp', 'ctx'), may hold values from -6 to 6
- block_order: int32 [32], replicated, may hold values from 0 to 31, each once
- log_table: float32 [2, 16], P('pipe'), may hold values from 0 to 3
- dim_index: int32 [2, 64], P('pipe'), may hold values from 0 to 15, as said below
Outputs:
- attended: bfloat16 [2, 4, 2048, 2048], P('pipe', 'dp', 'ctx')
- query_gradient: bfloat16 [2, 4, 2048, 2048], P('pipe', 'dp', 'ctx')
- key_gradient: bfloat16 [2, 4, 2048, 512], P('pipe', 'dp', 'ctx')
- value_gradient: bfloat16 [2, 4, 2048, 512], P('pipe', 'dp', 'ctx')
- table_grad: float32 [2, 16], P('pipe')
Inputs may be any that keep to these rules, and one draw needn't show every extreme that they name: `block_order`: a permutation. `dim_index`: each row names every table entry equally often.
All inputs are finite; a program needn't handle non-finite values.
Results may differ from a plain program's by a relative error of at most 0.025.
Values may be sent and summed in bfloat16 or wider, within the bound.
No kernel may reach another device: no remote copies, remote signals or barrier semaphores. Data moves between devices by JAX's collectives and lax.ppermute only.
A program may use at most 64 MiB of HBM per device.

v0:
```python
import jax
import jax.numpy as jnp
from jax import lax
from jax.sharding import PartitionSpec as P

HEAD_SIZE = 128


neg_large = -1e30
rope_base = 500000.0


def passed_along(value, axis, by):
    size = lax.axis_size(axis)
    return lax.ppermute(value, axis, [(i, (i + by) % size) for i in range(size)])


def apply_rotation(vectors, cosine_values, sine_lookup):
    half_len = vectors.shape[-1] // 2
    lower_half = vectors[..., :half_len]
    upper_half = vectors[..., half_len:]
    return jnp.concatenate(
        [
            lower_half * cosine_values - upper_half * sine_lookup,
            lower_half * sine_lookup + upper_half * cosine_values,
        ],
        axis=-1,
    )


def rotate_back(gradient, cosine_values, sine_lookup):
    half_len = gradient.shape[-1] // 2
    lower_half = gradient[..., :half_len]
    upper_half = gradient[..., half_len:]
    return jnp.concatenate(
        [
            lower_half * cosine_values + upper_half * sine_lookup,
            upper_half * cosine_values - lower_half * sine_lookup,
        ],
        axis=-1,
    )


def angle_grad(gradient, rotated):
    half_len = gradient.shape[-1] // 2
    return jnp.sum(
        gradient[..., half_len:] * rotated[..., :half_len]
        - gradient[..., :half_len] * rotated[..., half_len:],
        axis=1,
    )


def angles_for(table_row, index_row, positions, head_dim):
    half_len = head_dim // 2
    onehot = (
        index_row[:, None] == jnp.arange(table_row.shape[0], dtype=jnp.int32)[None, :]
    ).astype(jnp.float32)
    log_factor = jnp.dot(onehot, table_row, precision=lax.Precision.HIGHEST)
    base_rate = rope_base ** (-(jnp.arange(half_len, dtype=jnp.float32) * 2.0 / head_dim))
    scaled_rate = base_rate * jnp.exp(-log_factor)
    return (onehot, positions[:, None] * scaled_rate[None, :])


def slot_positions(block_order, device, tok_rows):
    half_len = tok_rows // 2
    blocks = lax.dynamic_slice_in_dim(block_order, device * 2, 2)
    return (
        (blocks[:, None] * half_len + jnp.arange(half_len, dtype=jnp.int32)[None, :])
        .reshape(-1)
        .astype(jnp.float32)
    )


def on_device(
    queries, key_rows, layer_value_rows, prior_output, later_grad, block_order, log_table, dim_index
):
    tok_rows = queries.shape[2]
    q_width = queries.shape[3]
    kv_width = key_rows.shape[3]
    kv_heads = kv_width // HEAD_SIZE
    group_size = q_width // kv_width
    cycle_size = lax.axis_size("ctx")
    my_index = lax.axis_index("ctx")
    score_scale = HEAD_SIZE ** (-0.5)
    arriving = passed_along(prior_output, "pipe", 1)
    returning = passed_along(later_grad, "pipe", -1)
    positions = slot_positions(block_order, my_index, tok_rows)
    onehot, angles = angles_for(log_table[0], dim_index[0], positions, HEAD_SIZE)
    cosine_values = jnp.cos(angles)[:, None, :]
    sine_lookup = jnp.sin(angles)[:, None, :]
    mixed = (queries[0, 0].astype(jnp.float32) + arriving[0, 0].astype(jnp.float32)).reshape(
        tok_rows, kv_heads * group_size, HEAD_SIZE
    )
    rotated_query_rows = apply_rotation(mixed, cosine_values, sine_lookup).astype(jnp.bfloat16)
    rotated_key_rows = apply_rotation(
        key_rows[0, 0].astype(jnp.float32).reshape(tok_rows, kv_heads, HEAD_SIZE),
        cosine_values,
        sine_lookup,
    ).astype(jnp.bfloat16)
    grouped_queries = rotated_query_rows.reshape(tok_rows, kv_heads, group_size, HEAD_SIZE)
    value_head_rows = layer_value_rows[0, 0].reshape(tok_rows, kv_heads, HEAD_SIZE)
    output_gradient = returning[0, 0].reshape(tok_rows, kv_heads, group_size, HEAD_SIZE)
    key_value = jnp.stack([rotated_key_rows, value_head_rows])

    def visit(softmax_state, block_pair, key_pos):
        maxima, totals, accumulated = softmax_state
        scores = (
            jnp.einsum(
                "qhgd,khd->hgqk", grouped_queries, block_pair[0], preferred_element_type=jnp.float32
            )
            * score_scale
        )
        visible = key_pos[None, :] <= positions[:, None]
        row_max = jnp.max(jnp.where(visible, scores, neg_large), axis=-1)
        new_max = jnp.maximum(maxima, row_max)
        weights = jnp.where(visible, jnp.exp(scores - new_max[..., None]), 0.0)
        rescale = jnp.exp(maxima - new_max)
        totals = totals * rescale + jnp.sum(weights, axis=-1)
        summed = jnp.einsum(
            "hgqk,khd->qhgd",
            weights.astype(jnp.bfloat16),
            block_pair[1],
            preferred_element_type=jnp.float32,
        )
        accumulated = accumulated * jnp.moveaxis(rescale, -1, 0)[..., None] + summed
        return (new_max, totals, accumulated)

    def visit_back(block_pair, key_pos, log_totals, row_delta):
        scores = (
            jnp.einsum(
                "qhgd,khd->hgqk", grouped_queries, block_pair[0], preferred_element_type=jnp.float32
            )
            * score_scale
        )
        visible = key_pos[None, :] <= positions[:, None]
        probs = jnp.where(visible, jnp.exp(scores - log_totals[..., None]), 0.0)
        value_part = jnp.einsum(
            "hgqk,qhgd->khd",
            probs.astype(jnp.bfloat16),
            output_gradient,
            preferred_element_type=jnp.float32,
        )
        prob_grad = jnp.einsum(
            "qhgd,khd->hgqk", output_gradient, block_pair[1], preferred_element_type=jnp.float32
        )
        score_grad = (probs * (prob_grad - row_delta[..., None])).astype(jnp.bfloat16)
        query_part = jnp.einsum(
            "hgqk,khd->qhgd", score_grad, block_pair[0], preferred_element_type=jnp.float32
        )
        key_part = jnp.einsum(
            "hgqk,qhgd->khd", score_grad, grouped_queries, preferred_element_type=jnp.float32
        )
        return (query_part, jnp.stack([key_part, value_part]))

    initial = (
        jnp.full((kv_heads, group_size, tok_rows), neg_large, jnp.float32),
        jnp.zeros((kv_heads, group_size, tok_rows), jnp.float32),
        jnp.zeros((tok_rows, kv_heads, group_size, HEAD_SIZE), jnp.float32),
    )

    def guarded(softmax_state, block_pair, key_pos):
        return lax.cond(
            jnp.min(key_pos) <= jnp.max(positions),
            lambda held: visit(held, block_pair, key_pos),
            lambda held: held,
            softmax_state,
        )

    empty_query = jnp.zeros((tok_rows, kv_heads, group_size, HEAD_SIZE), jnp.float32)
    empty_pair = jnp.zeros((2, tok_rows, kv_heads, HEAD_SIZE), jnp.float32)

    def back_terms(block_pair, key_pos, log_totals, row_delta):
        return lax.cond(
            jnp.min(key_pos) <= jnp.max(positions),
            lambda held: visit_back(held, key_pos, log_totals, row_delta),
            lambda held: (empty_query, empty_pair),
            block_pair,
        )

    def forward_turn(turn_index, carried):
        softmax_state, block_pair = carried
        source = (my_index - turn_index) % cycle_size
        softmax_state = guarded(
            softmax_state, block_pair, slot_positions(block_order, source, tok_rows)
        )
        block_pair = passed_along(block_pair, "ctx", 1)
        return (softmax_state, block_pair)

    softmax_state, block_pair = lax.fori_loop(0, cycle_size - 1, forward_turn, (initial, key_value))
    last_source = (my_index + 1) % cycle_size
    softmax_state = guarded(
        softmax_state, block_pair, slot_positions(block_order, last_source, tok_rows)
    )
    maxima, totals, accumulated = softmax_state
    final_result = (accumulated / jnp.moveaxis(totals, -1, 0)[..., None]).astype(jnp.bfloat16)
    finish_log_totals = maxima + jnp.log(totals)
    finish_row_delta = jnp.moveaxis(
        jnp.sum(output_gradient.astype(jnp.float32) * final_result.astype(jnp.float32), axis=-1),
        0,
        -1,
    )
    final_result, log_totals, row_delta = (final_result, finish_log_totals, finish_row_delta)

    def backward_turn(turn_index, carried):
        query_sum, block_pair, travel_grads = carried
        source = (my_index - turn_index) % cycle_size
        key_pos = slot_positions(block_order, source, tok_rows)
        query_part, pair_part = back_terms(block_pair, key_pos, log_totals, row_delta)
        query_sum = query_sum + query_part
        travel_grads = travel_grads + pair_part
        block_pair = passed_along(block_pair, "ctx", 1)
        travel_grads = passed_along(travel_grads.astype(jnp.bfloat16), "ctx", 1).astype(
            travel_grads.dtype
        )
        return (query_sum, block_pair, travel_grads)

    query_sum, block_pair, own_grads = lax.fori_loop(
        0, cycle_size, backward_turn, (empty_query, key_value, empty_pair)
    )
    query_rot_grad = (query_sum * score_scale).reshape(tok_rows, kv_heads * group_size, HEAD_SIZE)
    key_rot_grad = own_grads[0] * score_scale
    query_gradient = rotate_back(query_rot_grad, cosine_values, sine_lookup).astype(jnp.bfloat16)
    key_gradient = rotate_back(key_rot_grad, cosine_values, sine_lookup).astype(jnp.bfloat16)
    value_gradient = own_grads[1].astype(jnp.bfloat16)
    angle_sums = angle_grad(query_rot_grad, rotated_query_rows.astype(jnp.float32)) + angle_grad(
        key_rot_grad, rotated_key_rows.astype(jnp.float32)
    )
    log_gradient = -jnp.sum(angle_sums * angles, axis=0)
    partial_value = jnp.dot(log_gradient, onehot, precision=lax.Precision.HIGHEST)
    summed_table = lax.psum(partial_value, ("ctx", "dp"))
    table_grad = summed_table / (cycle_size * lax.axis_size("dp") * tok_rows)
    return (
        final_result.reshape(1, 1, tok_rows, q_width),
        query_gradient.reshape(1, 1, tok_rows, q_width),
        key_gradient.reshape(1, 1, tok_rows, kv_width),
        value_gradient.reshape(1, 1, tok_rows, kv_width),
        table_grad[None, :],
    )


def solution(mesh):
    placed = (
        P("pipe", "dp", "ctx", None),
        P("pipe", "dp", "ctx", None),
        P("pipe", "dp", "ctx", None),
        P("pipe", "dp", "ctx", None),
        P("pipe", "dp", "ctx", None),
        P(),
        P("pipe", None),
        P("pipe", None),
    )
    return jax.shard_map(
        on_device,
        mesh=mesh,
        in_specs=placed,
        out_specs=(
            P("pipe", "dp", "ctx", None),
            P("pipe", "dp", "ctx", None),
            P("pipe", "dp", "ctx", None),
            P("pipe", "dp", "ctx", None),
            P("pipe", None),
        ),
        check_vma=False,
    )
```

profile of v0, /device:TPU:0, one launch (start us, length us, event | category | flops | bytes accessed | tf_op | source)
XLA Modules:
  0.0 695.8 jit_solution(15029671179001092386)
XLA Ops:
  14.0 171.1 %while.42 = (s32[]{:T(128)}, f32[4,4,128]{2,1,0:T(4,128)S(1)}, f32[4,4,128]{2,1,0:T(4,128)S(1)}, f32[128,4,4,128]{3,0,2,1:T(8,128)S(1)}, bf16[2,128,4,128]{3,1,2...) while((s32[]{:T(128)}, f32[4,4,128]{2,1,0:T(4,128)S(1)}, ...), condition=%wide.region_8.9_spmd.clone, body=%wide.region_2.8_spmd.clone.sunk | while | flops 137124752 | bytes 7803410 | solution.py:189
  18.4 3.3 conditional.8
  21.7 5.0 collective-permute-done
  29.5 3.3 conditional.8
  32.8 5.8 collective-permute-done
  41.4 3.3 conditional.8
  44.7 4.8 collective-permute-done
  52.4 3.3 conditional.8
  55.7 4.5 collective-permute-done
  63.0 3.3 conditional.8
  66.3 4.5 collective-permute-done
  73.6 3.3 conditional.8
  76.9 4.5 collective-permute-done
  84.2 3.3 conditional.8
  87.5 4.6 collective-permute-done
  94.9 3.3 conditional.8
  98.3 5.7 collective-permute-done
  106.7 3.3 conditional.8
  110.1 6.9 collective-permute-done
  119.8 3.3 conditional.8
  123.1 6.6 collective-permute-done
  132.4 9.1 %collective-permute-done = bf16[2,128,4,128]{3,1,2,0:T(8,128)(2,1)S(1)} collective-permute-done((bf16[2,128,4,128]{3,1,2,0:T(8,128)(2,1)}, bf16[2,128,4,128]{3,1,2,0:T(8,128)(2,1)S(1)}, u32[]{:S(2)}, u32[]{:S(2)}) %collective-permute-start) | collective-permute-done | bytes 262176 | tf_op jit(solution)/shard_map/while/body/eval_jaxpr/ppermute | solution.py:15
  144.3 3.3 conditional.8
  147.6 4.8 collective-permute-done
  155.3 7.8 %collective-permute-done = bf16[2,128,4,128]{3,1,2,0:T(8,128)(2,1)S(1)} collective-permute-done((bf16[2,128,4,128]{3,1,2,0:T(8,128)(2,1)}, bf16[2,128,4,128]{3,1,2,0:T(8,128)(2,1)S(1)}, u32[]{:S(2)}, u32[]{:S(2)}) %collective-permute-start) | collective-permute-done | bytes 262176 | tf_op jit(solution)/shard_map/while/body/eval_jaxpr/ppermute | solution.py:15
  165.9 3.3 conditional.8
  169.2 4.5 collective-permute-done
  176.5 3.3 conditional.8
  179.8 5.2 collective-permute-done
  192.8 315.9 %while.43 = (s32[]{:T(128)}, f32[128,4,4,128]{3,0,2,1:T(8,128)}, bf16[2,128,4,128]{3,1,2,0:T(8,128)(2,1)S(1)}, f32[2,128,4,128]{3,1,2,0:T(8,128)S(1)}, s32[]{:T(...) while((s32[]{:T(128)}, f32[128,4,4,128]{3,0,2,1:T(8,128)}, ...), condition=%wide.region_18.19_spmd.clone, body=%wide.region_14.0_spmd.clone.sunk | while | flops 338576288 | bytes 17750600 | solution.py:217
  196.0 5.3 conditional.9
  203.3 10.5 %collective-permute-done.2 = bf16[2,128,4,128]{3,1,2,0:T(8,128)(2,1)S(1)} collective-permute-done((bf16[2,128,4,128]{3,1,2,0:T(8,128)(2,1)}, bf16[2,128,4,128]{3,1,2,0:T(8,128)(2,1)S(1)}, u32[]{:S(2)}, u32[]{:S(2)}) %collective-permute-start.2) | collective-permute-done | bytes 262176 | tf_op jit(solution)/shard_map/while/body/eval_jaxpr/ppermute | solution.py:15
  217.0 5.3 conditional.9
  223.1 2.4 select_add_fusion.3
  225.5 10.2 %collective-permute-done.2 = bf16[2,128,4,128]{3,1,2,0:T(8,128)(2,1)S(1)} collective-permute-done((bf16[2,128,4,128]{3,1,2,0:T(8,128)(2,1)}, bf16[2,128,4,128]{3,1,2,0:T(8,128)(2,1)S(1)}, u32[]{:S(2)}, u32[]{:S(2)}) %collective-permute-start.2) | collective-permute-done | bytes 262176 | tf_op jit(solution)/shard_map/while/body/eval_jaxpr/ppermute | solution.py:15
  239.0 5.3 conditional.9
  245.1 2.4 select_add_fusion.3
  247.5 9.4 %collective-permute-done.2 = bf16[2,128,4,128]{3,1,2,0:T(8,128)(2,1)S(1)} collective-permute-done((bf16[2,128,4,128]{3,1,2,0:T(8,128)(2,1)}, bf16[2,128,4,128]{3,1,2,0:T(8,128)(2,1)S(1)}, u32[]{:S(2)}, u32[]{:S(2)}) %collective-permute-start.2) | collective-permute-done | bytes 262176 | tf_op jit(solution)/shard_map/while/body/eval_jaxpr/ppermute | solution.py:15
  260.2 5.3 conditional.9
  266.2 2.4 select_add_fusion.3
  268.6 8.5 %collective-permute-done.2 = bf16[2,128,4,128]{3,1,2,0:T(8,128)(2,1)S(1)} collective-permute-done((bf16[2,128,4,128]{3,1,2,0:T(8,128)(2,1)}, bf16[2,128,4,128]{3,1,2,0:T(8,128)(2,1)S(1)}, u32[]{:S(2)}, u32[]{:S(2)}) %collective-permute-start.2) | collective-permute-done | bytes 262176 | tf_op jit(solution)/shard_map/while/body/eval_jaxpr/ppermute | solution.py:15
  280.5 5.3 conditional.9
  289.0 7.6 %collective-permute-done.2 = bf16[2,128,4,128]{3,1,2,0:T(8,128)(2,1)S(1)} collective-permute-done((bf16[2,128,4,128]{3,1,2,0:T(8,128)(2,1)}, bf16[2,128,4,128]{3,1,2,0:T(8,128)(2,1)S(1)}, u32[]{:S(2)}, u32[]{:S(2)}) %collective-permute-start.2) | collective-permute-done | bytes 262176 | tf_op jit(solution)/shard_map/while/body/eval_jaxpr/ppermute | solution.py:15
  299.9 5.3 conditional.9
  308.3 7.5 %collective-permute-done.2 = bf16[2,128,4,128]{3,1,2,0:T(8,128)(2,1)S(1)} collective-permute-done((bf16[2,128,4,128]{3,1,2,0:T(8,128)(2,1)}, bf16[2,128,4,128]{3,1,2,0:T(8,128)(2,1)S(1)}, u32[]{:S(2)}, u32[]{:S(2)}) %collective-permute-start.2) | collective-permute-done | bytes 262176 | tf_op jit(solution)/shard_map/while/body/eval_jaxpr/ppermute | solution.py:15
  319.2 5.3 conditional.9
  327.6 7.5 %collective-permute-done.2 = bf16[2,128,4,128]{3,1,2,0:T(8,128)(2,1)S(1)} collective-permute-done((bf16[2,128,4,128]{3,1,2,0:T(8,128)(2,1)}, bf16[2,128,4,128]{3,1,2,0:T(8,128)(2,1)S(1)}, u32[]{:S(2)}, u32[]{:S(2)}) %collective-permute-start.2) | collective-permute-done | bytes 262176 | tf_op jit(solution)/shard_map/while/body/eval_jaxpr/ppermute | solution.py:15
  338.4 5.3 conditional.9
  346.9 7.5 %collective-permute-done.2 = bf16[2,128,4,128]{3,1,2,0:T(8,128)(2,1)S(1)} collective-permute-done((bf16[2,128,4,128]{3,1,2,0:T(8,128)(2,1)}, bf16[2,128,4,128]{3,1,2,0:T(8,128)(2,1)S(1)}, u32[]{:S(2)}, u32[]{:S(2)}) %collective-permute-start.2) | collective-permute-done | bytes 262176 | tf_op jit(solution)/shard_map/while/body/eval_jaxpr/ppermute | solution.py:15
  357.7 5.3 conditional.9
  366.2 7.5 %collective-permute-done.2 = bf16[2,128,4,128]{3,1,2,0:T(8,128)(2,1)S(1)} collective-permute-done((bf16[2,128,4,128]{3,1,2,0:T(8,128)(2,1)}, bf16[2,128,4,128]{3,1,2,0:T(8,128)(2,1)S(1)}, u32[]{:S(2)}, u32[]{:S(2)}) %collective-permute-start.2) | collective-permute-done | bytes 262176 | tf_op jit(solution)/shard_map/while/body/eval_jaxpr/ppermute | solution.py:15
  377.0 5.3 conditional.9
  385.4 7.5 %collective-permute-done.2 = bf16[2,128,4,128]{3,1,2,0:T(8,128)(2,1)S(1)} collective-permute-done((bf16[2,128,4,128]{3,1,2,0:T(8,128)(2,1)}, bf16[2,128,4,128]{3,1,2,0:T(8,128)(2,1)S(1)}, u32[]{:S(2)}, u32[]{:S(2)}) %collective-permute-start.2) | collective-permute-done | bytes 262176 | tf_op jit(solution)/shard_map/while/body/eval_jaxpr/ppermute | solution.py:15
  401.4 10.8 %collective-permute-done.2 = bf16[2,128,4,128]{3,1,2,0:T(8,128)(2,1)S(1)} collective-permute-done((bf16[2,128,4,128]{3,1,2,0:T(8,128)(2,1)}, bf16[2,128,4,128]{3,1,2,0:T(8,128)(2,1)S(1)}, u32[]{:S(2)}, u32[]{:S(2)}) %collective-permute-start.2) | collective-permute-done | bytes 262176 | tf_op jit(solution)/shard_map/while/body/eval_jaxpr/ppermute | solution.py:15
  415.5 5.3 conditional.9
  424.0 7.5 %collective-permute-done.2 = bf16[2,128,4,128]{3,1,2,0:T(8,128)(2,1)S(1)} collective-permute-done((bf16[2,128,4,128]{3,1,2,0:T(8,128)(2,1)}, bf16[2,128,4,128]{3,1,2,0:T(8,128)(2,1)S(1)}, u32[]{:S(2)}, u32[]{:S(2)}) %collective-permute-start.2) | collective-permute-done | bytes 262176 | tf_op jit(solution)/shard_map/while/body/eval_jaxpr/ppermute | solution.py:15
  438.2 12.6 %collective-permute-done.2 = bf16[2,128,4,128]{3,1,2,0:T(8,128)(2,1)S(1)} collective-permute-done((bf16[2,128,4,128]{3,1,2,0:T(8,128)(2,1)}, bf16[2,128,4,128]{3,1,2,0:T(8,128)(2,1)S(1)}, u32[]{:S(2)}, u32[]{:S(2)}) %collective-permute-start.2) | collective-permute-done | bytes 262176 | tf_op jit(solution)/shard_map/while/body/eval_jaxpr/ppermute | solution.py:15
  454.1 5.3 conditional.9
  462.5 7.5 %collective-permute-done.2 = bf16[2,128,4,128]{3,1,2,0:T(8,128)(2,1)S(1)} collective-permute-done((bf16[2,128,4,128]{3,1,2,0:T(8,128)(2,1)}, bf16[2,128,4,128]{3,1,2,0:T(8,128)(2,1)S(1)}, u32[]{:S(2)}, u32[]{:S(2)}) %collective-permute-start.2) | collective-permute-done | bytes 262176 | tf_op jit(solution)/shard_map/while/body/eval_jaxpr/ppermute | solution.py:15
  473.4 5.3 conditional.9
  481.8 7.5 %collective-permute-done.2 = bf16[2,128,4,128]{3,1,2,0:T(8,128)(2,1)S(1)} collective-permute-done((bf16[2,128,4,128]{3,1,2,0:T(8,128)(2,1)}, bf16[2,128,4,128]{3,1,2,0:T(8,128)(2,1)S(1)}, u32[]{:S(2)}, u32[]{:S(2)}) %collective-permute-start.2) | collective-permute-done | bytes 262176 | tf_op jit(solution)/shard_map/while/body/eval_jaxpr/ppermute | solution.py:15
  492.6 5.3 conditional.9
  501.1 7.5 %collective-permute-done.2 = bf16[2,128,4,128]{3,1,2,0:T(8,128)(2,1)S(1)} collective-permute-done((bf16[2,128,4,128]{3,1,2,0:T(8,128)(2,1)}, bf16[2,128,4,128]{3,1,2,0:T(8,128)(2,1)S(1)}, u32[]{:S(2)}, u32[]{:S(2)}) %collective-permute-start.2) | collective-permute-done | bytes 262176 | tf_op jit(solution)/shard_map/while/body/eval_jaxpr/ppermute | solution.py:15
  514.5 176.6 %psum.7 = f32[16]{0:T(128)S(1)} all-reduce(f32[16]{0:T(128)S(1)} %convolution_bitcast_fusion.6), channel_id=1, replica_groups=mesh['pipe'=2,'ctx'=16,'dp'=4] {'ctx','dp'}, use_global_device_ids=true, to_apply=%region_22.23 | all-reduce | flops 16 | bytes 128 | tf_op jit(solution)/shard_map/psum | solution.py:230
  (650 shorter events, 252.6 us)
Async XLA Ops:
  0.6 3.7 copy-start
  0.6 10.1 %collective-permute-start.3 = (bf16[1,1,128,2048]{3,2,1,0:T(8,128)(2,1)}, bf16[1,1,128,2048]{3,2,1,0:T(8,128)(2,1)S(1)}, u32[]{:S(2)}, u32[]{:S(2)}) collective-permute-start(bf16[1,1,128,2048]{3,2,1,0:T(8,128)(2,1)} %param.21), channel_id=1, source_target_pairs={{0,64},{64,0},{1,65},{65,1},{2,66},{66,2},{3,67},{67,3},{4,68},{68... | collective-permute-start | bytes 1572872 | tf_op jit(solution)/shard_map/ppermute | solution.py:15
  0.7 3.5 copy-start.18
  2.8 186.4 %collective-permute-start.4 = (bf16[1,1,128,2048]{2,3,1,0:T(8,128)(2,1)}, bf16[1,1,128,2048]{2,3,1,0:T(8,128)(2,1)}, u32[]{:S(2)}, u32[]{:S(2)}) collective-permute-start(bf16[1,1,128,2048]{2,3,1,0:T(8,128)(2,1)} %copy.95), channel_id=1, source_target_pairs={{0,64},{64,0},{1,65},{65,1},{2,66},{66,2},{3,67},{67,3},{4,68},{68... | collective-permute-start | bytes 1572872 | tf_op jit(solution)/shard_map/ppermute | solution.py:15
  6.2 4.9 copy-start.13
  6.8 4.0 copy-start.17
  11.6 1.0 copy-start.8
  13.0 1.0 copy-start.4
  14.7 12.0 %collective-permute-start = (bf16[2,128,4,128]{3,1,2,0:T(8,128)(2,1)}, bf16[2,128,4,128]{3,1,2,0:T(8,128)(2,1)S(1)}, u32[]{:S(2)}, u32[]{:S(2)}) collective-permute-start(bf16[2,128,4,128]{3,1,2,0:T(8,128)(2,1)} %copy.144), channel_id=1, source_target_pairs={{0,4},{4,8},{8,12},{12,16},{16,20},{20,24},{24,28},{28,32},{32,36}... | collective-permute-start | bytes 786440 | tf_op jit(solution)/shard_map/while/body/eval_jaxpr/ppermute | solution.py:15
  27.4 11.2 %collective-permute-start = (bf16[2,128,4,128]{3,1,2,0:T(8,128)(2,1)}, bf16[2,128,4,128]{3,1,2,0:T(8,128)(2,1)S(1)}, u32[]{:S(2)}, u32[]{:S(2)}) collective-permute-start(bf16[2,128,4,128]{3,1,2,0:T(8,128)(2,1)} %copy.144), channel_id=1, source_target_pairs={{0,4},{4,8},{8,12},{12,16},{16,20},{20,24},{24,28},{28,32},{32,36}... | collective-permute-start | bytes 786440 | tf_op jit(solution)/shard_map/while/body/eval_jaxpr/ppermute | solution.py:15
  39.3 10.3 %collective-permute-start = (bf16[2,128,4,128]{3,1,2,0:T(8,128)(2,1)}, bf16[2,128,4,128]{3,1,2,0:T(8,128)(2,1)S(1)}, u32[]{:S(2)}, u32[]{:S(2)}) collective-permute-start(bf16[2,128,4,128]{3,1,2,0:T(8,128)(2,1)} %copy.144), channel_id=1, source_target_pairs={{0,4},{4,8},{8,12},{12,16},{16,20},{20,24},{24,28},{28,32},{32,36}... | collective-permute-start | bytes 786440 | tf_op jit(solution)/shard_map/while/body/eval_jaxpr/ppermute | solution.py:15
  50.3 9.9 %collective-permute-start = (bf16[2,128,4,128]{3,1,2,0:T(8,128)(2,1)}, bf16[2,128,4,128]{3,1,2,0:T(8,128)(2,1)S(1)}, u32[]{:S(2)}, u32[]{:S(2)}) collective-permute-start(bf16[2,128,4,128]{3,1,2,0:T(8,128)(2,1)} %copy.144), channel_id=1, source_target_pairs={{0,4},{4,8},{8,12},{12,16},{16,20},{20,24},{24,28},{28,32},{32,36}... | collective-permute-start | bytes 786440 | tf_op jit(solution)/shard_map/while/body/eval_jaxpr/ppermute | solution.py:15
  60.9 9.9 %collective-permute-start = (bf16[2,128,4,128]{3,1,2,0:T(8,128)(2,1)}, bf16[2,128,4,128]{3,1,2,0:T(8,128)(2,1)S(1)}, u32[]{:S(2)}, u32[]{:S(2)}) collective-permute-start(bf16[2,128,4,128]{3,1,2,0:T(8,128)(2,1)} %copy.144), channel_id=1, source_target_pairs={{0,4},{4,8},{8,12},{12,16},{16,20},{20,24},{24,28},{28,32},{32,36}... | collective-permute-start | bytes 786440 | tf_op jit(solution)/shard_map/while/body/eval_jaxpr/ppermute | solution.py:15
  71.5 9.9 %collective-permute-start = (bf16[2,128,4,128]{3,1,2,0:T(8,128)(2,1)}, bf16[2,128,4,128]{3,1,2,0:T(8,128)(2,1)S(1)}, u32[]{:S(2)}, u32[]{:S(2)}) collective-permute-start(bf16[2,128,4,128]{3,1,2,0:T(8,128)(2,1)} %copy.144), channel_id=1, source_target_pairs={{0,4},{4,8},{8,12},{12,16},{16,20},{20,24},{24,28},{28,32},{32,36}... | collective-permute-start | bytes 786440 | tf_op jit(solution)/shard_map/while/body/eval_jaxpr/ppermute | solution.py:15
  82.1 10.0 %collective-permute-start = (bf16[2,128,4,128]{3,1,2,0:T(8,128)(2,1)}, bf16[2,128,4,128]{3,1,2,0:T(8,128)(2,1)S(1)}, u32[]{:S(2)}, u32[]{:S(2)}) collective-permute-start(bf16[2,128,4,128]{3,1,2,0:T(8,128)(2,1)} %copy.144), channel_id=1, source_target_pairs={{0,4},{4,8},{8,12},{12,16},{16,20},{20,24},{24,28},{28,32},{32,36}... | collective-permute-start | bytes 786440 | tf_op jit(solution)/shard_map/while/body/eval_jaxpr/ppermute | solution.py:15
  92.9 11.1 %collective-permute-start = (bf16[2,128,4,128]{3,1,2,0:T(8,128)(2,1)}, bf16[2,128,4,128]{3,1,2,0:T(8,128)(2,1)S(1)}, u32[]{:S(2)}, u32[]{:S(2)}) collective-permute-start(bf16[2,128,4,128]{3,1,2,0:T(8,128)(2,1)} %copy.144), channel_id=1, source_target_pairs={{0,4},{4,8},{8,12},{12,16},{16,20},{20,24},{24,28},{28,32},{32,36}... | collective-permute-start | bytes 786440 | tf_op jit(solution)/shard_map/while/body/eval_jaxpr/ppermute | solution.py:15
  104.7 12.3 %collective-permute-start = (bf16[2,128,4,128]{3,1,2,0:T(8,128)(2,1)}, bf16[2,128,4,128]{3,1,2,0:T(8,128)(2,1)S(1)}, u32[]{:S(2)}, u32[]{:S(2)}) collective-permute-start(bf16[2,128,4,128]{3,1,2,0:T(8,128)(2,1)} %copy.144), channel_id=1, source_target_pairs={{0,4},{4,8},{8,12},{12,16},{16,20},{20,24},{24,28},{28,32},{32,36}... | collective-permute-start | bytes 786440 | tf_op jit(solution)/shard_map/while/body/eval_jaxpr/ppermute | solution.py:15
  117.7 12.0 %collective-permute-start = (bf16[2,128,4,128]{3,1,2,0:T(8,128)(2,1)}, bf16[2,128,4,128]{3,1,2,0:T(8,128)(2,1)S(1)}, u32[]{:S(2)}, u32[]{:S(2)}) collective-permute-start(bf16[2,128,4,128]{3,1,2,0:T(8,128)(2,1)} %copy.144), channel_id=1, source_target_pairs={{0,4},{4,8},{8,12},{12,16},{16,20},{20,24},{24,28},{28,32},{32,36}... | collective-permute-start | bytes 786440 | tf_op jit(solution)/shard_map/while/body/eval_jaxpr/ppermute | solution.py:15
  130.4 11.1 %collective-permute-start = (bf16[2,128,4,128]{3,1,2,0:T(8,128)(2,1)}, bf16[2,128,4,128]{3,1,2,0:T(8,128)(2,1)S(1)}, u32[]{:S(2)}, u32[]{:S(2)}) collective-permute-start(bf16[2,128,4,128]{3,1,2,0:T(8,128)(2,1)} %copy.144), channel_id=1, source_target_pairs={{0,4},{4,8},{8,12},{12,16},{16,20},{20,24},{24,28},{28,32},{32,36}... | collective-permute-start | bytes 786440 | tf_op jit(solution)/shard_map/while/body/eval_jaxpr/ppermute | solution.py:15
  142.2 10.2 %collective-permute-start = (bf16[2,128,4,128]{3,1,2,0:T(8,128)(2,1)}, bf16[2,128,4,128]{3,1,2,0:T(8,128)(2,1)S(1)}, u32[]{:S(2)}, u32[]{:S(2)}) collective-permute-start(bf16[2,128,4,128]{3,1,2,0:T(8,128)(2,1)} %copy.144), channel_id=1, source_target_pairs={{0,4},{4,8},{8,12},{12,16},{16,20},{20,24},{24,28},{28,32},{32,36}... | collective-permute-start | bytes 786440 | tf_op jit(solution)/shard_map/while/body/eval_jaxpr/ppermute | solution.py:15
  153.2 9.9 %collective-permute-start = (bf16[2,128,4,128]{3,1,2,0:T(8,128)(2,1)}, bf16[2,128,4,128]{3,1,2,0:T(8,128)(2,1)S(1)}, u32[]{:S(2)}, u32[]{:S(2)}) collective-permute-start(bf16[2,128,4,128]{3,1,2,0:T(8,128)(2,1)} %copy.144), channel_id=1, source_target_pairs={{0,4},{4,8},{8,12},{12,16},{16,20},{20,24},{24,28},{28,32},{32,36}... | collective-permute-start | bytes 786440 | tf_op jit(solution)/shard_map/while/body/eval_jaxpr/ppermute | solution.py:15
  163.8 9.9 %collective-permute-start = (bf16[2,128,4,128]{3,1,2,0:T(8,128)(2,1)}, bf16[2,128,4,128]{3,1,2,0:T(8,128)(2,1)S(1)}, u32[]{:S(2)}, u32[]{:S(2)}) collective-permute-start(bf16[2,128,4,128]{3,1,2,0:T(8,128)(2,1)} %copy.144), channel_id=1, source_target_pairs={{0,4},{4,8},{8,12},{12,16},{16,20},{20,24},{24,28},{28,32},{32,36}... | collective-permute-start | bytes 786440 | tf_op jit(solution)/shard_map/while/body/eval_jaxpr/ppermute | solution.py:15
  174.4 10.6 %collective-permute-start = (bf16[2,128,4,128]{3,1,2,0:T(8,128)(2,1)}, bf16[2,128,4,128]{3,1,2,0:T(8,128)(2,1)S(1)}, u32[]{:S(2)}, u32[]{:S(2)}) collective-permute-start(bf16[2,128,4,128]{3,1,2,0:T(8,128)(2,1)} %copy.144), channel_id=1, source_target_pairs={{0,4},{4,8},{8,12},{12,16},{16,20},{20,24},{24,28},{28,32},{32,36}... | collective-permute-start | bytes 786440 | tf_op jit(solution)/shard_map/while/body/eval_jaxpr/ppermute | solution.py:15
  186.7 1.3 copy-start.7
  186.7 1.3 copy-start.9
  189.3 1.4 copy-start.10
  190.7 2.1 copy-start.3
  193.5 20.3 %collective-permute-start.1 = (bf16[2,128,4,128]{3,1,2,0:T(8,128)(2,1)}, bf16[2,128,4,128]{3,1,2,0:T(8,128)(2,1)S(1)}, u32[]{:S(2)}, u32[]{:S(2)}) collective-permute-start(bf16[2,128,4,128]{3,1,2,0:T(8,128)(2,1)} %copy.162), channel_id=1, source_target_pairs={{0,4},{4,8},{8,12},{12,16},{16,20},{20,24},{24,28},{28,32},{32,36}... | collective-permute-start | bytes 786440 | tf_op jit(solution)/shard_map/while/body/eval_jaxpr/ppermute | solution.py:15
  202.1 11.6 %collective-permute-start.2 = (bf16[2,128,4,128]{3,1,2,0:T(8,128)(2,1)}, bf16[2,128,4,128]{3,1,2,0:T(8,128)(2,1)S(1)}, u32[]{:S(2)}, u32[]{:S(2)}) collective-permute-start(bf16[2,128,4,128]{3,1,2,0:T(8,128)(2,1)} %fusion.77), channel_id=1, source_target_pairs={{0,4},{4,8},{8,12},{12,16},{16,20},{20,24},{24,28},{28,32},{32,36}... | collective-permute-start | bytes 786440 | tf_op jit(solution)/shard_map/while/body/eval_jaxpr/ppermute | solution.py:15
  214.5 21.3 %collective-permute-start.1 = (bf16[2,128,4,128]{3,1,2,0:T(8,128)(2,1)}, bf16[2,128,4,128]{3,1,2,0:T(8,128)(2,1)S(1)}, u32[]{:S(2)}, u32[]{:S(2)}) collective-permute-start(bf16[2,128,4,128]{3,1,2,0:T(8,128)(2,1)} %copy.162), channel_id=1, source_target_pairs={{0,4},{4,8},{8,12},{12,16},{16,20},{20,24},{24,28},{28,32},{32,36}... | collective-permute-start | bytes 786440 | tf_op jit(solution)/shard_map/while/body/eval_jaxpr/ppermute | solution.py:15
  223.1 12.6 %collective-permute-start.2 = (bf16[2,128,4,128]{3,1,2,0:T(8,128)(2,1)}, bf16[2,128,4,128]{3,1,2,0:T(8,128)(2,1)S(1)}, u32[]{:S(2)}, u32[]{:S(2)}) collective-permute-start(bf16[2,128,4,128]{3,1,2,0:T(8,128)(2,1)} %fusion.77), channel_id=1, source_target_pairs={{0,4},{4,8},{8,12},{12,16},{16,20},{20,24},{24,28},{28,32},{32,36}... | collective-permute-start | bytes 786440 | tf_op jit(solution)/shard_map/while/body/eval_jaxpr/ppermute | solution.py:15
  236.5 20.4 %collective-permute-start.1 = (bf16[2,128,4,128]{3,1,2,0:T(8,128)(2,1)}, bf16[2,128,4,128]{3,1,2,0:T(8,128)(2,1)S(1)}, u32[]{:S(2)}, u32[]{:S(2)}) collective-permute-start(bf16[2,128,4,128]{3,1,2,0:T(8,128)(2,1)} %copy.162), channel_id=1, source_target_pairs={{0,4},{4,8},{8,12},{12,16},{16,20},{20,24},{24,28},{28,32},{32,36}... | collective-permute-start | bytes 786440 | tf_op jit(solution)/shard_map/while/body/eval_jaxpr/ppermute | solution.py:15
  245.1 11.8 %collective-permute-start.2 = (bf16[2,128,4,128]{3,1,2,0:T(8,128)(2,1)}, bf16[2,128,4,128]{3,1,2,0:T(8,128)(2,1)S(1)}, u32[]{:S(2)}, u32[]{:S(2)}) collective-permute-start(bf16[2,128,4,128]{3,1,2,0:T(8,128)(2,1)} %fusion.77), channel_id=1, source_target_pairs={{0,4},{4,8},{8,12},{12,16},{16,20},{20,24},{24,28},{28,32},{32,36}... | collective-permute-start | bytes 786440 | tf_op jit(solution)/shard_map/while/body/eval_jaxpr/ppermute | solution.py:15
  257.6 19.6 %collective-permute-start.1 = (bf16[2,128,4,128]{3,1,2,0:T(8,128)(2,1)}, bf16[2,128,4,128]{3,1,2,0:T(8,128)(2,1)S(1)}, u32[]{:S(2)}, u32[]{:S(2)}) collective-permute-start(bf16[2,128,4,128]{3,1,2,0:T(8,128)(2,1)} %copy.162), channel_id=1, source_target_pairs={{0,4},{4,8},{8,12},{12,16},{16,20},{20,24},{24,28},{28,32},{32,36}... | collective-permute-start | bytes 786440 | tf_op jit(solution)/shard_map/while/body/eval_jaxpr/ppermute | solution.py:15
  266.2 10.9 %collective-permute-start.2 = (bf16[2,128,4,128]{3,1,2,0:T(8,128)(2,1)}, bf16[2,128,4,128]{3,1,2,0:T(8,128)(2,1)S(1)}, u32[]{:S(2)}, u32[]{:S(2)}) collective-permute-start(bf16[2,128,4,128]{3,1,2,0:T(8,128)(2,1)} %fusion.77), channel_id=1, source_target_pairs={{0,4},{4,8},{8,12},{12,16},{16,20},{20,24},{24,28},{28,32},{32,36}... | collective-permute-start | bytes 786440 | tf_op jit(solution)/shard_map/while/body/eval_jaxpr/ppermute | solution.py:15
  278.0 18.7 %collective-permute-start.1 = (bf16[2,128,4,128]{3,1,2,0:T(8,128)(2,1)}, bf16[2,128,4,128]{3,1,2,0:T(8,128)(2,1)S(1)}, u32[]{:S(2)}, u32[]{:S(2)}) collective-permute-start(bf16[2,128,4,128]{3,1,2,0:T(8,128)(2,1)} %copy.162), channel_id=1, source_target_pairs={{0,4},{4,8},{8,12},{12,16},{16,20},{20,24},{24,28},{28,32},{32,36}... | collective-permute-start | bytes 786440 | tf_op jit(solution)/shard_map/while/body/eval_jaxpr/ppermute | solution.py:15
  286.6 10.0 %collective-permute-start.2 = (bf16[2,128,4,128]{3,1,2,0:T(8,128)(2,1)}, bf16[2,128,4,128]{3,1,2,0:T(8,128)(2,1)S(1)}, u32[]{:S(2)}, u32[]{:S(2)}) collective-permute-start(bf16[2,128,4,128]{3,1,2,0:T(8,128)(2,1)} %fusion.77), channel_id=1, source_target_pairs={{0,4},{4,8},{8,12},{12,16},{16,20},{20,24},{24,28},{28,32},{32,36}... | collective-permute-start | bytes 786440 | tf_op jit(solution)/shard_map/while/body/eval_jaxpr/ppermute | solution.py:15
  297.3 18.5 %collective-permute-start.1 = (bf16[2,128,4,128]{3,1,2,0:T(8,128)(2,1)}, bf16[2,128,4,128]{3,1,2,0:T(8,128)(2,1)S(1)}, u32[]{:S(2)}, u32[]{:S(2)}) collective-permute-start(bf16[2,128,4,128]{3,1,2,0:T(8,128)(2,1)} %copy.162), channel_id=1, source_target_pairs={{0,4},{4,8},{8,12},{12,16},{16,20},{20,24},{24,28},{28,32},{32,36}... | collective-permute-start | bytes 786440 | tf_op jit(solution)/shard_map/while/body/eval_jaxpr/ppermute | solution.py:15
  305.9 9.9 %collective-permute-start.2 = (bf16[2,128,4,128]{3,1,2,0:T(8,128)(2,1)}, bf16[2,128,4,128]{3,1,2,0:T(8,128)(2,1)S(1)}, u32[]{:S(2)}, u32[]{:S(2)}) collective-permute-start(bf16[2,128,4,128]{3,1,2,0:T(8,128)(2,1)} %fusion.77), channel_id=1, source_target_pairs={{0,4},{4,8},{8,12},{12,16},{16,20},{20,24},{24,28},{28,32},{32,36}... | collective-permute-start | bytes 786440 | tf_op jit(solution)/shard_map/while/body/eval_jaxpr/ppermute | solution.py:15
  316.6 18.5 %collective-permute-start.1 = (bf16[2,128,4,128]{3,1,2,0:T(8,128)(2,1)}, bf16[2,128,4,128]{3,1,2,0:T(8,128)(2,1)S(1)}, u32[]{:S(2)}, u32[]{:S(2)}) collective-permute-start(bf16[2,128,4,128]{3,1,2,0:T(8,128)(2,1)} %copy.162), channel_id=1, source_target_pairs={{0,4},{4,8},{8,12},{12,16},{16,20},{20,24},{24,28},{28,32},{32,36}... | collective-permute-start | bytes 786440 | tf_op jit(solution)/shard_map/while/body/eval_jaxpr/ppermute | solution.py:15
  325.2 9.9 %collective-permute-start.2 = (bf16[2,128,4,128]{3,1,2,0:T(8,128)(2,1)}, bf16[2,128,4,128]{3,1,2,0:T(8,128)(2,1)S(1)}, u32[]{:S(2)}, u32[]{:S(2)}) collective-permute-start(bf16[2,128,4,128]{3,1,2,0:T(8,128)(2,1)} %fusion.77), channel_id=1, source_target_pairs={{0,4},{4,8},{8,12},{12,16},{16,20},{20,24},{24,28},{28,32},{32,36}... | collective-permute-start | bytes 786440 | tf_op jit(solution)/shard_map/while/body/eval_jaxpr/ppermute | solution.py:15
  335.9 18.5 %collective-permute-start.1 = (bf16[2,128,4,128]{3,1,2,0:T(8,128)(2,1)}, bf16[2,128,4,128]{3,1,2,0:T(8,128)(2,1)S(1)}, u32[]{:S(2)}, u32[]{:S(2)}) collective-permute-start(bf16[2,128,4,128]{3,1,2,0:T(8,128)(2,1)} %copy.162), channel_id=1, source_target_pairs={{0,4},{4,8},{8,12},{12,16},{16,20},{20,24},{24,28},{28,32},{32,36}... | collective-permute-start | bytes 786440 | tf_op jit(solution)/shard_map/while/body/eval_jaxpr/ppermute | solution.py:15
  344.5 9.9 %collective-permute-start.2 = (bf16[2,128,4,128]{3,1,2,0:T(8,128)(2,1)}, bf16[2,128,4,128]{3,1,2,0:T(8,128)(2,1)S(1)}, u32[]{:S(2)}, u32[]{:S(2)}) collective-permute-start(bf16[2,128,4,128]{3,1,2,0:T(8,128)(2,1)} %fusion.77), channel_id=1, source_target_pairs={{0,4},{4,8},{8,12},{12,16},{16,20},{20,24},{24,28},{28,32},{32,36}... | collective-permute-start | bytes 786440 | tf_op jit(solution)/shard_map/while/body/eval_jaxpr/ppermute | solution.py:15
  355.2 18.5 %collective-permute-start.1 = (bf16[2,128,4,128]{3,1,2,0:T(8,128)(2,1)}, bf16[2,128,4,128]{3,1,2,0:T(8,128)(2,1)S(1)}, u32[]{:S(2)}, u32[]{:S(2)}) collective-permute-start(bf16[2,128,4,128]{3,1,2,0:T(8,128)(2,1)} %copy.162), channel_id=1, source_target_pairs={{0,4},{4,8},{8,12},{12,16},{16,20},{20,24},{24,28},{28,32},{32,36}... | collective-permute-start | bytes 786440 | tf_op jit(solution)/shard_map/while/body/eval_jaxpr/ppermute | solution.py:15
  363.8 9.9 %collective-permute-start.2 = (bf16[2,128,4,128]{3,1,2,0:T(8,128)(2,1)}, bf16[2,128,4,128]{3,1,2,0:T(8,128)(2,1)S(1)}, u32[]{:S(2)}, u32[]{:S(2)}) collective-permute-start(bf16[2,128,4,128]{3,1,2,0:T(8,128)(2,1)} %fusion.77), channel_id=1, source_target_pairs={{0,4},{4,8},{8,12},{12,16},{16,20},{20,24},{24,28},{28,32},{32,36}... | collective-permute-start | bytes 786440 | tf_op jit(solution)/shard_map/while/body/eval_jaxpr/ppermute | solution.py:15
  374.4 18.5 %collective-permute-start.1 = (bf16[2,128,4,128]{3,1,2,0:T(8,128)(2,1)}, bf16[2,128,4,128]{3,1,2,0:T(8,128)(2,1)S(1)}, u32[]{:S(2)}, u32[]{:S(2)}) collective-permute-start(bf16[2,128,4,128]{3,1,2,0:T(8,128)(2,1)} %copy.162), channel_id=1, source_target_pairs={{0,4},{4,8},{8,12},{12,16},{16,20},{20,24},{24,28},{28,32},{32,36}... | collective-permute-start | bytes 786440 | tf_op jit(solution)/shard_map/while/body/eval_jaxpr/ppermute | solution.py:15
  383.0 9.9 %collective-permute-start.2 = (bf16[2,128,4,128]{3,1,2,0:T(8,128)(2,1)}, bf16[2,128,4,128]{3,1,2,0:T(8,128)(2,1)S(1)}, u32[]{:S(2)}, u32[]{:S(2)}) collective-permute-start(bf16[2,128,4,128]{3,1,2,0:T(8,128)(2,1)} %fusion.77), channel_id=1, source_target_pairs={{0,4},{4,8},{8,12},{12,16},{16,20},{20,24},{24,28},{28,32},{32,36}... | collective-permute-start | bytes 786440 | tf_op jit(solution)/shard_map/while/body/eval_jaxpr/ppermute | solution.py:15
  393.7 18.5 %collective-permute-start.1 = (bf16[2,128,4,128]{3,1,2,0:T(8,128)(2,1)}, bf16[2,128,4,128]{3,1,2,0:T(8,128)(2,1)S(1)}, u32[]{:S(2)}, u32[]{:S(2)}) collective-permute-start(bf16[2,128,4,128]{3,1,2,0:T(8,128)(2,1)} %copy.162), channel_id=1, source_target_pairs={{0,4},{4,8},{8,12},{12,16},{16,20},{20,24},{24,28},{28,32},{32,36}... | collective-permute-start | bytes 786440 | tf_op jit(solution)/shard_map/while/body/eval_jaxpr/ppermute | solution.py:15
  397.2 15.0 %collective-permute-start.2 = (bf16[2,128,4,128]{3,1,2,0:T(8,128)(2,1)}, bf16[2,128,4,128]{3,1,2,0:T(8,128)(2,1)S(1)}, u32[]{:S(2)}, u32[]{:S(2)}) collective-permute-start(bf16[2,128,4,128]{3,1,2,0:T(8,128)(2,1)} %fusion.77), channel_id=1, source_target_pairs={{0,4},{4,8},{8,12},{12,16},{16,20},{20,24},{24,28},{28,32},{32,36}... | collective-permute-start | bytes 786440 | tf_op jit(solution)/shard_map/while/body/eval_jaxpr/ppermute | solution.py:15
  413.0 18.5 %collective-permute-start.1 = (bf16[2,128,4,128]{3,1,2,0:T(8,128)(2,1)}, bf16[2,128,4,128]{3,1,2,0:T(8,128)(2,1)S(1)}, u32[]{:S(2)}, u32[]{:S(2)}) collective-permute-start(bf16[2,128,4,128]{3,1,2,0:T(8,128)(2,1)} %copy.162), channel_id=1, source_target_pairs={{0,4},{4,8},{8,12},{12,16},{16,20},{20,24},{24,28},{28,32},{32,36}... | collective-permute-start | bytes 786440 | tf_op jit(solution)/shard_map/while/body/eval_jaxpr/ppermute | solution.py:15
  421.6 9.9 %collective-permute-start.2 = (bf16[2,128,4,128]{3,1,2,0:T(8,128)(2,1)}, bf16[2,128,4,128]{3,1,2,0:T(8,128)(2,1)S(1)}, u32[]{:S(2)}, u32[]{:S(2)}) collective-permute-start(bf16[2,128,4,128]{3,1,2,0:T(8,128)(2,1)} %fusion.77), channel_id=1, source_target_pairs={{0,4},{4,8},{8,12},{12,16},{16,20},{20,24},{24,28},{28,32},{32,36}... | collective-permute-start | bytes 786440 | tf_op jit(solution)/shard_map/while/body/eval_jaxpr/ppermute | solution.py:15
  432.3 18.5 %collective-permute-start.1 = (bf16[2,128,4,128]{3,1,2,0:T(8,128)(2,1)}, bf16[2,128,4,128]{3,1,2,0:T(8,128)(2,1)S(1)}, u32[]{:S(2)}, u32[]{:S(2)}) collective-permute-start(bf16[2,128,4,128]{3,1,2,0:T(8,128)(2,1)} %copy.162), channel_id=1, source_target_pairs={{0,4},{4,8},{8,12},{12,16},{16,20},{20,24},{24,28},{28,32},{32,36}... | collective-permute-start | bytes 786440 | tf_op jit(solution)/shard_map/while/body/eval_jaxpr/ppermute | solution.py:15
  435.8 15.0 %collective-permute-start.2 = (bf16[2,128,4,128]{3,1,2,0:T(8,128)(2,1)}, bf16[2,128,4,128]{3,1,2,0:T(8,128)(2,1)S(1)}, u32[]{:S(2)}, u32[]{:S(2)}) collective-permute-start(bf16[2,128,4,128]{3,1,2,0:T(8,128)(2,1)} %fusion.77), channel_id=1, source_target_pairs={{0,4},{4,8},{8,12},{12,16},{16,20},{20,24},{24,28},{28,32},{32,36}... | collective-permute-start | bytes 786440 | tf_op jit(solution)/shard_map/while/body/eval_jaxpr/ppermute | solution.py:15
  451.5 18.5 %collective-permute-start.1 = (bf16[2,128,4,128]{3,1,2,0:T(8,128)(2,1)}, bf16[2,128,4,128]{3,1,2,0:T(8,128)(2,1)S(1)}, u32[]{:S(2)}, u32[]{:S(2)}) collective-permute-start(bf16[2,128,4,128]{3,1,2,0:T(8,128)(2,1)} %copy.162), channel_id=1, source_target_pairs={{0,4},{4,8},{8,12},{12,16},{16,20},{20,24},{24,28},{28,32},{32,36}... | collective-permute-start | bytes 786440 | tf_op jit(solution)/shard_map/while/body/eval_jaxpr/ppermute | solution.py:15
  460.1 9.9 %collective-permute-start.2 = (bf16[2,128,4,128]{3,1,2,0:T(8,128)(2,1)}, bf16[2,128,4,128]{3,1,2,0:T(8,128)(2,1)S(1)}, u32[]{:S(2)}, u32[]{:S(2)}) collective-permute-start(bf16[2,128,4,128]{3,1,2,0:T(8,128)(2,1)} %fusion.77), channel_id=1, source_target_pairs={{0,4},{4,8},{8,12},{12,16},{16,20},{20,24},{24,28},{28,32},{32,36}... | collective-permute-start | bytes 786440 | tf_op jit(solution)/shard_map/while/body/eval_jaxpr/ppermute | solution.py:15
  470.8 18.5 %collective-permute-start.1 = (bf16[2,128,4,128]{3,1,2,0:T(8,128)(2,1)}, bf16[2,128,4,128]{3,1,2,0:T(8,128)(2,1)S(1)}, u32[]{:S(2)}, u32[]{:S(2)}) collective-permute-start(bf16[2,128,4,128]{3,1,2,0:T(8,128)(2,1)} %copy.162), channel_id=1, source_target_pairs={{0,4},{4,8},{8,12},{12,16},{16,20},{20,24},{24,28},{28,32},{32,36}... | collective-permute-start | bytes 786440 | tf_op jit(solution)/shard_map/while/body/eval_jaxpr/ppermute | solution.py:15
  479.4 9.9 %collective-permute-start.2 = (bf16[2,128,4,128]{3,1,2,0:T(8,128)(2,1)}, bf16[2,128,4,128]{3,1,2,0:T(8,128)(2,1)S(1)}, u32[]{:S(2)}, u32[]{:S(2)}) collective-permute-start(bf16[2,128,4,128]{3,1,2,0:T(8,128)(2,1)} %fusion.77), channel_id=1, source_target_pairs={{0,4},{4,8},{8,12},{12,16},{16,20},{20,24},{24,28},{28,32},{32,36}... | collective-permute-start | bytes 786440 | tf_op jit(solution)/shard_map/while/body/eval_jaxpr/ppermute | solution.py:15
  490.1 18.5 %collective-permute-start.1 = (bf16[2,128,4,128]{3,1,2,0:T(8,128)(2,1)}, bf16[2,128,4,128]{3,1,2,0:T(8,128)(2,1)S(1)}, u32[]{:S(2)}, u32[]{:S(2)}) collective-permute-start(bf16[2,128,4,128]{3,1,2,0:T(8,128)(2,1)} %copy.162), channel_id=1, source_target_pairs={{0,4},{4,8},{8,12},{12,16},{16,20},{20,24},{24,28},{28,32},{32,36}... | collective-permute-start | bytes 786440 | tf_op jit(solution)/shard_map/while/body/eval_jaxpr/ppermute | solution.py:15
  498.7 9.9 %collective-permute-start.2 = (bf16[2,128,4,128]{3,1,2,0:T(8,128)(2,1)}, bf16[2,128,4,128]{3,1,2,0:T(8,128)(2,1)S(1)}, u32[]{:S(2)}, u32[]{:S(2)}) collective-permute-start(bf16[2,128,4,128]{3,1,2,0:T(8,128)(2,1)} %fusion.77), channel_id=1, source_target_pairs={{0,4},{4,8},{8,12},{12,16},{16,20},{20,24},{24,28},{28,32},{32,36}... | collective-permute-start | bytes 786440 | tf_op jit(solution)/shard_map/while/body/eval_jaxpr/ppermute | solution.py:15
  508.7 1.2 copy-start.1
  510.0 1.2 copy-start.5
  510.0 1.2 copy-start.14
  511.2 1.8 copy-start.12
  693.8 1.0 copy-start.11
  (22 other events, 14.6 us)
where the time goes:
time: 697 us; the launch traced here: 696 us
  waiting for transfers between devices  221 us (32%)
  blocking collectives  177 us (25%)
  other arithmetic  103 us (15%)
  matrix products  97.8 us (14%)
  local copies, waits for them, and re-layouts  53.4 us (8%)
  loops' own time  37.7 us (5%)
    ppermute x49, waiting for transfers between devices, passed_along(): lax.ppermute(value, axis, [(i, (i + by) % size) for i in range(size)])  221 us
    psum x1, blocking collectives, on_device(): summed_table = lax.psum(partial_value, ('ctx', 'dp'))  177 us
    add x16, other arithmetic, backward_turn(): query_sum = query_sum + query_part  37.1 us
    while x31, local copies, waits for them, and re-layouts  22 us
    dot_general x14, matrix products, visit(): jnp.einsum('hgqk,khd->qhgd', weights.astype(jnp.bfloat16), block_pair[1],...  21.1 us
    another operation x1, loops' own time, on_device(): lax.fori_loop(0, cycle_size, backward_turn, (empty_query, key_value, empt...  18.4 us
    dot_general x14, matrix products, visit_back(): jnp.einsum('qhgd,khd->hgqk', grouped_queries, block_pair[0], preferred_el...  17.6 us
    dot_general x14, matrix products, visit_back(): jnp.einsum('hgqk,khd->qhgd', score_grad, block_pair[0], preferred_element...  17.6 us
  transfers between devices with their start and end apart: 49, of which 31 were waited for; matrix products, arithmetic and copies ran while one was open for 31% of the time, Pallas kernels for 0%

commit v1 on v0

v1 whole, which is shorter than its diff:
```python
import functools
import math

import jax
import jax.numpy as jnp
from jax import lax
from jax.experimental import pallas as pl
from jax.experimental.pallas import tpu as pltpu
from jax.sharding import PartitionSpec as P

HEAD = 128
HALF = 64
ROPE_BASE = 500000.0
LOG_ROWS = 16
TILE = 256
LOG2E = math.log2(math.e)

VMEM = pl.BlockSpec(memory_space=pltpu.VMEM)
SMEM = pl.BlockSpec(memory_space=pltpu.SMEM)
f32 = jnp.float32
bf16 = jnp.bfloat16


def dot(a, b):
    return jnp.dot(a, b, preferred_element_type=f32)


def dot_nt(a, b):
    return lax.dot_general(a, b, (((1,), (1,)), ((), ())), preferred_element_type=f32)


def swap_halves(u):
    return pltpu.roll(u, HALF, 1)


def lane_rates(table_ref, index_row):
    lane = lax.broadcasted_iota(jnp.int32, (1, HEAD), 1)
    pair = jnp.where(lane < HALF, lane, lane - HALF).astype(f32)
    log_factor = jnp.zeros((1, HEAD), f32)
    for entry in range(table_ref.shape[1]):
        log_factor = jnp.where(index_row == entry, table_ref[0, entry], log_factor)
    return jnp.exp(-pair * (2.0 / HEAD * math.log(ROPE_BASE)) - log_factor)


def before_kernel(order_ref, table_ref, index_ref, q_ref, prior_ref, k_ref, v_ref, do_ref,
                  out_ref, cos_ref, sin_ref):
    rows = q_ref.shape[0]
    half_rows = rows // 2
    heads = q_ref.shape[1] // HEAD
    group = q_ref.shape[1] // k_ref.shape[1]
    me = lax.axis_index("ctx")
    rate = lane_rates(table_ref, index_ref[...])
    row = lax.broadcasted_iota(jnp.int32, (rows, HEAD), 0)
    first, second = order_ref[2 * me] * half_rows, order_ref[2 * me + 1] * half_rows
    position = jnp.where(row < half_rows, first + row, second + row - half_rows).astype(f32)
    angle = position * rate
    lane = lax.broadcasted_iota(jnp.int32, (rows, HEAD), 1)
    cosine = jnp.cos(angle)
    sine = jnp.sin(angle)
    signed = jnp.where(lane < HALF, -sine, sine)
    cos_ref[...] = cosine
    sin_ref[...] = signed
    rotated_keys = []
    for head in range(heads // group):
        cols = slice(head * HEAD, (head + 1) * HEAD)
        u = k_ref[:, cols].astype(f32)
        rotated_keys.append((u * cosine + swap_halves(u) * signed).astype(bf16))
    for head in range(heads):
        cols = slice(head * HEAD, (head + 1) * HEAD)
        u = q_ref[:, cols].astype(f32) + prior_ref[:, cols].astype(f32)
        out_ref[head, 0:rows] = (u * cosine + swap_halves(u) * signed).astype(bf16)
        out_ref[head, rows:2 * rows] = do_ref[:, cols]
        out_ref[head, 2 * rows:3 * rows] = rotated_keys[head // group]
        kv = head // group
        out_ref[head, 3 * rows:4 * rows] = v_ref[:, kv * HEAD:(kv + 1) * HEAD]


def main_kernel(order_ref, in_ref, out_ref, qs, dos, ks, vs, kt, vt, dk, dv, atts, dqs, s_scr, e_scr, ds_scr):
    sources = in_ref.shape[0]
    rows = in_ref.shape[1] // 4
    half_rows = rows // 2
    tokens = sources * rows
    tiles = tokens // TILE
    scale = HEAD ** -0.5
    coef = scale * LOG2E

    for slot in range(2 * sources):
        to = pl.ds(pl.multiple_of(order_ref[slot] * half_rows, half_rows), half_rows)
        for number, ref in enumerate((qs, dos, ks, vs)):
            start = number * rows + (slot % 2) * half_rows
            ref[to, :] = in_ref[slot // 2, start:start + half_rows, :]
    kt[...] = ks[...].T
    vt[...] = vs[...].T

    key_iota = lax.broadcasted_iota(jnp.int32, (TILE, TILE), 0)
    query_iota = lax.broadcasted_iota(jnp.int32, (TILE, TILE), 1)
    visible = key_iota <= query_iota
    row_number = lax.broadcasted_iota(jnp.int32, (TILE, HEAD), 0)
    angle_sum = jnp.zeros((8, HEAD), f32)

    def weighted(gradient, rotated, base):
        term = gradient * swap_halves(rotated.astype(f32)) * (row_number + base).astype(f32)
        return jnp.sum(term.reshape(TILE // 8, 8, HEAD), axis=0)

    for i in range(tiles):
        tile = slice(i * TILE, (i + 1) * TILE)
        seen = (i + 1) * TILE
        q = qs[tile, :]
        do_t = dos[tile, :].T.astype(f32)
        top = None
        for c in range(i + 1):
            keys = slice(c * TILE, (c + 1) * TILE)
            s = dot_nt(ks[keys, :], q)
            if c == i:
                s = jnp.where(visible, s, -1e30)
            s_scr[keys, :] = s
            high = jnp.max(s, axis=0, keepdims=True)
            top = high if top is None else jnp.maximum(top, high)
        top = top * coef
        total = jnp.zeros((1, TILE), f32)
        for c in range(i + 1):
            keys = slice(c * TILE, (c + 1) * TILE)
            e = jnp.exp2(s_scr[keys, :] * coef - top)
            total = total + jnp.sum(e, axis=0, keepdims=True)
            e_scr[keys, :] = e.astype(bf16)
        inverse = 1.0 / total
        o_t = dot(vt[:, :seen], e_scr[:seen, :]) * inverse
        atts[tile, :] = o_t.T.astype(bf16)
        do_t = (do_t * inverse).astype(bf16)
        delta = jnp.sum(do_t.astype(f32) * o_t, axis=0, keepdims=True)
        do = do_t.T
        for c in range(i + 1):
            keys = slice(c * TILE, (c + 1) * TILE)
            e = e_scr[keys, :]
            value_part = dot(e, do)
            dp = dot(vs[keys, :], do_t)
            ds = (e.astype(f32) * (dp - delta)).astype(bf16)
            ds_scr[keys, :] = ds
            key_part = dot(ds, q)
            if c == i:
                dv[keys, :] = value_part
                dk[keys, :] = key_part
            else:
                dv[keys, :] += value_part
                dk[keys, :] += key_part
        gq = (dot(kt[:, :seen], ds_scr[:seen, :]) * scale).T
        dqs[tile, :] = gq.astype(bf16)
        angle_sum = angle_sum + weighted(gq, q, i * TILE)

    for i in range(tiles):
        tile = slice(i * TILE, (i + 1) * TILE)
        gk = dk[tile, :] * scale
        dk[tile, :] = gk
        angle_sum = angle_sum + weighted(gk, ks[tile, :], i * TILE)

    for slot in range(2 * sources):
        at = pl.ds(pl.multiple_of(order_ref[slot] * half_rows, half_rows), half_rows)
        for number, ref in enumerate((atts, dqs, dk, dv)):
            start = number * rows + (slot % 2) * half_rows
            out_ref[slot // 2, start:start + half_rows, :] = ref[at, :].astype(bf16)
    line = jnp.sum(angle_sum, axis=0, keepdims=True)
    high = line.astype(bf16).astype(f32)
    middle = (line - high).astype(bf16).astype(f32)
    low = line - high - middle
    which = lax.broadcasted_iota(jnp.int32, (LOG_ROWS, HEAD), 0)
    packed = jnp.where(which == 0, high, jnp.where(which == 1, middle, jnp.where(which == 2, low, 0.0)))
    for source in range(sources):
        out_ref[source, 4 * rows:, :] = packed.astype(bf16)


def after_kernel(in_ref, cos_ref, sin_ref, att_ref, dq_ref, dk_ref, dv_ref):
    rows = cos_ref.shape[0]
    heads = in_ref.shape[0]
    group = att_ref.shape[1] // dk_ref.shape[1]
    cosine, signed = cos_ref[...], sin_ref[...]

    def back(u):
        return (u * cosine - swap_halves(u) * signed).astype(bf16)

    for kv in range(heads // group):
        key_sum = jnp.zeros((rows, HEAD), f32)
        value_sum = jnp.zeros((rows, HEAD), f32)
        for head in range(kv * group, (kv + 1) * group):
            cols = slice(head * HEAD, (head + 1) * HEAD)
            att_ref[:, cols] = in_ref[head, 0:rows]
            dq_ref[:, cols] = back(in_ref[head, rows:2 * rows].astype(f32))
            key_sum = key_sum + in_ref[head, 2 * rows:3 * rows].astype(f32)
            value_sum = value_sum + in_ref[head, 3 * rows:4 * rows].astype(f32)
        cols = slice(kv * HEAD, (kv + 1) * HEAD)
        dk_ref[:, cols] = back(key_sum)
        dv_ref[:, cols] = value_sum.astype(bf16)


def shape(*dims, dtype=bf16):
    return jax.ShapeDtypeStruct(dims, dtype)


def on_device(queries, key_rows, values, prior, later, order, table, index):
    rows, width = queries.shape[2:]
    kv_width = key_rows.shape[3]
    heads = width // HEAD
    sources = lax.axis_size("ctx")
    pipe = lax.axis_size("pipe")
    tokens = rows * sources
    arriving = lax.ppermute(prior, "pipe", [(i, (i + 1) % pipe) for i in range(pipe)])
    returning = lax.ppermute(later, "pipe", [(i, (i - 1) % pipe) for i in range(pipe)])
    wide_index = jnp.concatenate([index, index], axis=1)
    params = pltpu.CompilerParams(vmem_limit_bytes=40 * 2**20)

    sent, cosine, sine = pl.pallas_call(
        before_kernel,
        out_shape=(shape(heads, 4 * rows, HEAD), shape(rows, HEAD, dtype=f32), shape(rows, HEAD, dtype=f32)),
        in_specs=[SMEM, SMEM] + [VMEM] * 6,
        out_specs=[VMEM] * 3,
        compiler_params=params,
    )(order, table, wide_index, queries[0, 0], arriving[0, 0], key_rows[0, 0], values[0, 0], returning[0, 0])

    held = lax.all_to_all(sent, "ctx", 0, 0)

    done = pl.pallas_call(
        main_kernel,
        out_shape=shape(sources, 4 * rows + LOG_ROWS, HEAD),
        in_specs=[SMEM, VMEM],
        out_specs=VMEM,
        scratch_shapes=[pltpu.VMEM((tokens, HEAD), bf16)] * 4
        + [pltpu.VMEM((HEAD, tokens), bf16)] * 2
        + [pltpu.VMEM((tokens, HEAD), f32)] * 2
        + [pltpu.VMEM((tokens, HEAD), bf16)] * 2
        + [pltpu.VMEM((tokens, TILE), f32)]
        + [pltpu.VMEM((tokens, TILE), bf16)] * 2,
        compiler_params=params,
    )(order, held)

    back = lax.all_to_all(done, "ctx", 0, 0)

    line = jnp.sum(back[:, 4 * rows:4 * rows + 3, :].astype(f32), axis=(0, 1))
    dp = lax.axis_size("dp")
    terms = [lax.ppermute(line, "dp", [(i, i ^ s) for i in range(dp)]) for s in range(1, dp)]

    attended, dq, dk, dv = pl.pallas_call(
        after_kernel,
        out_shape=(shape(rows, width), shape(rows, width), shape(rows, kv_width), shape(rows, kv_width)),
        in_specs=[VMEM] * 3,
        out_specs=[VMEM] * 4,
        compiler_params=params,
    )(back, cosine, sine)

    level = [line] + terms
    while len(level) > 1:
        level = [a + b for a, b in zip(level[0::2], level[1::2])]
    line = level[0]
    base = ROPE_BASE ** (-(jnp.arange(HALF, dtype=f32) * 2.0 / HEAD))
    onehot = (index[0][:, None] == jnp.arange(table.shape[1], dtype=jnp.int32)[None, :]).astype(f32)
    log_factor = jnp.sum(onehot * table[0][None, :], axis=1)
    log_gradient = (line[:HALF] - line[HALF:]) * base * jnp.exp(-log_factor)
    table_grad = jnp.sum(onehot * log_gradient[:, None], axis=0) / (tokens * dp)
    return attended[None, None], dq[None, None], dk[None, None], dv[None, None], table_grad[None, :]


def solution(mesh):
    block = P("pipe", "dp", "ctx", None)
    return jax.shard_map(
        on_device,
        mesh=mesh,
        in_specs=(block,) * 5 + (P(), P("pipe", None), P("pipe", None)),
        out_specs=(block,) * 4 + (P("pipe", None),),
        check_vma=False,
    )
```

time: 697 us -> 100 us (0.14)
  waiting for transfers between devices: 221 us -> 4.74 us
  blocking collectives: 177 us -> 67.3 us
  other arithmetic: 103 us -> 1.64 us
  matrix products: 97.8 us -> 0 us
  local copies, waits for them, and re-layouts: 53.4 us -> 4.17 us
  loops' own time: 37.7 us -> 0 us
  Pallas kernels: 0 us -> 15.2 us
    ppermute x49 -> x5, waiting for transfers between devices: 221 us -> 4.74 us  [the longest x3 3.18 us: on_device(): lax.ppermute(line, 'dp', [(i, i ^ s) for i in range(dp)])]
    psum x1 -> x0, blocking collectives: 177 us -> none  [on_device(): summed_table = lax.psum(partial_value, ('ctx', 'dp'))]
    dot_general x100 -> x0, matrix products: 97.8 us -> none  [the longest x14 21.1 us: visit(): jnp.einsum('hgqk,khd->qhgd', weights.astype(jnp.bfloat16), block_pair[1],...]
    all_to_all x0 -> x2, blocking collectives: none -> 67.3 us  [the longest x1 35.6 us: on_device(): held = lax.all_to_all(sent, 'ctx', 0, 0)]
    another operation x34 -> x0, loops' own time: 37.7 us -> none  [the longest x1 18.4 us: on_device(): lax.fori_loop(0, cycle_size, backward_turn, (empty_query, key_value, empt...]
    add x30 -> x1, other arithmetic: 37.3 us -> 0.01 us  [on_device(): level = [a + b for a, b in zip(level[0::2], level[1::2])]]
    convert_element_type x98 -> x0, other arithmetic: 28.2 us -> none  [the longest x63 13.2 us: slot_positions(): return (blocks[:, None] * half_len + jnp.arange(half_len, dtype=jnp.int32...]
    while x32 -> x0, local copies, waits for them, and re-layouts: 22.2 us -> none
  transfers between devices with their start and end apart: 49 -> 5, of which waited for: 31 -> 3; matrix products, arithmetic and copies ran while one was open for 31% -> 1% of each run, Pallas kernels for 0% -> 1%
where the time goes in v1:
time: 100 us; the launch traced here: 99.9 us
  blocking collectives  67.3 us (67%)
  Pallas kernels  15.2 us (15%)
  starting transfers between devices  6.15 us (6%)
  waiting for transfers between devices  4.74 us (5%)
  local copies, waits for them, and re-layouts  4.17 us (4%)
  other arithmetic  1.64 us (2%)
    all_to_all x1, blocking collectives, on_device(): held = lax.all_to_all(sent, 'ctx', 0, 0)  35.6 us
    all_to_all x1, blocking collectives, on_device(): back = lax.all_to_all(done, 'ctx', 0, 0)  31.7 us
    pallas_call x1, Pallas kernels, on_device(): pl.pallas_call(main_kernel, out_shape=shape(sources, 4 * rows + LOG_ROWS,...  12.4 us
    ppermute x3, starting transfers between devices, on_device(): lax.ppermute(line, 'dp', [(i, i ^ s) for i in range(dp)])  5.57 us
    unnamed x14, local copies, waits for them, and re-layouts  4.17 us
    ppermute x3, waiting for transfers between devices, on_device(): lax.ppermute(line, 'dp', [(i, i ^ s) for i in range(dp)])  3.18 us
  transfers between devices with their start and end apart: 5, of which 3 were waited for; matrix products, arithmetic and copies ran while one was open for 1% of the time, Pallas kernels for 1%

profile of v1, /device:TPU:0, one launch (start us, length us, event | category | flops | bytes accessed | tf_op | source)
XLA Modules:
  0.0 99.9 jit_solution(12498999523927047648)
XLA Ops:
  0.6 0.1 collective-permute-start
  0.7 0.5 collective-permute-start.1
  1.2 0.8 pad_add_fusion.index_ref
  2.0 0.8 collective-permute-done
  2.8 0.7 collective-permute-done.1
  3.6 0.0 copy-start
  3.6 1.0 %copy-done = bf16[1,1,128,2048]{3,2,1,0:T(8,128)(2,1)S(1)} copy-done((bf16[1,1,128,2048]{3,2,1,0:T(8,128)(2,1)S(1)}, bf16[1,1,128,2048]{3,2,1,0:T(8,128)(2,1)}, u32[]{:S(2)}) %copy-start) | copy-done | bytes 524312
  4.6 0.0 copy-start.1
  4.6 0.9 copy-done.1
  5.5 0.0 copy-start.2
  5.5 0.9 copy-done.2
  6.4 0.0 copy-start.3
  6.4 0.7 copy-done.3
  7.1 0.0 copy-start.4
  7.1 0.7 copy-done.4
  7.7 1.3 %shard_map.119 = (bf16[16,512,128]{2,1,0:T(8,128)(2,1)S(1)}, f32[128,128]{1,0:T(8,128)S(1)}, f32[128,128]{1,0:T(8,128)S(1)}) custom-call(s32[32]{0:T(128)S(1)} %copy-done.3, f32[1,16]{1,0:T(1,128)S(1)} %copy-done.4, s32[1,128]{1,0:T(1,128)S(1)} %pad_add_fusion.index_ref, bf16[128,2048]{1,0:T(8,128)(2,1)S(1)} %bitcast.13, bf16[128,2048]{1,0:T(8,128)(2,1)S(1)} %bitcast.14, ...), custom_call_target="tpu_custom_call" | custom-call | tf_op jit(solution)/shard_map/pallas_call | solution.py:210
  9.0 35.6 %all_to_all.10.in_ref = bf16[16,512,128]{2,1,0:T(8,128)(2,1)S(1)} all-to-all(bf16[16,512,128]{2,1,0:T(8,128)(2,1)S(1)} %get-tuple-element.12), channel_id=1, replica_groups=mesh['pipe'=2,'ctx'=16,'dp'=4] {'ctx'}, dimensions={0} | all-to-all | bytes 4194304 | tf_op jit(solution)/shard_map/all_to_all | solution.py:218
  44.6 12.4 %shard_map.120 = bf16[16,528,128]{2,1,0:T(8,128)(2,1)S(1)} custom-call(s32[32]{0:T(128)S(1)} %copy-done.3, bf16[16,512,128]{2,1,0:T(8,128)(2,1)S(1)} %all_to_all.10.in_ref), custom_call_target="tpu_custom_call" | custom-call | tf_op jit(solution)/shard_map/pallas_call | solution.py:220
  57.1 0.0 copy-start.5
  57.1 0.0 copy-start.6
  57.1 31.7 %all_to_all.11.in_ref = bf16[16,528,128]{2,1,0:T(8,128)(2,1)S(1)} all-to-all(bf16[16,528,128]{2,1,0:T(8,128)(2,1)S(1)} %shard_map.120), channel_id=1, replica_groups=mesh['pipe'=2,'ctx'=16,'dp'=4] {'ctx'}, dimensions={0} | all-to-all | bytes 4325376 | tf_op jit(solution)/shard_map/all_to_all | solution.py:234
  88.8 2.0 %collective-permute-start.2 = (f32[128]{0:T(128)S(1)}, f32[128]{0:T(128)S(1)}, u32[]{:S(2)}, u32[]{:S(2)}) collective-permute-start(f32[128]{0:T(128)S(1)} %convert_reduce_fusion), channel_id=1, source_target_pairs={{0,1},{1,0},{2,3},{3,2},{4,5},{5,4},{6,7},{7,6},{8,9},{9,8},{10,11... | collective-permute-start | bytes 1544 | tf_op jit(solution)/shard_map/ppermute | solution.py:238
  90.8 3.6 %collective-permute-start.3 = (f32[128]{0:T(128)S(1)}, f32[128]{0:T(128)S(1)}, u32[]{:S(2)}, u32[]{:S(2)}) collective-permute-start(f32[128]{0:T(128)S(1)} %convert_reduce_fusion), channel_id=1, source_target_pairs={{0,2},{1,3},{2,0},{3,1},{4,6},{5,7},{6,4},{7,5},{8,10},{9,11},{10,... | collective-permute-start | bytes 1544 | tf_op jit(solution)/shard_map/ppermute | solution.py:238
  94.4 0.0 collective-permute-start.4
  94.4 0.0 copy-done.5
  94.4 0.0 copy-done.6
  94.4 0.1 select_reduce_fusion.1
  94.5 1.5 %shard_map.121 = (bf16[128,2048]{1,0:T(8,128)(2,1)}, bf16[128,2048]{1,0:T(8,128)(2,1)}, bf16[128,512]{1,0:T(8,128)(2,1)}, bf16[128,512]{1,0:T(8,128)(2,1)}) custom-call(bf16[16,528,128]{2,1,0:T(8,128)(2,1)S(1)} %all_to_all.11.in_ref, f32[128,128]{1,0:T(8,128)S(1)} %get-tuple-element.13.cos_ref, f32[128,128]{1,0:T(8,128)S(1)} %get-tuple-element.14.sin_ref), custom_call_target="tpu_custom_call" | custom-call | tf_op jit(solution)/shard_map/pallas_call | solution.py:240
  96.0 0.0 collective-permute-done.2
  96.0 0.0 collective-permute-done.3
  96.0 3.2 %collective-permute-done.4 = f32[128]{0:T(128)S(1)} collective-permute-done((f32[128]{0:T(128)S(1)}, f32[128]{0:T(128)S(1)}, u32[]{:S(2)}, u32[]{:S(2)}) %collective-permute-start.4) | collective-permute-done | bytes 544 | tf_op jit(solution)/shard_map/ppermute | solution.py:238
  99.1 0.1 exponential_multiply_fusion
  99.2 0.1 select_reduce_fusion
  99.3 0.5 multiply_bitcast_fusion
  (2 shorter events, 0.0 us)
Async XLA Ops:
  0.6 2.2 %collective-permute-start = (bf16[1,1,128,2048]{3,2,1,0:T(8,128)(2,1)}, bf16[1,1,128,2048]{3,2,1,0:T(8,128)(2,1)S(1)}, u32[]{:S(2)}, u32[]{:S(2)}) collective-permute-start(bf16[1,1,128,2048]{3,2,1,0:T(8,128)(2,1)} %param.11), channel_id=1, source_target_pairs={{0,64},{64,0},{1,65},{65,1},{2,66},{66,2},{3,67},{67,3},{4,68},{68... | collective-permute-start | bytes 1572872 | tf_op jit(solution)/shard_map/ppermute | solution.py:205
  0.7 2.9 %collective-permute-start.1 = (bf16[1,1,128,2048]{3,2,1,0:T(8,128)(2,1)}, bf16[1,1,128,2048]{3,2,1,0:T(8,128)(2,1)S(1)}, u32[]{:S(2)}, u32[]{:S(2)}) collective-permute-start(bf16[1,1,128,2048]{3,2,1,0:T(8,128)(2,1)} %param.12), channel_id=1, source_target_pairs={{0,64},{64,0},{1,65},{65,1},{2,66},{66,2},{3,67},{67,3},{4,68},{68... | collective-permute-start | bytes 1572872 | tf_op jit(solution)/shard_map/ppermute | solution.py:206
  3.6 1.0 %copy-start = (bf16[1,1,128,2048]{3,2,1,0:T(8,128)(2,1)S(1)}, bf16[1,1,128,2048]{3,2,1,0:T(8,128)(2,1)}, u32[]{:S(2)}) copy-start(bf16[1,1,128,2048]{3,2,1,0:T(8,128)(2,1)} %param.8) | copy-start | bytes 1572868
  4.6 0.9 copy-start.1
  5.5 0.9 copy-start.2
  6.4 0.7 copy-start.3
  7.1 0.7 copy-start.4
  57.1 37.3 %copy-start.5 = (f32[1,16]{1,0:T(1,128)S(1)}, f32[1,16]{1,0:T(1,128)}, u32[]{:S(2)}) copy-start(f32[1,16]{1,0:T(1,128)} %table_ref.1) | copy-start | bytes 196
  57.1 37.3 %copy-start.6 = (s32[1,64]{1,0:T(1,128)S(1)}, s32[1,64]{1,0:T(1,128)}, u32[]{:S(2)}) copy-start(s32[1,64]{1,0:T(1,128)} %param.15) | copy-start | bytes 772
  88.8 7.1 %collective-permute-start.2 = (f32[128]{0:T(128)S(1)}, f32[128]{0:T(128)S(1)}, u32[]{:S(2)}, u32[]{:S(2)}) collective-permute-start(f32[128]{0:T(128)S(1)} %convert_reduce_fusion), channel_id=1, source_target_pairs={{0,1},{1,0},{2,3},{3,2},{4,5},{5,4},{6,7},{7,6},{8,9},{9,8},{10,11... | collective-permute-start | bytes 1544 | tf_op jit(solution)/shard_map/ppermute | solution.py:238
  90.8 5.2 %collective-permute-start.3 = (f32[128]{0:T(128)S(1)}, f32[128]{0:T(128)S(1)}, u32[]{:S(2)}, u32[]{:S(2)}) collective-permute-start(f32[128]{0:T(128)S(1)} %convert_reduce_fusion), channel_id=1, source_target_pairs={{0,2},{1,3},{2,0},{3,1},{4,6},{5,7},{6,4},{7,5},{8,10},{9,11},{10,... | collective-permute-start | bytes 1544 | tf_op jit(solution)/shard_map/ppermute | solution.py:238
  94.4 4.8 %collective-permute-start.4 = (f32[128]{0:T(128)S(1)}, f32[128]{0:T(128)S(1)}, u32[]{:S(2)}, u32[]{:S(2)}) collective-permute-start(f32[128]{0:T(128)S(1)} %convert_reduce_fusion), channel_id=1, source_target_pairs={{0,3},{1,2},{2,1},{3,0},{4,7},{5,6},{6,5},{7,4},{8,11},{9,10},{10,... | collective-permute-start | bytes 1544 | tf_op jit(solution)/shard_map/ppermute | solution.py:238

commit v2 on v1

--- a/solution.py
+++ b/solution.py
@@ -1,4 +1,3 @@
-import functools
 import math
 
 import jax
@@ -11,12 +10,13 @@
 HEAD = 128
 HALF = 64
 ROPE_BASE = 500000.0
-LOG_ROWS = 16
 TILE = 256
 LOG2E = math.log2(math.e)
 
 VMEM = pl.BlockSpec(memory_space=pltpu.VMEM)
 SMEM = pl.BlockSpec(memory_space=pltpu.SMEM)
+ANY = pl.BlockSpec(memory_space=pl.ANY)
+HBM = pl.BlockSpec(memory_space=pltpu.HBM)
 f32 = jnp.float32
 bf16 = jnp.bfloat16
 
@@ -33,49 +33,65 @@
     return pltpu.roll(u, HALF, 1)
 
 
-def lane_rates(table_ref, index_row):
-    lane = lax.broadcasted_iota(jnp.int32, (1, HEAD), 1)
-    pair = jnp.where(lane < HALF, lane, lane - HALF).astype(f32)
-    log_factor = jnp.zeros((1, HEAD), f32)
+def half_rates(table_ref, index_row):
+    pair = lax.broadcasted_iota(jnp.int32, (1, HALF), 1).astype(f32)
+    log_factor = jnp.zeros((1, HALF), f32)
     for entry in range(table_ref.shape[1]):
         log_factor = jnp.where(index_row == entry, table_ref[0, entry], log_factor)
     return jnp.exp(-pair * (2.0 / HEAD * math.log(ROPE_BASE)) - log_factor)
 
 
-def before_kernel(order_ref, table_ref, index_ref, q_ref, prior_ref, k_ref, v_ref, do_ref,
-                  out_ref, cos_ref, sin_ref):
+def first_kernel(order_hbm, table_hbm, index_hbm, q_hbm, k_hbm, v_hbm,
+                 out_ref, cos_ref, sin_ref, q_ref,
+                 order_ref, table_ref, index_ref, k_ref, v_ref, sems):
+    pairs = ((order_hbm, order_ref), (table_hbm, table_ref), (index_hbm, index_ref),
+             (k_hbm, k_ref), (v_hbm, v_ref), (q_hbm, q_ref))
+    copies = [pltpu.make_async_copy(a, b, sems.at[i]) for i, (a, b) in enumerate(pairs)]
+    for copy in copies:
+        copy.start()
+    for copy in copies[:3]:
+        copy.wait()
     rows = q_ref.shape[0]
     half_rows = rows // 2
     heads = q_ref.shape[1] // HEAD
     group = q_ref.shape[1] // k_ref.shape[1]
     me = lax.axis_index("ctx")
-    rate = lane_rates(table_ref, index_ref[...])
-    row = lax.broadcasted_iota(jnp.int32, (rows, HEAD), 0)
+    rate = half_rates(table_ref, index_ref[...])
+    row = lax.broadcasted_iota(jnp.int32, (rows, HALF), 0)
     first, second = order_ref[2 * me] * half_rows, order_ref[2 * me + 1] * half_rows
     position = jnp.where(row < half_rows, first + row, second + row - half_rows).astype(f32)
     angle = position * rate
-    lane = lax.broadcasted_iota(jnp.int32, (rows, HEAD), 1)
     cosine = jnp.cos(angle)
     sine = jnp.sin(angle)
-    signed = jnp.where(lane < HALF, -sine, sine)
+    cosine = jnp.concatenate([cosine, cosine], axis=1)
+    signed = jnp.concatenate([-sine, sine], axis=1)
     cos_ref[...] = cosine
     sin_ref[...] = signed
-    rotated_keys = []
-    for head in range(heads // group):
-        cols = slice(head * HEAD, (head + 1) * HEAD)
+    copies[3].wait()
+    copies[4].wait()
+    for kv in range(heads // group):
+        cols = slice(kv * HEAD, (kv + 1) * HEAD)
         u = k_ref[:, cols].astype(f32)
-        rotated_keys.append((u * cosine + swap_halves(u) * signed).astype(bf16))
+        rotated = (u * cosine + swap_halves(u) * signed).astype(bf16)
+        value = v_ref[:, cols]
+        for head in range(kv * group, (kv + 1) * group):
+            out_ref[head, 2 * rows:3 * rows] = rotated
+            out_ref[head, 3 * rows:4 * rows] = value
+    copies[5].wait()
+
+
+def second_kernel(held_ref, q_ref, cos_ref, sin_ref, prior_ref, do_ref, out_ref):
+    rows = q_ref.shape[0]
+    heads = q_ref.shape[1] // HEAD
+    cosine, signed = cos_ref[...], sin_ref[...]
     for head in range(heads):
         cols = slice(head * HEAD, (head + 1) * HEAD)
         u = q_ref[:, cols].astype(f32) + prior_ref[:, cols].astype(f32)
         out_ref[head, 0:rows] = (u * cosine + swap_halves(u) * signed).astype(bf16)
         out_ref[head, rows:2 * rows] = do_ref[:, cols]
-        out_ref[head, 2 * rows:3 * rows] = rotated_keys[head // group]
-        kv = head // group
-        out_ref[head, 3 * rows:4 * rows] = v_ref[:, kv * HEAD:(kv + 1) * HEAD]
-
-
-def main_kernel(order_ref, in_ref, out_ref, qs, dos, ks, vs, kt, vt, dk, dv, atts, dqs, s_scr, e_scr, ds_scr):
+
+
+def main_kernel(order_ref, in_ref, out_ref, line_ref, qs, dos, ks, vs, kt, vt, dk, dv, atts, dqs, s_scr, e_scr, ds_scr):
     sources = in_ref.shape[0]
     rows = in_ref.shape[1] // 4
     half_rows = rows // 2
@@ -159,13 +175,7 @@
             start = number * rows + (slot % 2) * half_rows
             out_ref[slot // 2, start:start + half_rows, :] = ref[at, :].astype(bf16)
     line = jnp.sum(angle_sum, axis=0, keepdims=True)
-    high = line.astype(bf16).astype(f32)
-    middle = (line - high).astype(bf16).astype(f32)
-    low = line - high - middle
-    which = lax.broadcasted_iota(jnp.int32, (LOG_ROWS, HEAD), 0)
-    packed = jnp.where(which == 0, high, jnp.where(which == 1, middle, jnp.where(which == 2, low, 0.0)))
-    for source in range(sources):
-        out_ref[source, 4 * rows:, :] = packed.astype(bf16)
+    line_ref[...] = jnp.broadcast_to(line, line_ref.shape)
 
 
 def after_kernel(in_ref, cos_ref, sin_ref, att_ref, dq_ref, dk_ref, dv_ref):
@@ -195,6 +205,14 @@
     return jax.ShapeDtypeStruct(dims, dtype)
 
 
+def added_up(value, axis, size, stride):
+    devices = range(lax.axis_size(axis))
+    level = [value] + [lax.ppermute(value, axis, [(i, i ^ (s * stride)) for i in devices]) for s in range(1, size)]
+    while len(level) > 1:
+        level = [a + b for a, b in zip(level[0::2], level[1::2])]
+    return level[0]
+
+
 def on_device(queries, key_rows, values, prior, later, order, table, index):
     rows, width = queries.shape[2:]
     kv_width = key_rows.shape[3]
@@ -204,24 +222,44 @@
     tokens = rows * sources
     arriving = lax.ppermute(prior, "pipe", [(i, (i + 1) % pipe) for i in range(pipe)])
     returning = lax.ppermute(later, "pipe", [(i, (i - 1) % pipe) for i in range(pipe)])
-    wide_index = jnp.concatenate([index, index], axis=1)
     params = pltpu.CompilerParams(vmem_limit_bytes=40 * 2**20)
-
-    sent, cosine, sine = pl.pallas_call(
-        before_kernel,
-        out_shape=(shape(heads, 4 * rows, HEAD), shape(rows, HEAD, dtype=f32), shape(rows, HEAD, dtype=f32)),
-        in_specs=[SMEM, SMEM] + [VMEM] * 6,
-        out_specs=[VMEM] * 3,
+    payload = shape(heads, 4 * rows, HEAD)
+    wave = shape(rows, HEAD, dtype=f32)
+
+    partly, cosine, sine, own = pl.pallas_call(
+        first_kernel,
+        out_shape=(payload, wave, wave, shape(rows, width)),
+        in_specs=[HBM] * 6,
+        out_specs=[VMEM] * 4,
+        scratch_shapes=[
+            pltpu.SMEM(order.shape, jnp.int32),
+            pltpu.SMEM(table.shape, f32),
+            pltpu.VMEM(index.shape, jnp.int32),
+            pltpu.VMEM((rows, kv_width), bf16),
+            pltpu.VMEM((rows, kv_width), bf16),
+            pltpu.SemaphoreType.DMA((6,)),
+        ],
+        compiler_params=pltpu.CompilerParams(vmem_limit_bytes=56 * 2**20),
+        cost_estimate=pl.CostEstimate(flops=10**7, bytes_accessed=4 * 10**6, transcendentals=0),
+    )(order, table, index, queries[0, 0], key_rows[0, 0], values[0, 0])
+
+    sent = pl.pallas_call(
+        second_kernel,
+        out_shape=payload,
+        in_specs=[ANY] + [VMEM] * 5,
+        out_specs=VMEM,
+        input_output_aliases={0: 0},
         compiler_params=params,
-    )(order, table, wide_index, queries[0, 0], arriving[0, 0], key_rows[0, 0], values[0, 0], returning[0, 0])
+    )(partly, own, cosine, sine, arriving[0, 0], returning[0, 0])
 
     held = lax.all_to_all(sent, "ctx", 0, 0)
 
-    done = pl.pallas_call(
+    dp = lax.axis_size("dp")
+    done, line = pl.pallas_call(
         main_kernel,
-        out_shape=shape(sources, 4 * rows + LOG_ROWS, HEAD),
+        out_shape=(payload, shape(8, HEAD, dtype=f32)),
         in_specs=[SMEM, VMEM],
-        out_specs=VMEM,
+        out_specs=[VMEM, VMEM],
         scratch_shapes=[pltpu.VMEM((tokens, HEAD), bf16)] * 4
         + [pltpu.VMEM((HEAD, tokens), bf16)] * 2
         + [pltpu.VMEM((tokens, HEAD), f32)] * 2
@@ -232,10 +270,9 @@
     )(order, held)
 
     back = lax.all_to_all(done, "ctx", 0, 0)
-
-    line = jnp.sum(back[:, 4 * rows:4 * rows + 3, :].astype(f32), axis=(0, 1))
-    dp = lax.axis_size("dp")
-    terms = [lax.ppermute(line, "dp", [(i, i ^ s) for i in range(dp)]) for s in range(1, dp)]
+    line = added_up(line, "dp", dp, 1)
+    line = added_up(line, "ctx", 4, 1)
+    line = added_up(line, "ctx", sources // 4, 4)
 
     attended, dq, dk, dv = pl.pallas_call(
         after_kernel,
@@ -245,10 +282,7 @@
         compiler_params=params,
     )(back, cosine, sine)
 
-    level = [line] + terms
-    while len(level) > 1:
-        level = [a + b for a, b in zip(level[0::2], level[1::2])]
-    line = level[0]
+    line = line[0]
     base = ROPE_BASE ** (-(jnp.arange(HALF, dtype=f32) * 2.0 / HEAD))
     onehot = (index[0][:, None] == jnp.arange(table.shape[1], dtype=jnp.int32)[None, :]).astype(f32)
     log_factor = jnp.sum(onehot * table[0][None, :], axis=1)

time: 100 us -> 101 us (1.010)
  blocking collectives: 67.3 us -> 35.6 us
  waiting for transfers between devices: 4.74 us -> 21.4 us
  starting transfers between devices: 6.15 us -> 19.5 us
  Pallas kernels: 15.2 us -> 17 us
  local copies, waits for them, and re-layouts: 4.17 us -> 5.66 us
    all_to_all x1 -> x0, blocking collectives: 31.7 us -> none  [on_device(): back = lax.all_to_all(done, 'ctx', 0, 0)]
    ppermute x3 -> x9, waiting for transfers between devices: 3.18 us -> 21.3 us  [added_up(): lax.ppermute(value, axis, [(i, i ^ s * stride) for i in devices])]
    ppermute x3 -> x9, starting transfers between devices: 5.57 us -> 15.1 us  [added_up(): lax.ppermute(value, axis, [(i, i ^ s * stride) for i in devices])]
    all_to_all x0 -> x1, starting transfers between devices: none -> 3.86 us  [on_device(): back = lax.all_to_all(done, 'ctx', 0, 0)]
    pallas_call x2 -> x3, Pallas kernels: 13.7 us -> 15.6 us  [the longest x1 12.4 us: on_device(): pl.pallas_call(main_kernel, out_shape=(payload, shape(8, HEAD, dtype=f32)...]
    unnamed x14 -> x20, local copies, waits for them, and re-layouts: 4.17 us -> 5.66 us
  transfers between devices with their start and end apart: 5 -> 12, of which waited for: 3 -> 6; matrix products, arithmetic and copies ran while one was open for 1% -> 1% of each run, Pallas kernels for 1% -> 3%
where the time goes in v2:
time: 101 us
  blocking collectives  35.6 us (35%)
  waiting for transfers between devices  21.4 us (21%)
  starting transfers between devices  19.5 us (19%)
  Pallas kernels  17 us (17%)
  local copies, waits for them, and re-layouts  5.66 us (6%)
    all_to_all x1, blocking collectives, on_device(): held = lax.all_to_all(sent, 'ctx', 0, 0)  35.6 us
    ppermute x9, waiting for transfers between devices, added_up(): lax.ppermute(value, axis, [(i, i ^ s * stride) for i in devices])  21.3 us
    ppermute x9, starting transfers between devices, added_up(): lax.ppermute(value, axis, [(i, i ^ s * stride) for i in devices])  15.1 us
    pallas_call x1, Pallas kernels, on_device(): pl.pallas_call(main_kernel, out_shape=(payload, shape(8, HEAD, dtype=f32)...  12.4 us
    unnamed x20, local copies, waits for them, and re-layouts  5.66 us
    all_to_all x1, starting transfers between devices, on_device(): back = lax.all_to_all(done, 'ctx', 0, 0)  3.86 us
    pallas_call x1, Pallas kernels, on_device(): pl.pallas_call(first_kernel, out_shape=(payload, wave, wave, shape(rows,...  2.77 us
  transfers between devices with their start and end apart: 12, of which 6 were waited for; matrix products, arithmetic and copies ran while one was open for 1% of the time, Pallas kernels for 3%

profile of v2, /device:TPU:0, one launch (start us, length us, event | category | flops | bytes accessed | tf_op | source)
XLA Modules:
  0.0 100.7 jit_solution(1289012558573158721)
XLA Ops:
  0.6 0.1 collective-permute-start
  0.7 0.5 collective-permute-start.1
  1.2 2.8 %shard_map.119 = (bf16[16,512,128]{2,1,0:T(8,128)(2,1)}, f32[128,128]{1,0:T(8,128)}, f32[128,128]{1,0:T(8,128)}, bf16[128,2048]{1,0:T(8,128)(2,1)}) custom-call(s32[32]{0:T(128)} %order_ref.1, f32[1,16]{1,0:T(1,128)} %table_hbm.1, s32[1,64]{1,0:T(1,128)} %index_hbm.1, bf16[128,2048]{1,0:T(8,128)(2,1)} %bitcast.19, bf16[128,512]{1,0:T(8,128)(2,1)} %bitcast.20, ...), custom_call_target="tpu_custom_call" | custom-call | flops 10000000 | bytes 4000000 | tf_op jit(solution)/shard_map/pallas_call | solution.py:229
  4.0 0.0 collective-permute-done
  4.0 0.0 collective-permute-done.1
  4.0 0.0 copy-start
  4.0 1.6 %copy-done = bf16[16,512,128]{2,1,0:T(8,128)(2,1)S(1)} copy-done((bf16[16,512,128]{2,1,0:T(8,128)(2,1)S(1)}, bf16[16,512,128]{2,1,0:T(8,128)(2,1)}, u32[]{:S(2)}) %copy-start) | copy-done | bytes 2097176
  5.6 0.0 copy-start.2
  5.6 1.0 %copy-done.2 = bf16[128,2048]{1,0:T(8,128)(2,1)S(1)} copy-done((bf16[128,2048]{1,0:T(8,128)(2,1)S(1)}, bf16[128,2048]{1,0:T(8,128)(2,1)}, u32[]{:S(2)}) %copy-start.2) | copy-done | bytes 524312
  6.7 0.0 copy-start.3
  6.7 0.8 copy-done.3
  7.5 0.0 copy-start.5
  7.5 0.8 copy-done.5
  8.3 0.4 shard_map.120
  8.7 0.0 copy-start.7
  8.7 35.6 %all_to_all.10.in_ref = bf16[16,512,128]{2,1,0:T(8,128)(2,1)S(1)} all-to-all(bf16[16,512,128]{2,1,0:T(8,128)(2,1)S(1)} %shard_map.120), channel_id=1, replica_groups=mesh['pipe'=2,'ctx'=16,'dp'=4] {'ctx'}, dimensions={0} | all-to-all | bytes 4194304 | tf_op jit(solution)/shard_map/all_to_all | solution.py:255
  44.3 0.0 copy-done.7
  44.3 12.4 %shard_map.121 = (bf16[16,512,128]{2,1,0:T(8,128)(2,1)S(1)}, f32[8,128]{1,0:T(8,128)S(1)}) custom-call(s32[32]{0:T(128)S(1)} %copy-done.7, bf16[16,512,128]{2,1,0:T(8,128)(2,1)S(1)} %all_to_all.10.in_ref), custom_call_target="tpu_custom_call" | custom-call | tf_op jit(solution)/shard_map/pallas_call | solution.py:258
  56.7 0.0 copy-start.1
  56.7 1.3 %copy-done.1 = bf16[16,512,128]{2,1,0:T(8,128)(2,1)} copy-done((bf16[16,512,128]{2,1,0:T(8,128)(2,1)}, bf16[16,512,128]{2,1,0:T(8,128)(2,1)S(1)}, u32[]{:S(2)}) %copy-start.1) | copy-done | bytes 2097176
  58.0 0.0 copy-start.8
  58.1 0.0 copy-start.9
  58.1 0.0 copy-start.4
  58.1 0.0 copy-start.6
  58.1 3.9 %all-to-all-start.1 = ((bf16[16,512,128]{2,1,0:T(8,128)(2,1)}), bf16[16,512,128]{2,1,0:T(8,128)(2,1)S(1)}, u32[]{:S(2)}, u32[]{:S(2)}) async-start(bf16[16,512,128]{2,1,0:T(8,128)(2,1)} %copy-done.1), calls=%async_computation.1 | async-start | bytes 4194304 | tf_op jit(solution)/shard_map/all_to_all | solution.py:272
  61.9 2.0 %collective-permute-start.2 = (f32[8,128]{1,0:T(8,128)S(1)}, f32[8,128]{1,0:T(8,128)S(1)}, u32[]{:S(2)}, u32[]{:S(2)}) collective-permute-start(f32[8,128]{1,0:T(8,128)S(1)} %get-tuple-element.24), channel_id=1, source_target_pairs={{0,1},{1,0},{2,3},{3,2},{4,5},{5,4},{6,7},{7,6},{8,9},{9,8},{10,11... | collective-permute-start | bytes 12296 | tf_op jit(solution)/shard_map/ppermute | solution.py:210
  63.9 3.6 %collective-permute-start.3 = (f32[8,128]{1,0:T(8,128)S(1)}, f32[8,128]{1,0:T(8,128)S(1)}, u32[]{:S(2)}, u32[]{:S(2)}) collective-permute-start(f32[8,128]{1,0:T(8,128)S(1)} %get-tuple-element.24), channel_id=1, source_target_pairs={{0,2},{1,3},{2,0},{3,1},{4,6},{5,7},{6,4},{7,5},{8,10},{9,11},{10,... | collective-permute-start | bytes 12296 | tf_op jit(solution)/shard_map/ppermute | solution.py:210
  67.5 0.0 collective-permute-start.4
  67.5 0.0 collective-permute-done.2
  67.5 1.6 %collective-permute-done.3 = f32[8,128]{1,0:T(8,128)S(1)} collective-permute-done((f32[8,128]{1,0:T(8,128)S(1)}, f32[8,128]{1,0:T(8,128)S(1)}, u32[]{:S(2)}, u32[]{:S(2)}) %collective-permute-start.3) | collective-permute-done | bytes 4128 | tf_op jit(solution)/shard_map/ppermute | solution.py:210
  69.1 3.2 %collective-permute-done.4 = f32[8,128]{1,0:T(8,128)S(1)} collective-permute-done((f32[8,128]{1,0:T(8,128)S(1)}, f32[8,128]{1,0:T(8,128)S(1)}, u32[]{:S(2)}, u32[]{:S(2)}) %collective-permute-start.4) | collective-permute-done | bytes 4128 | tf_op jit(solution)/shard_map/ppermute | solution.py:210
  72.3 1.7 %collective-permute-start.5 = (f32[8,128]{1,0:T(8,128)S(1)}, f32[8,128]{1,0:T(8,128)S(1)}, u32[]{:S(2)}, u32[]{:S(2)}) collective-permute-start(f32[8,128]{1,0:T(8,128)S(1)} %add_add_fusion.2), channel_id=1, source_target_pairs={{0,4},{4,0},{8,12},{12,8},{16,20},{20,16},{24,28},{28,24},{32,36},... | collective-permute-start | bytes 12296 | tf_op jit(solution)/shard_map/ppermute | solution.py:210
  74.1 2.7 %collective-permute-start.6 = (f32[8,128]{1,0:T(8,128)S(1)}, f32[8,128]{1,0:T(8,128)S(1)}, u32[]{:S(2)}, u32[]{:S(2)}) collective-permute-start(f32[8,128]{1,0:T(8,128)S(1)} %add_add_fusion.2), channel_id=1, source_target_pairs={{0,8},{4,12},{8,0},{12,4},{16,24},{20,28},{24,16},{28,20},{32,40},... | collective-permute-start | bytes 12296 | tf_op jit(solution)/shard_map/ppermute | solution.py:210
  76.8 0.3 collective-permute-start.7
  77.0 10.5 %collective-permute-done.5 = f32[8,128]{1,0:T(8,128)S(1)} collective-permute-done((f32[8,128]{1,0:T(8,128)S(1)}, f32[8,128]{1,0:T(8,128)S(1)}, u32[]{:S(2)}, u32[]{:S(2)}) %collective-permute-start.5) | collective-permute-done | bytes 4128 | tf_op jit(solution)/shard_map/ppermute | solution.py:210
  87.5 2.9 %collective-permute-done.6 = f32[8,128]{1,0:T(8,128)S(1)} collective-permute-done((f32[8,128]{1,0:T(8,128)S(1)}, f32[8,128]{1,0:T(8,128)S(1)}, u32[]{:S(2)}, u32[]{:S(2)}) %collective-permute-start.6) | collective-permute-done | bytes 4128 | tf_op jit(solution)/shard_map/ppermute | solution.py:210
  90.4 0.0 collective-permute-done.7
  90.4 2.0 %collective-permute-start.10 = (f32[8,128]{1,0:T(8,128)S(1)}, f32[8,128]{1,0:T(8,128)S(1)}, u32[]{:S(2)}, u32[]{:S(2)}) collective-permute-start(f32[8,128]{1,0:T(8,128)S(1)} %add_add_fusion.1), channel_id=1, source_target_pairs={{0,48},{4,52},{8,56},{12,60},{16,32},{20,36},{24,40},{28,44},{32,1... | collective-permute-start | bytes 12296 | tf_op jit(solution)/shard_map/ppermute | solution.py:210
  92.4 0.9 collective-permute-start.8
  93.3 1.8 %collective-permute-start.9 = (f32[8,128]{1,0:T(8,128)S(1)}, f32[8,128]{1,0:T(8,128)S(1)}, u32[]{:S(2)}, u32[]{:S(2)}) collective-permute-start(f32[8,128]{1,0:T(8,128)S(1)} %add_add_fusion.1), channel_id=1, source_target_pairs={{0,32},{4,36},{8,40},{12,44},{16,48},{20,52},{24,56},{28,60},{32,0... | collective-permute-start | bytes 12296 | tf_op jit(solution)/shard_map/ppermute | solution.py:210
  95.2 0.0 copy-done.8
  95.2 0.0 copy-done.9
  95.2 0.1 select_reduce_fusion.1
  95.3 0.0 collective-permute-done.10
  95.3 0.8 collective-permute-done.8
  96.0 2.4 %collective-permute-done.9 = f32[8,128]{1,0:T(8,128)S(1)} collective-permute-done((f32[8,128]{1,0:T(8,128)S(1)}, f32[8,128]{1,0:T(8,128)S(1)}, u32[]{:S(2)}, u32[]{:S(2)}) %collective-permute-start.9) | collective-permute-done | bytes 4128 | tf_op jit(solution)/shard_map/ppermute | solution.py:210
  98.5 0.1 fusion
  98.5 0.1 select_reduce_fusion
  98.7 0.5 multiply_bitcast_fusion
  99.2 0.0 all-to-all-done.1.in_ref
  99.2 0.0 copy-done.4
  99.2 0.0 copy-done.6
  99.2 1.5 %shard_map.122 = (bf16[128,2048]{1,0:T(8,128)(2,1)}, bf16[128,2048]{1,0:T(8,128)(2,1)}, bf16[128,512]{1,0:T(8,128)(2,1)}, bf16[128,512]{1,0:T(8,128)(2,1)}) custom-call(bf16[16,512,128]{2,1,0:T(8,128)(2,1)S(1)} %all-to-all-done.1.in_ref, f32[128,128]{1,0:T(8,128)S(1)} %copy-done.4, f32[128,128]{1,0:T(8,128)S(1)} %copy-done.6), custom_call_target="tpu_custom_call" | custom-call | tf_op jit(solution)/shard_map/pallas_call | solution.py:277
  (3 shorter events, 0.0 us)
Async XLA Ops:
  0.6 3.4 %collective-permute-start = (bf16[1,1,128,2048]{3,2,1,0:T(8,128)(2,1)}, bf16[1,1,128,2048]{3,2,1,0:T(8,128)(2,1)S(1)}, u32[]{:S(2)}, u32[]{:S(2)}) collective-permute-start(bf16[1,1,128,2048]{3,2,1,0:T(8,128)(2,1)} %param.11), channel_id=1, source_target_pairs={{0,64},{64,0},{1,65},{65,1},{2,66},{66,2},{3,67},{67,3},{4,68},{68... | collective-permute-start | bytes 1572872 | tf_op jit(solution)/shard_map/ppermute | solution.py:223
  0.7 3.3 %collective-permute-start.1 = (bf16[1,1,128,2048]{3,2,1,0:T(8,128)(2,1)}, bf16[1,1,128,2048]{3,2,1,0:T(8,128)(2,1)S(1)}, u32[]{:S(2)}, u32[]{:S(2)}) collective-permute-start(bf16[1,1,128,2048]{3,2,1,0:T(8,128)(2,1)} %param.12), channel_id=1, source_target_pairs={{0,64},{64,0},{1,65},{65,1},{2,66},{66,2},{3,67},{67,3},{4,68},{68... | collective-permute-start | bytes 1572872 | tf_op jit(solution)/shard_map/ppermute | solution.py:224
  4.0 1.6 %copy-start = (bf16[16,512,128]{2,1,0:T(8,128)(2,1)S(1)}, bf16[16,512,128]{2,1,0:T(8,128)(2,1)}, u32[]{:S(2)}) copy-start(bf16[16,512,128]{2,1,0:T(8,128)(2,1)} %get-tuple-element.15.held_ref) | copy-start | bytes 6291460
  5.6 1.0 %copy-start.2 = (bf16[128,2048]{1,0:T(8,128)(2,1)S(1)}, bf16[128,2048]{1,0:T(8,128)(2,1)}, u32[]{:S(2)}) copy-start(bf16[128,2048]{1,0:T(8,128)(2,1)} %get-tuple-element.16.q_ref) | copy-start | bytes 1572868
  6.7 0.8 copy-start.3
  7.5 0.8 copy-start.5
  8.7 35.6 %copy-start.7 = (s32[32]{0:T(128)S(1)}, s32[32]{0:T(128)}, u32[]{:S(2)}) copy-start(s32[32]{0:T(128)} %order_ref.1) | copy-start | bytes 388
  56.7 1.3 %copy-start.1 = (bf16[16,512,128]{2,1,0:T(8,128)(2,1)}, bf16[16,512,128]{2,1,0:T(8,128)(2,1)S(1)}, u32[]{:S(2)}) copy-start(bf16[16,512,128]{2,1,0:T(8,128)(2,1)S(1)} %get-tuple-element.19) | copy-start | bytes 6291460
  58.0 37.1 %copy-start.8 = (f32[1,16]{1,0:T(1,128)S(1)}, f32[1,16]{1,0:T(1,128)}, u32[]{:S(2)}) copy-start(f32[1,16]{1,0:T(1,128)} %table_hbm.1) | copy-start | bytes 196
  58.1 37.1 %copy-start.9 = (s32[1,64]{1,0:T(1,128)S(1)}, s32[1,64]{1,0:T(1,128)}, u32[]{:S(2)}) copy-start(s32[1,64]{1,0:T(1,128)} %index_hbm.1) | copy-start | bytes 772
  58.1 41.1 %copy-start.4 = (f32[128,128]{1,0:T(8,128)S(1)}, f32[128,128]{1,0:T(8,128)}, u32[]{:S(2)}) copy-start(f32[128,128]{1,0:T(8,128)} %get-tuple-element.17.cos_ref) | copy-start | bytes 196612
  58.1 41.1 %copy-start.6 = (f32[128,128]{1,0:T(8,128)S(1)}, f32[128,128]{1,0:T(8,128)}, u32[]{:S(2)}) copy-start(f32[128,128]{1,0:T(8,128)} %get-tuple-element.18.sin_ref) | copy-start | bytes 196612
  58.1 41.1 %all-to-all-start.1 = ((bf16[16,512,128]{2,1,0:T(8,128)(2,1)}), bf16[16,512,128]{2,1,0:T(8,128)(2,1)S(1)}, u32[]{:S(2)}, u32[]{:S(2)}) async-start(bf16[16,512,128]{2,1,0:T(8,128)(2,1)} %copy-done.1), calls=%async_computation.1 | async-start | bytes 4194304 | tf_op jit(solution)/shard_map/all_to_all | solution.py:272
  61.9 5.6 %collective-permute-start.2 = (f32[8,128]{1,0:T(8,128)S(1)}, f32[8,128]{1,0:T(8,128)S(1)}, u32[]{:S(2)}, u32[]{:S(2)}) collective-permute-start(f32[8,128]{1,0:T(8,128)S(1)} %get-tuple-element.24), channel_id=1, source_target_pairs={{0,1},{1,0},{2,3},{3,2},{4,5},{5,4},{6,7},{7,6},{8,9},{9,8},{10,11... | collective-permute-start | bytes 12296 | tf_op jit(solution)/shard_map/ppermute | solution.py:210
  63.9 5.2 %collective-permute-start.3 = (f32[8,128]{1,0:T(8,128)S(1)}, f32[8,128]{1,0:T(8,128)S(1)}, u32[]{:S(2)}, u32[]{:S(2)}) collective-permute-start(f32[8,128]{1,0:T(8,128)S(1)} %get-tuple-element.24), channel_id=1, source_target_pairs={{0,2},{1,3},{2,0},{3,1},{4,6},{5,7},{6,4},{7,5},{8,10},{9,11},{10,... | collective-permute-start | bytes 12296 | tf_op jit(solution)/shard_map/ppermute | solution.py:210
  67.5 4.8 %collective-permute-start.4 = (f32[8,128]{1,0:T(8,128)S(1)}, f32[8,128]{1,0:T(8,128)S(1)}, u32[]{:S(2)}, u32[]{:S(2)}) collective-permute-start(f32[8,128]{1,0:T(8,128)S(1)} %get-tuple-element.24), channel_id=1, source_target_pairs={{0,3},{1,2},{2,1},{3,0},{4,7},{5,6},{6,5},{7,4},{8,11},{9,10},{10,... | collective-permute-start | bytes 12296 | tf_op jit(solution)/shard_map/ppermute | solution.py:210
  72.3 15.2 %collective-permute-start.5 = (f32[8,128]{1,0:T(8,128)S(1)}, f32[8,128]{1,0:T(8,128)S(1)}, u32[]{:S(2)}, u32[]{:S(2)}) collective-permute-start(f32[8,128]{1,0:T(8,128)S(1)} %add_add_fusion.2), channel_id=1, source_target_pairs={{0,4},{4,0},{8,12},{12,8},{16,20},{20,16},{24,28},{28,24},{32,36},... | collective-permute-start | bytes 12296 | tf_op jit(solution)/shard_map/ppermute | solution.py:210
  74.1 16.3 %collective-permute-start.6 = (f32[8,128]{1,0:T(8,128)S(1)}, f32[8,128]{1,0:T(8,128)S(1)}, u32[]{:S(2)}, u32[]{:S(2)}) collective-permute-start(f32[8,128]{1,0:T(8,128)S(1)} %add_add_fusion.2), channel_id=1, source_target_pairs={{0,8},{4,12},{8,0},{12,4},{16,24},{20,28},{24,16},{28,20},{32,40},... | collective-permute-start | bytes 12296 | tf_op jit(solution)/shard_map/ppermute | solution.py:210
  76.8 13.6 %collective-permute-start.7 = (f32[8,128]{1,0:T(8,128)S(1)}, f32[8,128]{1,0:T(8,128)S(1)}, u32[]{:S(2)}, u32[]{:S(2)}) collective-permute-start(f32[8,128]{1,0:T(8,128)S(1)} %add_add_fusion.2), channel_id=1, source_target_pairs={{0,12},{4,8},{8,4},{12,0},{16,28},{20,24},{24,20},{28,16},{32,44},... | collective-permute-start | bytes 12296 | tf_op jit(solution)/shard_map/ppermute | solution.py:210
  90.4 4.9 %collective-permute-start.10 = (f32[8,128]{1,0:T(8,128)S(1)}, f32[8,128]{1,0:T(8,128)S(1)}, u32[]{:S(2)}, u32[]{:S(2)}) collective-permute-start(f32[8,128]{1,0:T(8,128)S(1)} %add_add_fusion.1), channel_id=1, source_target_pairs={{0,48},{4,52},{8,56},{12,60},{16,32},{20,36},{24,40},{28,44},{32,1... | collective-permute-start | bytes 12296 | tf_op jit(solution)/shard_map/ppermute | solution.py:210
  92.4 3.6 %collective-permute-start.8 = (f32[8,128]{1,0:T(8,128)S(1)}, f32[8,128]{1,0:T(8,128)S(1)}, u32[]{:S(2)}, u32[]{:S(2)}) collective-permute-start(f32[8,128]{1,0:T(8,128)S(1)} %add_add_fusion.1), channel_id=1, source_target_pairs={{0,16},{4,20},{8,24},{12,28},{16,0},{20,4},{24,8},{28,12},{32,48},... | collective-permute-start | bytes 12296 | tf_op jit(solution)/shard_map/ppermute | solution.py:210
  93.3 5.1 %collective-permute-start.9 = (f32[8,128]{1,0:T(8,128)S(1)}, f32[8,128]{1,0:T(8,128)S(1)}, u32[]{:S(2)}, u32[]{:S(2)}) collective-permute-start(f32[8,128]{1,0:T(8,128)S(1)} %add_add_fusion.1), channel_id=1, source_target_pairs={{0,32},{4,36},{8,40},{12,44},{16,48},{20,52},{24,56},{28,60},{32,0... | collective-permute-start | bytes 12296 | tf_op jit(solution)/shard_map/ppermute | solution.py:210

commit v3 on v1

--- a/solution.py
+++ b/solution.py
@@ -1,4 +1,3 @@
-import functools
 import math
 
 import jax
@@ -12,11 +11,12 @@
 HALF = 64
 ROPE_BASE = 500000.0
 LOG_ROWS = 16
-TILE = 256
+TILE = 512
 LOG2E = math.log2(math.e)
 
 VMEM = pl.BlockSpec(memory_space=pltpu.VMEM)
 SMEM = pl.BlockSpec(memory_space=pltpu.SMEM)
+HBM = pl.BlockSpec(memory_space=pltpu.HBM)
 f32 = jnp.float32
 bf16 = jnp.bfloat16
 
@@ -33,46 +33,72 @@
     return pltpu.roll(u, HALF, 1)
 
 
-def lane_rates(table_ref, index_row):
-    lane = lax.broadcasted_iota(jnp.int32, (1, HEAD), 1)
-    pair = jnp.where(lane < HALF, lane, lane - HALF).astype(f32)
-    log_factor = jnp.zeros((1, HEAD), f32)
+def half_rates(table_ref, index_row):
+    pair = lax.broadcasted_iota(jnp.int32, (1, HALF), 1).astype(f32)
+    log_factor = jnp.zeros((1, HALF), f32)
     for entry in range(table_ref.shape[1]):
         log_factor = jnp.where(index_row == entry, table_ref[0, entry], log_factor)
     return jnp.exp(-pair * (2.0 / HEAD * math.log(ROPE_BASE)) - log_factor)
 
 
-def before_kernel(order_ref, table_ref, index_ref, q_ref, prior_ref, k_ref, v_ref, do_ref,
-                  out_ref, cos_ref, sin_ref):
-    rows = q_ref.shape[0]
+def before_kernel(order_hbm, table_hbm, index_hbm, q_hbm, k_hbm, v_hbm, prior_hbm, do_hbm,
+                  out_hbm, cos_hbm, sin_hbm,
+                  order_ref, table_ref, index_ref, q_ref, k_ref, prior_ref, do_ref, v_ref, packed_q, packed_k, cos_ref, sin_ref,
+                  in_sems, do_sems, v_sems, q_sems, k_sems, wave_sems):
+    rows, width = q_ref.shape
     half_rows = rows // 2
-    heads = q_ref.shape[1] // HEAD
-    group = q_ref.shape[1] // k_ref.shape[1]
+    heads = width // HEAD
+    group = width // k_ref.shape[1]
+    pairs = ((order_hbm, order_ref), (table_hbm, table_ref), (index_hbm, index_ref),
+             (k_hbm, k_ref), (q_hbm, q_ref), (prior_hbm, prior_ref), (do_hbm, do_ref), (v_hbm, v_ref))
+    copies = [pltpu.make_async_copy(a, b, in_sems.at[i]) for i, (a, b) in enumerate(pairs)]
+    for copy in copies:
+        copy.start()
+    sent = []
+
+    def send(source, head, part, sem):
+        copy = pltpu.make_async_copy(source, out_hbm.at[head, pl.ds(part * rows, rows), :], sem)
+        copy.start()
+        sent.append(copy)
+
+    for copy in copies[:3]:
+        copy.wait()
     me = lax.axis_index("ctx")
-    rate = lane_rates(table_ref, index_ref[...])
-    row = lax.broadcasted_iota(jnp.int32, (rows, HEAD), 0)
+    rate = half_rates(table_ref, index_ref[...])
+    row = lax.broadcasted_iota(jnp.int32, (rows, HALF), 0)
     first, second = order_ref[2 * me] * half_rows, order_ref[2 * me + 1] * half_rows
     position = jnp.where(row < half_rows, first + row, second + row - half_rows).astype(f32)
     angle = position * rate
-    lane = lax.broadcasted_iota(jnp.int32, (rows, HEAD), 1)
     cosine = jnp.cos(angle)
     sine = jnp.sin(angle)
-    signed = jnp.where(lane < HALF, -sine, sine)
+    cosine = jnp.concatenate([cosine, cosine], axis=1)
+    signed = jnp.concatenate([-sine, sine], axis=1)
     cos_ref[...] = cosine
     sin_ref[...] = signed
-    rotated_keys = []
-    for head in range(heads // group):
-        cols = slice(head * HEAD, (head + 1) * HEAD)
-        u = k_ref[:, cols].astype(f32)
-        rotated_keys.append((u * cosine + swap_halves(u) * signed).astype(bf16))
+    for number, (a, b) in enumerate(((cos_ref, cos_hbm), (sin_ref, sin_hbm))):
+        copy = pltpu.make_async_copy(a, b, wave_sems.at[number])
+        copy.start()
+        sent.append(copy)
+    copies[6].wait()
+    copies[7].wait()
+    for head in range(heads):
+        send(do_ref.at[:, pl.ds(head * HEAD, HEAD)], head, 1, do_sems.at[head])
+        send(v_ref.at[:, pl.ds(head // group * HEAD, HEAD)], head, 3, v_sems.at[head])
+    copies[3].wait()
+    for kv in range(heads // group):
+        u = k_ref[:, kv * HEAD:(kv + 1) * HEAD].astype(f32)
+        packed_k[kv] = (u * cosine + swap_halves(u) * signed).astype(bf16)
+        for head in range(kv * group, (kv + 1) * group):
+            send(packed_k.at[kv], head, 2, k_sems.at[head])
+    copies[4].wait()
+    copies[5].wait()
     for head in range(heads):
         cols = slice(head * HEAD, (head + 1) * HEAD)
         u = q_ref[:, cols].astype(f32) + prior_ref[:, cols].astype(f32)
-        out_ref[head, 0:rows] = (u * cosine + swap_halves(u) * signed).astype(bf16)
-        out_ref[head, rows:2 * rows] = do_ref[:, cols]
-        out_ref[head, 2 * rows:3 * rows] = rotated_keys[head // group]
-        kv = head // group
-        out_ref[head, 3 * rows:4 * rows] = v_ref[:, kv * HEAD:(kv + 1) * HEAD]
+        packed_q[head] = (u * cosine + swap_halves(u) * signed).astype(bf16)
+        send(packed_q.at[head], head, 0, q_sems.at[head])
+    for copy in sent:
+        copy.wait()
 
 
 def main_kernel(order_ref, in_ref, out_ref, qs, dos, ks, vs, kt, vt, dk, dv, atts, dqs, s_scr, e_scr, ds_scr):
@@ -102,40 +128,52 @@
         term = gradient * swap_halves(rotated.astype(f32)) * (row_number + base).astype(f32)
         return jnp.sum(term.reshape(TILE // 8, 8, HEAD), axis=0)
 
-    for i in range(tiles):
+    kept = {}
+
+    def scores(i):
         tile = slice(i * TILE, (i + 1) * TILE)
-        seen = (i + 1) * TILE
         q = qs[tile, :]
-        do_t = dos[tile, :].T.astype(f32)
         top = None
         for c in range(i + 1):
             keys = slice(c * TILE, (c + 1) * TILE)
             s = dot_nt(ks[keys, :], q)
             if c == i:
                 s = jnp.where(visible, s, -1e30)
-            s_scr[keys, :] = s
+            s_scr[i % 2, keys, :] = s
             high = jnp.max(s, axis=0, keepdims=True)
             top = high if top is None else jnp.maximum(top, high)
-        top = top * coef
+        kept[i] = top * coef
+
+    def forward(i):
+        tile = slice(i * TILE, (i + 1) * TILE)
+        seen = (i + 1) * TILE
+        top = kept[i]
         total = jnp.zeros((1, TILE), f32)
         for c in range(i + 1):
             keys = slice(c * TILE, (c + 1) * TILE)
-            e = jnp.exp2(s_scr[keys, :] * coef - top)
+            e = jnp.exp2(s_scr[i % 2, keys, :] * coef - top)
             total = total + jnp.sum(e, axis=0, keepdims=True)
-            e_scr[keys, :] = e.astype(bf16)
+            e_scr[i % 2, keys, :] = e.astype(bf16)
         inverse = 1.0 / total
-        o_t = dot(vt[:, :seen], e_scr[:seen, :]) * inverse
+        o_t = dot(vt[:, :seen], e_scr[i % 2, :seen, :]) * inverse
         atts[tile, :] = o_t.T.astype(bf16)
-        do_t = (do_t * inverse).astype(bf16)
+        do_t = (dos[tile, :].T.astype(f32) * inverse).astype(bf16)
         delta = jnp.sum(do_t.astype(f32) * o_t, axis=0, keepdims=True)
+        kept[i] = do_t, delta
+
+    def backward(i):
+        tile = slice(i * TILE, (i + 1) * TILE)
+        seen = (i + 1) * TILE
+        do_t, delta = kept[i]
         do = do_t.T
+        q = qs[tile, :]
         for c in range(i + 1):
             keys = slice(c * TILE, (c + 1) * TILE)
-            e = e_scr[keys, :]
+            e = e_scr[i % 2, keys, :]
             value_part = dot(e, do)
             dp = dot(vs[keys, :], do_t)
             ds = (e.astype(f32) * (dp - delta)).astype(bf16)
-            ds_scr[keys, :] = ds
+            ds_scr[i % 2, keys, :] = ds
             key_part = dot(ds, q)
             if c == i:
                 dv[keys, :] = value_part
@@ -143,9 +181,16 @@
             else:
                 dv[keys, :] += value_part
                 dk[keys, :] += key_part
-        gq = (dot(kt[:, :seen], ds_scr[:seen, :]) * scale).T
+        gq = (dot(kt[:, :seen], ds_scr[i % 2, :seen, :]) * scale).T
         dqs[tile, :] = gq.astype(bf16)
-        angle_sum = angle_sum + weighted(gq, q, i * TILE)
+        return weighted(gq, q, i * TILE)
+
+    scores(0)
+    for i in range(tiles):
+        forward(i)
+        if i + 1 < tiles:
+            scores(i + 1)
+        angle_sum = angle_sum + backward(i)
 
     for i in range(tiles):
         tile = slice(i * TILE, (i + 1) * TILE)
@@ -204,16 +249,32 @@
     tokens = rows * sources
     arriving = lax.ppermute(prior, "pipe", [(i, (i + 1) % pipe) for i in range(pipe)])
     returning = lax.ppermute(later, "pipe", [(i, (i - 1) % pipe) for i in range(pipe)])
-    wide_index = jnp.concatenate([index, index], axis=1)
     params = pltpu.CompilerParams(vmem_limit_bytes=40 * 2**20)
 
     sent, cosine, sine = pl.pallas_call(
         before_kernel,
         out_shape=(shape(heads, 4 * rows, HEAD), shape(rows, HEAD, dtype=f32), shape(rows, HEAD, dtype=f32)),
-        in_specs=[SMEM, SMEM] + [VMEM] * 6,
-        out_specs=[VMEM] * 3,
-        compiler_params=params,
-    )(order, table, wide_index, queries[0, 0], arriving[0, 0], key_rows[0, 0], values[0, 0], returning[0, 0])
+        in_specs=[HBM] * 8,
+        out_specs=[HBM] * 3,
+        scratch_shapes=[
+            pltpu.SMEM(order.shape, jnp.int32),
+            pltpu.SMEM(table.shape, f32),
+            pltpu.VMEM(index.shape, jnp.int32),
+            pltpu.VMEM((rows, width), bf16),
+            pltpu.VMEM((rows, kv_width), bf16),
+            pltpu.VMEM((rows, width), bf16),
+            pltpu.VMEM((rows, width), bf16),
+            pltpu.VMEM((rows, kv_width), bf16),
+            pltpu.VMEM((heads, rows, HEAD), bf16),
+            pltpu.VMEM((kv_width // HEAD, rows, HEAD), bf16),
+            pltpu.VMEM((rows, HEAD), f32),
+            pltpu.VMEM((rows, HEAD), f32),
+            pltpu.SemaphoreType.DMA((8,)),
+        ]
+        + [pltpu.SemaphoreType.DMA((heads,))] * 4
+        + [pltpu.SemaphoreType.DMA((2,))],
+        compiler_params=pltpu.CompilerParams(vmem_limit_bytes=56 * 2**20),
+    )(order, table, index, queries[0, 0], key_rows[0, 0], values[0, 0], arriving[0, 0], returning[0, 0])
 
     held = lax.all_to_all(sent, "ctx", 0, 0)
 
@@ -226,8 +287,8 @@
         + [pltpu.VMEM((HEAD, tokens), bf16)] * 2
         + [pltpu.VMEM((tokens, HEAD), f32)] * 2
         + [pltpu.VMEM((tokens, HEAD), bf16)] * 2
-        + [pltpu.VMEM((tokens, TILE), f32)]
-        + [pltpu.VMEM((tokens, TILE), bf16)] * 2,
+        + [pltpu.VMEM((2, tokens, TILE), f32)]
+        + [pltpu.VMEM((2, tokens, TILE), bf16)] * 2,
         compiler_params=params,
     )(order, held)
 

time: 100 us -> 96.1 us (0.961)
  local copies, waits for them, and re-layouts: 4.17 us -> 0.83 us
  Pallas kernels: 15.2 us -> 14.1 us
    unnamed x14, local copies, waits for them, and re-layouts: 4.17 us -> 0.83 us
    pallas_call x1, Pallas kernels: 12.4 us -> 9.27 us  [on_device(): pl.pallas_call(main_kernel, out_shape=shape(sources, 4 * rows + LOG_ROWS,...]
    pallas_call x1, Pallas kernels: 1.29 us -> 3.39 us  [on_device(): pl.pallas_call(before_kernel, out_shape=(shape(heads, 4 * rows, HEAD), sh...]
  transfers between devices with their start and end apart: 5 -> 5, of which waited for: 3 -> 3; matrix products, arithmetic and copies ran while one was open for 1% -> 0% of each run, Pallas kernels for 1% -> 2%
where the time goes in v3:
time: 96.1 us; the launch traced here: 95.8 us
  blocking collectives  67.6 us (70%)
  Pallas kernels  14.1 us (15%)
  starting transfers between devices  6.16 us (6%)
  waiting for transfers between devices  5.53 us (6%)
    all_to_all x1, blocking collectives, on_device(): held = lax.all_to_all(sent, 'ctx', 0, 0)  35.8 us
    all_to_all x1, blocking collectives, on_device(): back = lax.all_to_all(done, 'ctx', 0, 0)  31.8 us
    pallas_call x1, Pallas kernels, on_device(): pl.pallas_call(main_kernel, out_shape=shape(sources, 4 * rows + LOG_ROWS,...  9.27 us
    ppermute x3, starting transfers between devices, on_device(): lax.ppermute(line, 'dp', [(i, i ^ s) for i in range(dp)])  5.57 us
    pallas_call x1, Pallas kernels, on_device(): pl.pallas_call(before_kernel, out_shape=(shape(heads, 4 * rows, HEAD), sh...  3.39 us
    ppermute x3, waiting for transfers between devices, on_device(): lax.ppermute(line, 'dp', [(i, i ^ s) for i in range(dp)])  3.17 us
  transfers between devices with their start and end apart: 5, of which 3 were waited for; matrix products, arithmetic and copies ran while one was open for 0% of the time, Pallas kernels for 2%

profile of v3, /device:TPU:0, one launch (start us, length us, event | category | flops | bytes accessed | tf_op | source)
XLA Modules:
  0.0 95.8 jit_solution(829447389918697094)
XLA Ops:
  0.6 0.1 collective-permute-start
  0.7 0.5 collective-permute-start.1
  1.2 1.6 %collective-permute-done = bf16[1,1,128,2048]{3,2,1,0:T(8,128)(2,1)S(1)} collective-permute-done((bf16[1,1,128,2048]{3,2,1,0:T(8,128)(2,1)}, bf16[1,1,128,2048]{3,2,1,0:T(8,128)(2,1)S(1)}, u32[]{:S(2)}, u32[]{:S(2)}) %collective-permute-start) | collective-permute-done | bytes 524320 | tf_op jit(solution)/shard_map/ppermute | solution.py:250
  2.8 0.0 copy-start.3
  2.8 0.7 collective-permute-done.1
  3.6 0.0 copy-start.4
  3.6 0.0 copy-done.3
  3.6 0.7 copy-done.4
  4.4 3.4 %shard_map.119 = (bf16[16,512,128]{2,1,0:T(8,128)(2,1)}, f32[128,128]{1,0:T(8,128)}, f32[128,128]{1,0:T(8,128)}) custom-call(s32[32]{0:T(128)} %order_ref.1, f32[1,16]{1,0:T(1,128)} %table_hbm.1, s32[1,64]{1,0:T(1,128)} %index_hbm.1, bf16[128,2048]{1,0:T(8,128)(2,1)} %bitcast.13, bf16[128,512]{1,0:T(8,128)(2,1)} %bitcast.16, bf16[128,512]{1,0:T(8,128)(2,1)} %bitcast.17, ...), custom_call_target="tpu_custom_call" | custom-call | tf_op jit(solution)/shard_map/pallas_call | solution.py:254
  7.8 0.0 copy-start.2
  7.8 35.8 %all_to_all.10.in_ref = bf16[16,512,128]{2,1,0:T(8,128)(2,1)S(1)} all-to-all(bf16[16,512,128]{2,1,0:T(8,128)(2,1)} %get-tuple-element.12), channel_id=1, replica_groups=mesh['pipe'=2,'ctx'=16,'dp'=4] {'ctx'}, dimensions={0} | all-to-all | bytes 4194304 | tf_op jit(solution)/shard_map/all_to_all | solution.py:279
  43.6 0.0 copy-done.2
  43.6 9.3 %shard_map.120 = bf16[16,528,128]{2,1,0:T(8,128)(2,1)S(1)} custom-call(s32[32]{0:T(128)S(1)} %copy-done.2, bf16[16,512,128]{2,1,0:T(8,128)(2,1)S(1)} %all_to_all.10.in_ref), custom_call_target="tpu_custom_call" | custom-call | tf_op jit(solution)/shard_map/pallas_call | solution.py:281
  52.9 0.0 copy-start.5
  52.9 0.0 copy-start.6
  52.9 0.0 copy-start
  52.9 0.0 copy-start.1
  52.9 31.8 %all_to_all.11.in_ref = bf16[16,528,128]{2,1,0:T(8,128)(2,1)S(1)} all-to-all(bf16[16,528,128]{2,1,0:T(8,128)(2,1)S(1)} %shard_map.120), channel_id=1, replica_groups=mesh['pipe'=2,'ctx'=16,'dp'=4] {'ctx'}, dimensions={0} | all-to-all | bytes 4325376 | tf_op jit(solution)/shard_map/all_to_all | solution.py:295
  84.8 2.0 %collective-permute-start.2 = (f32[128]{0:T(128)S(1)}, f32[128]{0:T(128)S(1)}, u32[]{:S(2)}, u32[]{:S(2)}) collective-permute-start(f32[128]{0:T(128)S(1)} %convert_reduce_fusion), channel_id=1, source_target_pairs={{0,1},{1,0},{2,3},{3,2},{4,5},{5,4},{6,7},{7,6},{8,9},{9,8},{10,11... | collective-permute-start | bytes 1544 | tf_op jit(solution)/shard_map/ppermute | solution.py:299
  86.8 3.6 %collective-permute-start.3 = (f32[128]{0:T(128)S(1)}, f32[128]{0:T(128)S(1)}, u32[]{:S(2)}, u32[]{:S(2)}) collective-permute-start(f32[128]{0:T(128)S(1)} %convert_reduce_fusion), channel_id=1, source_target_pairs={{0,2},{1,3},{2,0},{3,1},{4,6},{5,7},{6,4},{7,5},{8,10},{9,11},{10,... | collective-permute-start | bytes 1544 | tf_op jit(solution)/shard_map/ppermute | solution.py:299
  90.4 0.0 collective-permute-start.4
  90.4 0.0 copy-done.5
  90.4 0.0 copy-done.6
  90.4 0.1 select_reduce_fusion.1
  90.5 0.0 copy-done
  90.5 0.0 copy-done.1
  90.5 1.5 %shard_map.121 = (bf16[128,2048]{1,0:T(8,128)(2,1)}, bf16[128,2048]{1,0:T(8,128)(2,1)}, bf16[128,512]{1,0:T(8,128)(2,1)}, bf16[128,512]{1,0:T(8,128)(2,1)}) custom-call(bf16[16,528,128]{2,1,0:T(8,128)(2,1)S(1)} %all_to_all.11.in_ref, f32[128,128]{1,0:T(8,128)S(1)} %copy-done, f32[128,128]{1,0:T(8,128)S(1)} %copy-done.1), custom_call_target="tpu_custom_call" | custom-call | tf_op jit(solution)/shard_map/pallas_call | solution.py:301
  91.9 0.0 collective-permute-done.2
  91.9 0.0 collective-permute-done.3
  91.9 3.2 %collective-permute-done.4 = f32[128]{0:T(128)S(1)} collective-permute-done((f32[128]{0:T(128)S(1)}, f32[128]{0:T(128)S(1)}, u32[]{:S(2)}, u32[]{:S(2)}) %collective-permute-start.4) | collective-permute-done | bytes 544 | tf_op jit(solution)/shard_map/ppermute | solution.py:299
  95.1 0.1 exponential_multiply_fusion
  95.2 0.1 select_reduce_fusion
  95.3 0.5 multiply_bitcast_fusion
  (2 shorter events, 0.0 us)
Async XLA Ops:
  0.6 2.2 %collective-permute-start = (bf16[1,1,128,2048]{3,2,1,0:T(8,128)(2,1)}, bf16[1,1,128,2048]{3,2,1,0:T(8,128)(2,1)S(1)}, u32[]{:S(2)}, u32[]{:S(2)}) collective-permute-start(bf16[1,1,128,2048]{3,2,1,0:T(8,128)(2,1)} %param.11), channel_id=1, source_target_pairs={{0,64},{64,0},{1,65},{65,1},{2,66},{66,2},{3,67},{67,3},{4,68},{68... | collective-permute-start | bytes 1572872 | tf_op jit(solution)/shard_map/ppermute | solution.py:250
  0.7 2.9 %collective-permute-start.1 = (bf16[1,1,128,2048]{3,2,1,0:T(8,128)(2,1)}, bf16[1,1,128,2048]{3,2,1,0:T(8,128)(2,1)S(1)}, u32[]{:S(2)}, u32[]{:S(2)}) collective-permute-start(bf16[1,1,128,2048]{3,2,1,0:T(8,128)(2,1)} %param.12), channel_id=1, source_target_pairs={{0,64},{64,0},{1,65},{65,1},{2,66},{66,2},{3,67},{67,3},{4,68},{68... | collective-permute-start | bytes 1572872 | tf_op jit(solution)/shard_map/ppermute | solution.py:251
  2.8 0.8 copy-start.3
  3.6 0.8 copy-start.4
  7.8 35.8 %copy-start.2 = (s32[32]{0:T(128)S(1)}, s32[32]{0:T(128)}, u32[]{:S(2)}) copy-start(s32[32]{0:T(128)} %order_ref.1) | copy-start | bytes 388
  52.9 37.5 %copy-start.5 = (f32[1,16]{1,0:T(1,128)S(1)}, f32[1,16]{1,0:T(1,128)}, u32[]{:S(2)}) copy-start(f32[1,16]{1,0:T(1,128)} %table_hbm.1) | copy-start | bytes 196
  52.9 37.5 %copy-start.6 = (s32[1,64]{1,0:T(1,128)S(1)}, s32[1,64]{1,0:T(1,128)}, u32[]{:S(2)}) copy-start(s32[1,64]{1,0:T(1,128)} %index_hbm.1) | copy-start | bytes 772
  52.9 37.6 %copy-start = (f32[128,128]{1,0:T(8,128)S(1)}, f32[128,128]{1,0:T(8,128)}, u32[]{:S(2)}) copy-start(f32[128,128]{1,0:T(8,128)} %get-tuple-element.13.cos_ref) | copy-start | bytes 196612
  52.9 37.6 %copy-start.1 = (f32[128,128]{1,0:T(8,128)S(1)}, f32[128,128]{1,0:T(8,128)}, u32[]{:S(2)}) copy-start(f32[128,128]{1,0:T(8,128)} %get-tuple-element.14.sin_ref) | copy-start | bytes 196612
  84.8 7.2 %collective-permute-start.2 = (f32[128]{0:T(128)S(1)}, f32[128]{0:T(128)S(1)}, u32[]{:S(2)}, u32[]{:S(2)}) collective-permute-start(f32[128]{0:T(128)S(1)} %convert_reduce_fusion), channel_id=1, source_target_pairs={{0,1},{1,0},{2,3},{3,2},{4,5},{5,4},{6,7},{7,6},{8,9},{9,8},{10,11... | collective-permute-start | bytes 1544 | tf_op jit(solution)/shard_map/ppermute | solution.py:299
  86.8 5.2 %collective-permute-start.3 = (f32[128]{0:T(128)S(1)}, f32[128]{0:T(128)S(1)}, u32[]{:S(2)}, u32[]{:S(2)}) collective-permute-start(f32[128]{0:T(128)S(1)} %convert_reduce_fusion), channel_id=1, source_target_pairs={{0,2},{1,3},{2,0},{3,1},{4,6},{5,7},{6,4},{7,5},{8,10},{9,11},{10,... | collective-permute-start | bytes 1544 | tf_op jit(solution)/shard_map/ppermute | solution.py:299
  90.4 4.8 %collective-permute-start.4 = (f32[128]{0:T(128)S(1)}, f32[128]{0:T(128)S(1)}, u32[]{:S(2)}, u32[]{:S(2)}) collective-permute-start(f32[128]{0:T(128)S(1)} %convert_reduce_fusion), channel_id=1, source_target_pairs={{0,3},{1,2},{2,1},{3,0},{4,7},{5,6},{6,5},{7,4},{8,11},{9,10},{10,... | collective-permute-start | bytes 1544 | tf_op jit(solution)/shard_map/ppermute | solution.py:299

commit v4 on v3

v4 whole, which is shorter than its diff:
```python
import math

import jax
import jax.numpy as jnp
from jax import lax
from jax.experimental import pallas as pl
from jax.experimental.pallas import tpu as pltpu
from jax.sharding import PartitionSpec as P

HEAD = 128
HALF = 64
ROPE_BASE = 500000.0
LOG_ROWS = 16
TILE = 512
RING = 4
LOG2E = math.log2(math.e)

VMEM = pl.BlockSpec(memory_space=pltpu.VMEM)
SMEM = pl.BlockSpec(memory_space=pltpu.SMEM)
ANY = pl.BlockSpec(memory_space=pl.ANY)
HBM = pl.BlockSpec(memory_space=pltpu.HBM)
f32 = jnp.float32
bf16 = jnp.bfloat16


def dot(a, b):
    return jnp.dot(a, b, preferred_element_type=f32)


def dot_nt(a, b):
    return lax.dot_general(a, b, (((1,), (1,)), ((), ())), preferred_element_type=f32)


def swap_halves(u):
    return pltpu.roll(u, HALF, 1)


def half_rates(table_ref, index_row):
    pair = lax.broadcasted_iota(jnp.int32, (1, HALF), 1).astype(f32)
    log_factor = jnp.zeros((1, HALF), f32)
    for entry in range(table_ref.shape[1]):
        log_factor = jnp.where(index_row == entry, table_ref[0, entry], log_factor)
    return jnp.exp(-pair * (2.0 / HEAD * math.log(ROPE_BASE)) - log_factor)


def before_kernel(order_hbm, table_hbm, index_hbm, q_hbm, k_hbm, v_hbm, prior_hbm, do_hbm,
                  out_hbm, cos_hbm, sin_hbm,
                  order_ref, table_ref, index_ref, q_ref, k_ref, prior_ref, do_ref, v_ref, packed_q, packed_k, cos_ref, sin_ref,
                  in_sems, do_sems, v_sems, q_sems, k_sems, wave_sems):
    rows, width = q_ref.shape
    half_rows = rows // 2
    heads = width // HEAD
    group = width // k_ref.shape[1]
    pairs = ((order_hbm, order_ref), (table_hbm, table_ref), (index_hbm, index_ref),
             (k_hbm, k_ref), (q_hbm, q_ref), (prior_hbm, prior_ref), (do_hbm, do_ref), (v_hbm, v_ref))
    copies = [pltpu.make_async_copy(a, b, in_sems.at[i]) for i, (a, b) in enumerate(pairs)]
    for copy in copies:
        copy.start()
    sent = []

    def send(source, kv, part, sem):
        copy = pltpu.make_async_copy(source, out_hbm.at[kv, pl.ds(part * rows, rows), :], sem)
        copy.start()
        sent.append(copy)

    for copy in copies[:3]:
        copy.wait()
    me = lax.axis_index("ctx")
    rate = half_rates(table_ref, index_ref[...])
    row = lax.broadcasted_iota(jnp.int32, (rows, HALF), 0)
    first, second = order_ref[2 * me] * half_rows, order_ref[2 * me + 1] * half_rows
    position = jnp.where(row < half_rows, first + row, second + row - half_rows).astype(f32)
    angle = position * rate
    cosine = jnp.cos(angle)
    sine = jnp.sin(angle)
    cosine = jnp.concatenate([cosine, cosine], axis=1)
    signed = jnp.concatenate([-sine, sine], axis=1)
    cos_ref[...] = cosine
    sin_ref[...] = signed
    for number, (a, b) in enumerate(((cos_ref, cos_hbm), (sin_ref, sin_hbm))):
        copy = pltpu.make_async_copy(a, b, wave_sems.at[number])
        copy.start()
        sent.append(copy)
    copies[6].wait()
    copies[7].wait()
    for head in range(heads):
        send(do_ref.at[:, pl.ds(head * HEAD, HEAD)], head // group, group + head % group, do_sems.at[head])
    for kv in range(heads // group):
        send(v_ref.at[:, pl.ds(kv * HEAD, HEAD)], kv, 2 * group + 1, v_sems.at[kv])
    copies[3].wait()
    for kv in range(heads // group):
        u = k_ref[:, kv * HEAD:(kv + 1) * HEAD].astype(f32)
        packed_k[kv] = (u * cosine + swap_halves(u) * signed).astype(bf16)
        send(packed_k.at[kv], kv, 2 * group, k_sems.at[kv])
    copies[4].wait()
    copies[5].wait()
    for head in range(heads):
        cols = slice(head * HEAD, (head + 1) * HEAD)
        u = q_ref[:, cols].astype(f32) + prior_ref[:, cols].astype(f32)
        packed_q[head] = (u * cosine + swap_halves(u) * signed).astype(bf16)
        send(packed_q.at[head], head // group, head % group, q_sems.at[head])
    for copy in sent:
        copy.wait()


def placed_at():
    chip = lax.axis_index("ctx")
    core = lax.axis_index("pipe")
    row, column = chip // RING, chip % RING
    return core == 0, jnp.where(core == 0, row, column), jnp.where(core == 0, column, row)


def main_kernel(order_ref, in_ref, own_ref, next_ref, far_ref, last_ref,
                out_ref, grad_own, grad_next, grad_far, grad_last,
                qs, dos, ks, vs, kt, vt, dk, dv, atts, dqs, s_scr, e_scr, ds_scr, angle_ref, place_ref):
    rows = own_ref.shape[1] // 2
    half_rows = rows // 2
    group = in_ref.shape[1] // rows // 2 - 1
    tokens = ks.shape[0]
    block = group * half_rows
    scale = HEAD ** -0.5
    coef = scale * LOG2E
    straight, _, column = placed_at()

    def slot_of(rank, offset, half):
        at = lax.rem(column + offset, RING)
        return order_ref[2 * jnp.where(straight, rank * RING + at, at * RING + rank) + half]

    def half_block(ref, number):
        return ref.at[pl.ds(pl.multiple_of(number * half_rows, half_rows), half_rows), :]

    pieces = [(rank, half) for rank in range(RING) for half in range(2)]
    keys_of = [own_ref, next_ref, far_ref, last_ref]
    for offset, ref in enumerate(keys_of):
        for rank, half in pieces:
            number = slot_of(rank, offset, half)
            half_block(ks, number)[...] = ref[rank, half * half_rows:(half + 1) * half_rows, :]
            half_block(vs, number)[...] = ref[rank, rows + half * half_rows:rows + (half + 1) * half_rows, :]
    places = [slot_of(rank, 0, half) for rank, half in pieces]
    ranks = []
    for place in places:
        above = jnp.int32(0)
        for other in places:
            above = above + jnp.where(other < place, 1, 0)
        ranks.append(above)
        place_ref[above] = place
    for (rank, half), at in zip(pieces, ranks):
        for head in range(group):
            start = head * rows + half * half_rows
            half_block(qs, at * group + head)[...] = in_ref[rank, start:start + half_rows, :]
            start = start + group * rows
            half_block(dos, at * group + head)[...] = in_ref[rank, start:start + half_rows, :]
    kt[...] = ks[...].T
    vt[...] = vs[...].T
    dk[...] = jnp.zeros_like(dk)
    dv[...] = jnp.zeros_like(dv)
    angle_ref[...] = jnp.zeros_like(angle_ref)

    key_iota = lax.broadcasted_iota(jnp.int32, (TILE, TILE), 0)
    lane = lax.broadcasted_iota(jnp.int32, (1, TILE), 1)
    line = lax.broadcasted_iota(jnp.int32, (TILE, 1), 0)
    row_number = lax.broadcasted_iota(jnp.int32, (TILE, HEAD), 0)

    def weighted(gradient, rotated, position):
        term = gradient * swap_halves(rotated.astype(f32)) * position
        return jnp.sum(term.reshape(TILE // 8, 8, HEAD), axis=0)

    def attend(m, chunks):
        low, high = place_ref[2 * m] * half_rows, place_ref[2 * m + 1] * half_rows
        tile = pl.ds(pl.multiple_of(m * TILE, TILE), TILE)
        seen = chunks * TILE
        q = qs[tile, :]
        position = jnp.where(lane < block, low, high) + lax.rem(lane, half_rows)
        top = None
        for c in range(chunks):
            keys = slice(c * TILE, (c + 1) * TILE)
            s = dot_nt(ks[keys, :], q)
            s = jnp.where(key_iota <= position - c * TILE, s, -1e30)
            s_scr[keys, :] = s
            peak = jnp.max(s, axis=0, keepdims=True)
            top = peak if top is None else jnp.maximum(top, peak)
        top = top * coef
        total = jnp.zeros((1, TILE), f32)
        for c in range(chunks):
            keys = slice(c * TILE, (c + 1) * TILE)
            e = jnp.exp2(s_scr[keys, :] * coef - top)
            total = total + jnp.sum(e, axis=0, keepdims=True)
            e_scr[keys, :] = e.astype(bf16)
        inverse = 1.0 / total
        o_t = dot(vt[:, :seen], e_scr[:seen, :]) * inverse
        atts[tile, :] = o_t.T.astype(bf16)
        do_t = (dos[tile, :].T.astype(f32) * inverse).astype(bf16)
        delta = jnp.sum(do_t.astype(f32) * o_t, axis=0, keepdims=True)
        do = do_t.T
        for c in range(chunks):
            keys = slice(c * TILE, (c + 1) * TILE)
            e = e_scr[keys, :]
            dv[keys, :] += dot(e, do)
            dp = dot(vs[keys, :], do_t)
            ds = (e.astype(f32) * (dp - delta)).astype(bf16)
            ds_scr[keys, :] = ds
            dk[keys, :] += dot(ds, q)
        gq = (dot(kt[:, :seen], ds_scr[:seen, :]) * scale).T
        dqs[tile, :] = gq.astype(bf16)
        at = (jnp.where(line < block, low, high) + lax.rem(line, half_rows)).astype(f32)
        angle_ref[...] += weighted(gq, q, at)

    def one_tile(m, carry):
        chunks = place_ref[2 * m + 1] * half_rows // TILE
        for n in range(tokens // TILE):
            @pl.when(chunks == n)
            def _():
                attend(m, n + 1)
        return carry

    lax.fori_loop(0, qs.shape[0] // TILE, one_tile, 0)

    for i in range(tokens // TILE):
        tile = slice(i * TILE, (i + 1) * TILE)
        gk = dk[tile, :] * scale
        dk[tile, :] = gk
        angle_ref[...] += weighted(gk, ks[tile, :], (row_number + i * TILE).astype(f32))

    for (rank, half), at in zip(pieces, ranks):
        for head in range(group):
            start = head * rows + half * half_rows
            out_ref[rank, start:start + half_rows, :] = half_block(atts, at * group + head)[...]
            start = start + group * rows
            out_ref[rank, start:start + half_rows, :] = half_block(dqs, at * group + head)[...]
    packed = split_line(jnp.sum(angle_ref[...], axis=0, keepdims=True))
    for offset, ref in enumerate((grad_own, grad_next, grad_far, grad_last)):
        for rank, half in pieces:
            number = slot_of(rank, offset, half)
            start = half * half_rows
            ref[rank, start:start + half_rows, :] = half_block(dk, number)[...].astype(bf16)
            ref[rank, rows + start:rows + start + half_rows, :] = half_block(dv, number)[...].astype(bf16)
        for rank in range(RING):
            ref[rank, 2 * rows:, :] = packed


def split_line(line):
    high = line.astype(bf16).astype(f32)
    middle = (line - high).astype(bf16).astype(f32)
    low = line - high - middle
    which = lax.broadcasted_iota(jnp.int32, (LOG_ROWS, HEAD), 0)
    packed = jnp.where(which == 0, high, jnp.where(which == 1, middle, jnp.where(which == 2, low, 0.0)))
    return packed.astype(bf16)


def sum_kernel(held_ref, own_ref, next_ref, far_ref, last_ref, out_ref):
    grads = (own_ref, next_ref, far_ref, last_ref)
    size = own_ref.shape[1] - LOG_ROWS
    start = out_ref.shape[1] - LOG_ROWS - size
    for rank in range(RING):
        total = grads[0][rank, :size].astype(f32)
        for ref in grads[1:]:
            total = total + ref[rank, :size].astype(f32)
        out_ref[rank, start:start + size, :] = total.astype(bf16)
    _, _, column = placed_at()
    lines = [jnp.sum(ref[0, size:].astype(f32), axis=0, keepdims=True) for ref in grads]
    line = jnp.zeros((1, HEAD), f32)
    for at in range(RING):
        offset = lax.rem(column - at + RING, RING)
        term = lines[0]
        for number in range(1, RING):
            term = jnp.where(offset == number, lines[number], term)
        line = line + term
    packed = split_line(line)
    for rank in range(RING):
        out_ref[rank, start + size:, :] = packed


def after_kernel(in_ref, cos_ref, sin_ref, att_ref, dq_ref, dk_ref, dv_ref):
    rows = cos_ref.shape[0]
    group = att_ref.shape[1] // dk_ref.shape[1]
    cosine, signed = cos_ref[...], sin_ref[...]

    def back(u):
        u = u.astype(f32)
        return (u * cosine - swap_halves(u) * signed).astype(bf16)

    for kv in range(RING):
        for number in range(group):
            head = kv * group + number
            cols = slice(head * HEAD, (head + 1) * HEAD)
            att_ref[:, cols] = in_ref[kv, number * rows:(number + 1) * rows]
            dq_ref[:, cols] = back(in_ref[kv, (group + number) * rows:(group + number + 1) * rows])
        cols = slice(kv * HEAD, (kv + 1) * HEAD)
        start = 2 * group * rows
        dk_ref[:, cols] = back(in_ref[kv, start:start + rows])
        dv_ref[:, cols] = in_ref[kv, start + rows:start + 2 * rows]


def shape(*dims, dtype=bf16):
    return jax.ShapeDtypeStruct(dims, dtype)


def on_device(queries, key_rows, values, prior, later, order, table, index):
    rows, width = queries.shape[2:]
    kv_width = key_rows.shape[3]
    heads = width // HEAD
    sources = lax.axis_size("ctx")
    pipe = lax.axis_size("pipe")
    tokens = rows * sources
    group = width // kv_width
    arriving = lax.ppermute(prior, "pipe", [(i, (i + 1) % pipe) for i in range(pipe)])
    returning = lax.ppermute(later, "pipe", [(i, (i - 1) % pipe) for i in range(pipe)])
    params = pltpu.CompilerParams(vmem_limit_bytes=40 * 2**20)
    both = ("pipe", "ctx")

    def device(core, rank, column):
        return core * sources + (rank * RING + column if core == 0 else column * RING + rank)

    heads_over = [[device(core, rank, column) for rank in range(RING)]
                  for core in range(pipe) for column in range(RING)]

    def moved(value, by):
        pairs = [(device(core, rank, column), device(core, rank, (column + by) % RING))
                 for core in range(pipe) for rank in range(RING) for column in range(RING)]
        return lax.ppermute(value, both, pairs)

    sent, cosine, sine = pl.pallas_call(
        before_kernel,
        out_shape=(shape(RING, 2 * (group + 1) * rows, HEAD), shape(rows, HEAD, dtype=f32), shape(rows, HEAD, dtype=f32)),
        in_specs=[HBM] * 8,
        out_specs=[HBM] * 3,
        scratch_shapes=[
            pltpu.SMEM(order.shape, jnp.int32),
            pltpu.SMEM(table.shape, f32),
            pltpu.VMEM(index.shape, jnp.int32),
            pltpu.VMEM((rows, width), bf16),
            pltpu.VMEM((rows, kv_width), bf16),
            pltpu.VMEM((rows, width), bf16),
            pltpu.VMEM((rows, width), bf16),
            pltpu.VMEM((rows, kv_width), bf16),
            pltpu.VMEM((heads, rows, HEAD), bf16),
            pltpu.VMEM((kv_width // HEAD, rows, HEAD), bf16),
            pltpu.VMEM((rows, HEAD), f32),
            pltpu.VMEM((rows, HEAD), f32),
            pltpu.SemaphoreType.DMA((8,)),
        ]
        + [pltpu.SemaphoreType.DMA((heads,))] * 4
        + [pltpu.SemaphoreType.DMA((2,))],
        compiler_params=pltpu.CompilerParams(vmem_limit_bytes=56 * 2**20),
    )(order, table, index, queries[0, 0], key_rows[0, 0], values[0, 0], arriving[0, 0], returning[0, 0])

    held = lax.all_to_all(sent, both, 0, 0, axis_index_groups=heads_over)
    own = held[:, 2 * group * rows:, :]
    others = [moved(own, RING - offset) for offset in range(1, RING)]

    grads = shape(RING, 2 * rows + LOG_ROWS, HEAD)
    done, *grads = pl.pallas_call(
        main_kernel,
        out_shape=[shape(RING, 2 * (group + 1) * rows + LOG_ROWS, HEAD)] + [grads] * RING,
        in_specs=[SMEM] + [VMEM] * (1 + RING),
        out_specs=[VMEM] * (1 + RING),
        scratch_shapes=[pltpu.VMEM((tokens, HEAD), bf16)] * 4
        + [pltpu.VMEM((HEAD, tokens), bf16)] * 2
        + [pltpu.VMEM((tokens, HEAD), f32)] * 2
        + [pltpu.VMEM((tokens, HEAD), bf16)] * 2
        + [pltpu.VMEM((tokens, TILE), f32)]
        + [pltpu.VMEM((tokens, TILE), bf16)] * 2
        + [pltpu.VMEM((8, HEAD), f32), pltpu.SMEM((2 * RING,), jnp.int32)],
        compiler_params=params,
    )(order, held, own, *others)
    arrived = [moved(grads[offset], offset) for offset in range(1, RING)]
    done = pl.pallas_call(
        sum_kernel,
        out_shape=shape(*done.shape),
        in_specs=[ANY] + [VMEM] * RING,
        out_specs=VMEM,
        input_output_aliases={0: 0},
        compiler_params=params,
    )(done, grads[0], *arrived)
    back = lax.all_to_all(done, both, 0, 0, axis_index_groups=heads_over)

    line = jnp.sum(back[:, -LOG_ROWS:-LOG_ROWS + 3, :].astype(f32), axis=(0, 1))
    dp = lax.axis_size("dp")
    terms = [lax.ppermute(line, "dp", [(i, i ^ s) for i in range(dp)]) for s in range(1, dp)]

    attended, dq, dk, dv = pl.pallas_call(
        after_kernel,
        out_shape=(shape(rows, width), shape(rows, width), shape(rows, kv_width), shape(rows, kv_width)),
        in_specs=[VMEM] * 3,
        out_specs=[VMEM] * 4,
        compiler_params=params,
    )(back, cosine, sine)

    level = [line] + terms
    while len(level) > 1:
        level = [a + b for a, b in zip(level[0::2], level[1::2])]
    line = level[0]
    base = ROPE_BASE ** (-(jnp.arange(HALF, dtype=f32) * 2.0 / HEAD))
    onehot = (index[0][:, None] == jnp.arange(table.shape[1], dtype=jnp.int32)[None, :]).astype(f32)
    log_factor = jnp.sum(onehot * table[0][None, :], axis=1)
    log_gradient = (line[:HALF] - line[HALF:]) * base * jnp.exp(-log_factor)
    table_grad = jnp.sum(onehot * log_gradient[:, None], axis=0) / (tokens * dp)
    return attended[None, None], dq[None, None], dk[None, None], dv[None, None], table_grad[None, :]


def solution(mesh):
    block = P("pipe", "dp", "ctx", None)
    return jax.shard_map(
        on_device,
        mesh=mesh,
        in_specs=(block,) * 5 + (P(), P("pipe", None), P("pipe", None)),
        out_specs=(block,) * 4 + (P("pipe", None),),
        check_vma=False,
    )
```

time: 96.1 us -> 88.9 us (0.925)
  blocking collectives: 67.6 us -> 31.8 us
  waiting for transfers between devices: 5.53 us -> 20.8 us
  starting transfers between devices: 6.16 us -> 15.7 us
  Pallas kernels: 14.1 us -> 17.4 us
    all_to_all x2, blocking collectives: 67.6 us -> 31.8 us  [the longest x1 16.9 us: on_device(): held = lax.all_to_all(sent, both, 0, 0, axis_index_groups=heads_over)]
    ppermute x0 -> x6, waiting for transfers between devices: none -> 16.5 us  [moved(): return lax.ppermute(value, both, pairs)]
    ppermute x0 -> x6, starting transfers between devices: none -> 9.43 us  [moved(): return lax.ppermute(value, both, pairs)]
    pallas_call x2 -> x3, Pallas kernels: 12.7 us -> 15.9 us  [the longest x1 12.6 us: on_device(): pl.pallas_call(main_kernel, out_shape=[shape(RING, 2 * (group + 1) * rows...]
    ppermute x3, waiting for transfers between devices: 3.17 us -> 1.96 us  [on_device(): lax.ppermute(line, 'dp', [(i, i ^ s) for i in range(dp)])]
  transfers between devices with their start and end apart: 5 -> 11, of which waited for: 3 -> 9; matrix products, arithmetic and copies ran while one was open for 0% -> 0% of each run, Pallas kernels for 2% -> 2%
where the time goes in v4:
time: 88.9 us; the launch traced here: 88 us
  blocking collectives  31.8 us (36%)
  waiting for transfers between devices  20.8 us (23%)
  Pallas kernels  17.4 us (20%)
  starting transfers between devices  15.7 us (18%)
    all_to_all x1, blocking collectives, on_device(): held = lax.all_to_all(sent, both, 0, 0, axis_index_groups=heads_over)  16.9 us
    ppermute x6, waiting for transfers between devices, moved(): return lax.ppermute(value, both, pairs)  16.5 us
    all_to_all x1, blocking collectives, on_device(): back = lax.all_to_all(done, both, 0, 0, axis_index_groups=heads_over)  14.9 us
    pallas_call x1, Pallas kernels, on_device(): pl.pallas_call(main_kernel, out_shape=[shape(RING, 2 * (group + 1) * rows...  12.6 us
    ppermute x6, starting transfers between devices, moved(): return lax.ppermute(value, both, pairs)  9.43 us
    ppermute x3, starting transfers between devices, on_device(): lax.ppermute(line, 'dp', [(i, i ^ s) for i in range(dp)])  5.66 us
    pallas_call x1, Pallas kernels, on_device(): pl.pallas_call(before_kernel, out_shape=(shape(RING, 2 * (group + 1) * ro...  3.18 us
    ppermute x3, waiting for transfers between devices, on_device(): lax.ppermute(line, 'dp', [(i, i ^ s) for i in range(dp)])  1.96 us
  transfers between devices with their start and end apart: 11, of which 9 were waited for; matrix products, arithmetic and copies ran while one was open for 0% of the time, Pallas kernels for 2%

profile of v4, /device:TPU:0, one launch (start us, length us, event | category | flops | bytes accessed | tf_op | source)
XLA Modules:
  0.0 88.0 jit_solution(12128989063128660886)
XLA Ops:
  0.6 0.1 collective-permute-start
  0.7 0.5 collective-permute-start.1
  1.2 1.6 %collective-permute-done = bf16[1,1,128,2048]{3,2,1,0:T(8,128)(2,1)S(1)} collective-permute-done((bf16[1,1,128,2048]{3,2,1,0:T(8,128)(2,1)}, bf16[1,1,128,2048]{3,2,1,0:T(8,128)(2,1)S(1)}, u32[]{:S(2)}, u32[]{:S(2)}) %collective-permute-start) | collective-permute-done | bytes 524320 | tf_op jit(solution)/shard_map/ppermute | solution.py:306
  2.8 0.0 copy-start.3
  2.8 0.7 collective-permute-done.1
  3.6 0.0 copy-start.4
  3.6 0.0 copy-done.3
  3.6 0.7 copy-done.4
  4.4 3.2 %shard_map.119 = (bf16[4,1280,128]{2,1,0:T(8,128)(2,1)}, f32[128,128]{1,0:T(8,128)}, f32[128,128]{1,0:T(8,128)}) custom-call(s32[32]{0:T(128)} %order_ref.1, f32[1,16]{1,0:T(1,128)} %table_hbm.1, s32[1,64]{1,0:T(1,128)} %index_hbm.1, bf16[128,2048]{1,0:T(8,128)(2,1)} %bitcast.13, bf16[128,512]{1,0:T(8,128)(2,1)} %bitcast.16, bf16[128,512]{1,0:T(8,128)(2,1)} %bitcast.17, ...), custom_call_target="tpu_custom_call" | custom-call | tf_op jit(solution)/shard_map/pallas_call | solution.py:322
  7.6 0.0 copy-start.2
  7.6 16.9 %all_to_all.10.in_ref = bf16[4,1280,128]{2,1,0:T(8,128)(2,1)S(1)} all-to-all(bf16[4,1280,128]{2,1,0:T(8,128)(2,1)} %get-tuple-element.17), channel_id=1, replica_groups={{0,16,32,48},{4,20,36,52},{8,24,40,56},{12,28,44,60},{64,68,72,76},{80,..., dimensions={0} | all-to-all | bytes 2621440 | tf_op jit(solution)/shard_map/all_to_all | solution.py:347
  24.5 2.8 %collective-permute-start.2 = (bf16[4,256,128]{2,1,0:T(8,128)(2,1)S(1)}, bf16[4,256,128]{2,1,0:T(8,128)(2,1)S(1)}, u32[]{:S(2)}, u32[]{:S(2)}) collective-permute-start(bf16[4,256,128]{2,1,0:T(8,128)(2,1)S(1)} %slice.16.own_ref), channel_id=1, source_target_pairs={{0,12},{4,0},{8,4},{12,8},{16,28},{20,16},{24,20},{28,24},{32,44},... | collective-permute-start | bytes 786440 | tf_op jit(solution)/shard_map/ppermute | solution.py:320
  27.3 0.8 collective-permute-start.3
  28.1 0.9 %collective-permute-start.4 = (bf16[4,256,128]{2,1,0:T(8,128)(2,1)S(1)}, bf16[4,256,128]{2,1,0:T(8,128)(2,1)S(1)}, u32[]{:S(2)}, u32[]{:S(2)}) collective-permute-start(bf16[4,256,128]{2,1,0:T(8,128)(2,1)S(1)} %slice.16.own_ref), channel_id=1, source_target_pairs={{0,4},{4,8},{8,12},{12,0},{16,20},{20,24},{24,28},{28,16},{32,36},... | collective-permute-start | bytes 786440 | tf_op jit(solution)/shard_map/ppermute | solution.py:320
  29.0 5.0 %collective-permute-done.2.next_ref = bf16[4,256,128]{2,1,0:T(8,128)(2,1)S(1)} collective-permute-done((bf16[4,256,128]{2,1,0:T(8,128)(2,1)S(1)}, bf16[4,256,128]{2,1,0:T(8,128)(2,1)S(1)}, u32[]{:S(2)}, u32[]{:S(2)}) %collective-permute-start.2) | collective-permute-done | bytes 262176 | tf_op jit(solution)/shard_map/ppermute | solution.py:320
  34.0 1.2 %collective-permute-done.3.far_ref = bf16[4,256,128]{2,1,0:T(8,128)(2,1)S(1)} collective-permute-done((bf16[4,256,128]{2,1,0:T(8,128)(2,1)S(1)}, bf16[4,256,128]{2,1,0:T(8,128)(2,1)S(1)}, u32[]{:S(2)}, u32[]{:S(2)}) %collective-permute-start.3) | collective-permute-done | bytes 262176 | tf_op jit(solution)/shard_map/ppermute | solution.py:320
  35.3 2.7 %collective-permute-done.4.last_ref = bf16[4,256,128]{2,1,0:T(8,128)(2,1)S(1)} collective-permute-done((bf16[4,256,128]{2,1,0:T(8,128)(2,1)S(1)}, bf16[4,256,128]{2,1,0:T(8,128)(2,1)S(1)}, u32[]{:S(2)}, u32[]{:S(2)}) %collective-permute-start.4) | collective-permute-done | bytes 262176 | tf_op jit(solution)/shard_map/ppermute | solution.py:320
  38.0 0.0 copy-done.2
  38.0 12.6 %shard_map.120 = (bf16[4,1296,128]{2,1,0:T(8,128)(2,1)S(1)}, bf16[4,272,128]{2,1,0:T(8,128)(2,1)S(1)}, bf16[4,272,128]{2,1,0:T(8,128)(2,1)S(1)}, bf16[4,272,128]...) custom-call(s32[32]{0:T(128)S(1)} %copy-done.2, bf16[4,1280,128]{2,1,0:T(8,128)(2,1)S(1)} %all_to_all.10.in_ref, ...), custom_call_target="tpu_custom_call" | custom-call | tf_op jit(solution)/shard_map/pallas_call | solution.py:352
  50.6 2.1 %collective-permute-start.5 = (bf16[4,272,128]{2,1,0:T(8,128)(2,1)S(1)}, bf16[4,272,128]{2,1,0:T(8,128)(2,1)S(1)}, u32[]{:S(2)}, u32[]{:S(2)}) collective-permute-start(bf16[4,272,128]{2,1,0:T(8,128)(2,1)S(1)} %get-tuple-element.20), channel_id=1, source_target_pairs={{0,4},{4,8},{8,12},{12,0},{16,20},{20,24},{24,28},{28,16},{32,36},... | collective-permute-start | bytes 835592 | tf_op jit(solution)/shard_map/ppermute | solution.py:320
  52.7 2.8 %collective-permute-start.6 = (bf16[4,272,128]{2,1,0:T(8,128)(2,1)S(1)}, bf16[4,272,128]{2,1,0:T(8,128)(2,1)S(1)}, u32[]{:S(2)}, u32[]{:S(2)}) collective-permute-start(bf16[4,272,128]{2,1,0:T(8,128)(2,1)S(1)} %get-tuple-element.21), channel_id=1, source_target_pairs={{0,8},{4,12},{8,0},{12,4},{16,24},{20,28},{24,16},{28,20},{32,40},... | collective-permute-start | bytes 835592 | tf_op jit(solution)/shard_map/ppermute | solution.py:320
  55.5 0.0 collective-permute-start.7
  55.5 3.1 %collective-permute-done.5.next_ref = bf16[4,272,128]{2,1,0:T(8,128)(2,1)S(1)} collective-permute-done((bf16[4,272,128]{2,1,0:T(8,128)(2,1)S(1)}, bf16[4,272,128]{2,1,0:T(8,128)(2,1)S(1)}, u32[]{:S(2)}, u32[]{:S(2)}) %collective-permute-start.5) | collective-permute-done | bytes 278560 | tf_op jit(solution)/shard_map/ppermute | solution.py:320
  58.6 4.4 %collective-permute-done.6.far_ref = bf16[4,272,128]{2,1,0:T(8,128)(2,1)S(1)} collective-permute-done((bf16[4,272,128]{2,1,0:T(8,128)(2,1)S(1)}, bf16[4,272,128]{2,1,0:T(8,128)(2,1)S(1)}, u32[]{:S(2)}, u32[]{:S(2)}) %collective-permute-start.6) | collective-permute-done | bytes 278560 | tf_op jit(solution)/shard_map/ppermute | solution.py:320
  63.0 0.0 collective-permute-done.7.last_ref
  63.0 0.2 shard_map.121
  63.2 0.0 copy-start.5
  63.2 0.0 copy-start.6
  63.2 0.0 copy-start
  63.2 0.0 copy-start.1
  63.2 14.9 %all_to_all.11.in_ref = bf16[4,1296,128]{2,1,0:T(8,128)(2,1)S(1)} all-to-all(bf16[4,1296,128]{2,1,0:T(8,128)(2,1)S(1)} %shard_map.121), channel_id=1, replica_groups={{0,16,32,48},{4,20,36,52},{8,24,40,56},{12,28,44,60},{64,68,72,76},{80,..., dimensions={0} | all-to-all | bytes 2654208 | tf_op jit(solution)/shard_map/all_to_all | solution.py:375
  78.2 4.1 %collective-permute-start.10 = (f32[128]{0:T(128)S(1)}, f32[128]{0:T(128)S(1)}, u32[]{:S(2)}, u32[]{:S(2)}) collective-permute-start(f32[128]{0:T(128)S(1)} %convert_reduce_fusion), channel_id=1, source_target_pairs={{0,3},{1,2},{2,1},{3,0},{4,7},{5,6},{6,5},{7,4},{8,11},{9,10},{10,... | collective-permute-start | bytes 1544 | tf_op jit(solution)/shard_map/ppermute | solution.py:379
  82.3 0.0 collective-permute-start.8
  82.3 1.6 %collective-permute-start.9 = (f32[128]{0:T(128)S(1)}, f32[128]{0:T(128)S(1)}, u32[]{:S(2)}, u32[]{:S(2)}) collective-permute-start(f32[128]{0:T(128)S(1)} %convert_reduce_fusion), channel_id=1, source_target_pairs={{0,2},{1,3},{2,0},{3,1},{4,6},{5,7},{6,4},{7,5},{8,10},{9,11},{10,... | collective-permute-start | bytes 1544 | tf_op jit(solution)/shard_map/ppermute | solution.py:379
  83.8 0.0 copy-done.5
  83.8 0.0 copy-done.6
  83.8 0.1 select_reduce_fusion.1
  83.9 0.0 copy-done
  83.9 0.0 copy-done.1
  83.9 1.4 %shard_map.122 = (bf16[128,2048]{1,0:T(8,128)(2,1)}, bf16[128,2048]{1,0:T(8,128)(2,1)}, bf16[128,512]{1,0:T(8,128)(2,1)}, bf16[128,512]{1,0:T(8,128)(2,1)}) custom-call(bf16[4,1296,128]{2,1,0:T(8,128)(2,1)S(1)} %all_to_all.11.in_ref, f32[128,128]{1,0:T(8,128)S(1)} %copy-done, f32[128,128]{1,0:T(8,128)S(1)} %copy-done.1), custom_call_target="tpu_custom_call" | custom-call | tf_op jit(solution)/shard_map/pallas_call | solution.py:381
  85.4 0.0 collective-permute-done.10
  85.4 0.4 collective-permute-done.8
  85.8 1.5 %collective-permute-done.9 = f32[128]{0:T(128)S(1)} collective-permute-done((f32[128]{0:T(128)S(1)}, f32[128]{0:T(128)S(1)}, u32[]{:S(2)}, u32[]{:S(2)}) %collective-permute-start.9) | collective-permute-done | bytes 544 | tf_op jit(solution)/shard_map/ppermute | solution.py:379
  87.3 0.1 exponential_multiply_fusion
  87.4 0.1 select_reduce_fusion
  87.5 0.5 multiply_bitcast_fusion
  (3 shorter events, 0.0 us)
Async XLA Ops:
  0.6 2.2 %collective-permute-start = (bf16[1,1,128,2048]{3,2,1,0:T(8,128)(2,1)}, bf16[1,1,128,2048]{3,2,1,0:T(8,128)(2,1)S(1)}, u32[]{:S(2)}, u32[]{:S(2)}) collective-permute-start(bf16[1,1,128,2048]{3,2,1,0:T(8,128)(2,1)} %param.11), channel_id=1, source_target_pairs={{0,64},{64,0},{1,65},{65,1},{2,66},{66,2},{3,67},{67,3},{4,68},{68... | collective-permute-start | bytes 1572872 | tf_op jit(solution)/shard_map/ppermute | solution.py:306
  0.7 2.9 %collective-permute-start.1 = (bf16[1,1,128,2048]{3,2,1,0:T(8,128)(2,1)}, bf16[1,1,128,2048]{3,2,1,0:T(8,128)(2,1)S(1)}, u32[]{:S(2)}, u32[]{:S(2)}) collective-permute-start(bf16[1,1,128,2048]{3,2,1,0:T(8,128)(2,1)} %param.12), channel_id=1, source_target_pairs={{0,64},{64,0},{1,65},{65,1},{2,66},{66,2},{3,67},{67,3},{4,68},{68... | collective-permute-start | bytes 1572872 | tf_op jit(solution)/shard_map/ppermute | solution.py:307
  2.8 0.8 copy-start.3
  3.6 0.8 copy-start.4
  7.6 30.4 %copy-start.2 = (s32[32]{0:T(128)S(1)}, s32[32]{0:T(128)}, u32[]{:S(2)}) copy-start(s32[32]{0:T(128)} %order_ref.1) | copy-start | bytes 388
  24.5 9.6 %collective-permute-start.2 = (bf16[4,256,128]{2,1,0:T(8,128)(2,1)S(1)}, bf16[4,256,128]{2,1,0:T(8,128)(2,1)S(1)}, u32[]{:S(2)}, u32[]{:S(2)}) collective-permute-start(bf16[4,256,128]{2,1,0:T(8,128)(2,1)S(1)} %slice.16.own_ref), channel_id=1, source_target_pairs={{0,12},{4,0},{8,4},{12,8},{16,28},{20,16},{24,20},{28,24},{32,44},... | collective-permute-start | bytes 786440 | tf_op jit(solution)/shard_map/ppermute | solution.py:320
  27.3 8.0 %collective-permute-start.3 = (bf16[4,256,128]{2,1,0:T(8,128)(2,1)S(1)}, bf16[4,256,128]{2,1,0:T(8,128)(2,1)S(1)}, u32[]{:S(2)}, u32[]{:S(2)}) collective-permute-start(bf16[4,256,128]{2,1,0:T(8,128)(2,1)S(1)} %slice.16.own_ref), channel_id=1, source_target_pairs={{0,8},{4,12},{8,0},{12,4},{16,24},{20,28},{24,16},{28,20},{32,40},... | collective-permute-start | bytes 786440 | tf_op jit(solution)/shard_map/ppermute | solution.py:320
  28.1 9.9 %collective-permute-start.4 = (bf16[4,256,128]{2,1,0:T(8,128)(2,1)S(1)}, bf16[4,256,128]{2,1,0:T(8,128)(2,1)S(1)}, u32[]{:S(2)}, u32[]{:S(2)}) collective-permute-start(bf16[4,256,128]{2,1,0:T(8,128)(2,1)S(1)} %slice.16.own_ref), channel_id=1, source_target_pairs={{0,4},{4,8},{8,12},{12,0},{16,20},{20,24},{24,28},{28,16},{32,36},... | collective-permute-start | bytes 786440 | tf_op jit(solution)/shard_map/ppermute | solution.py:320
  50.6 8.0 %collective-permute-start.5 = (bf16[4,272,128]{2,1,0:T(8,128)(2,1)S(1)}, bf16[4,272,128]{2,1,0:T(8,128)(2,1)S(1)}, u32[]{:S(2)}, u32[]{:S(2)}) collective-permute-start(bf16[4,272,128]{2,1,0:T(8,128)(2,1)S(1)} %get-tuple-element.20), channel_id=1, source_target_pairs={{0,4},{4,8},{8,12},{12,0},{16,20},{20,24},{24,28},{28,16},{32,36},... | collective-permute-start | bytes 835592 | tf_op jit(solution)/shard_map/ppermute | solution.py:320
  52.7 10.3 %collective-permute-start.6 = (bf16[4,272,128]{2,1,0:T(8,128)(2,1)S(1)}, bf16[4,272,128]{2,1,0:T(8,128)(2,1)S(1)}, u32[]{:S(2)}, u32[]{:S(2)}) collective-permute-start(bf16[4,272,128]{2,1,0:T(8,128)(2,1)S(1)} %get-tuple-element.21), channel_id=1, source_target_pairs={{0,8},{4,12},{8,0},{12,4},{16,24},{20,28},{24,16},{28,20},{32,40},... | collective-permute-start | bytes 835592 | tf_op jit(solution)/shard_map/ppermute | solution.py:320
  55.5 7.5 %collective-permute-start.7 = (bf16[4,272,128]{2,1,0:T(8,128)(2,1)S(1)}, bf16[4,272,128]{2,1,0:T(8,128)(2,1)S(1)}, u32[]{:S(2)}, u32[]{:S(2)}) collective-permute-start(bf16[4,272,128]{2,1,0:T(8,128)(2,1)S(1)} %get-tuple-element.22), channel_id=1, source_target_pairs={{0,12},{4,0},{8,4},{12,8},{16,28},{20,16},{24,20},{28,24},{32,44},... | collective-permute-start | bytes 835592 | tf_op jit(solution)/shard_map/ppermute | solution.py:320
  63.2 20.7 %copy-start.5 = (f32[1,16]{1,0:T(1,128)S(1)}, f32[1,16]{1,0:T(1,128)}, u32[]{:S(2)}) copy-start(f32[1,16]{1,0:T(1,128)} %table_hbm.1) | copy-start | bytes 196
  63.2 20.6 %copy-start.6 = (s32[1,64]{1,0:T(1,128)S(1)}, s32[1,64]{1,0:T(1,128)}, u32[]{:S(2)}) copy-start(s32[1,64]{1,0:T(1,128)} %index_hbm.1) | copy-start | bytes 772
  63.2 20.7 %copy-start = (f32[128,128]{1,0:T(8,128)S(1)}, f32[128,128]{1,0:T(8,128)}, u32[]{:S(2)}) copy-start(f32[128,128]{1,0:T(8,128)} %get-tuple-element.23.cos_ref) | copy-start | bytes 196612
  63.2 20.7 %copy-start.1 = (f32[128,128]{1,0:T(8,128)S(1)}, f32[128,128]{1,0:T(8,128)}, u32[]{:S(2)}) copy-start(f32[128,128]{1,0:T(8,128)} %get-tuple-element.24.sin_ref) | copy-start | bytes 196612
  78.2 7.2 %collective-permute-start.10 = (f32[128]{0:T(128)S(1)}, f32[128]{0:T(128)S(1)}, u32[]{:S(2)}, u32[]{:S(2)}) collective-permute-start(f32[128]{0:T(128)S(1)} %convert_reduce_fusion), channel_id=1, source_target_pairs={{0,3},{1,2},{2,1},{3,0},{4,7},{5,6},{6,5},{7,4},{8,11},{9,10},{10,... | collective-permute-start | bytes 1544 | tf_op jit(solution)/shard_map/ppermute | solution.py:379
  82.3 3.5 %collective-permute-start.8 = (f32[128]{0:T(128)S(1)}, f32[128]{0:T(128)S(1)}, u32[]{:S(2)}, u32[]{:S(2)}) collective-permute-start(f32[128]{0:T(128)S(1)} %convert_reduce_fusion), channel_id=1, source_target_pairs={{0,1},{1,0},{2,3},{3,2},{4,5},{5,4},{6,7},{7,6},{8,9},{9,8},{10,11... | collective-permute-start | bytes 1544 | tf_op jit(solution)/shard_map/ppermute | solution.py:379
  82.3 5.0 %collective-permute-start.9 = (f32[128]{0:T(128)S(1)}, f32[128]{0:T(128)S(1)}, u32[]{:S(2)}, u32[]{:S(2)}) collective-permute-start(f32[128]{0:T(128)S(1)} %convert_reduce_fusion), channel_id=1, source_target_pairs={{0,2},{1,3},{2,0},{3,1},{4,6},{5,7},{6,4},{7,5},{8,10},{9,11},{10,... | collective-permute-start | bytes 1544 | tf_op jit(solution)/shard_map/ppermute | solution.py:379

commit v5 on v4

--- a/solution.py
+++ b/solution.py
@@ -43,23 +43,22 @@
     return jnp.exp(-pair * (2.0 / HEAD * math.log(ROPE_BASE)) - log_factor)
 
 
-def before_kernel(order_hbm, table_hbm, index_hbm, q_hbm, k_hbm, v_hbm, prior_hbm, do_hbm,
-                  out_hbm, cos_hbm, sin_hbm,
-                  order_ref, table_ref, index_ref, q_ref, k_ref, prior_ref, do_ref, v_ref, packed_q, packed_k, cos_ref, sin_ref,
-                  in_sems, do_sems, v_sems, q_sems, k_sems, wave_sems):
-    rows, width = q_ref.shape
+def first_kernel(order_hbm, table_hbm, index_hbm, k_hbm, v_hbm,
+                 out_hbm, cos_hbm, sin_hbm,
+                 order_ref, table_ref, index_ref, k_ref, v_ref, packed_k, cos_ref, sin_ref,
+                 in_sems, v_sems, k_sems, wave_sems):
+    rows = k_ref.shape[0]
     half_rows = rows // 2
-    heads = width // HEAD
-    group = width // k_ref.shape[1]
-    pairs = ((order_hbm, order_ref), (table_hbm, table_ref), (index_hbm, index_ref),
-             (k_hbm, k_ref), (q_hbm, q_ref), (prior_hbm, prior_ref), (do_hbm, do_ref), (v_hbm, v_ref))
+    kv_heads = k_ref.shape[1] // HEAD
+    start = out_hbm.shape[1] - 2 * rows
+    pairs = ((order_hbm, order_ref), (table_hbm, table_ref), (index_hbm, index_ref), (k_hbm, k_ref), (v_hbm, v_ref))
     copies = [pltpu.make_async_copy(a, b, in_sems.at[i]) for i, (a, b) in enumerate(pairs)]
     for copy in copies:
         copy.start()
     sent = []
 
-    def send(source, kv, part, sem):
-        copy = pltpu.make_async_copy(source, out_hbm.at[kv, pl.ds(part * rows, rows), :], sem)
+    def send(source, to, sem):
+        copy = pltpu.make_async_copy(source, to, sem)
         copy.start()
         sent.append(copy)
 
@@ -77,28 +76,52 @@
     signed = jnp.concatenate([-sine, sine], axis=1)
     cos_ref[...] = cosine
     sin_ref[...] = signed
-    for number, (a, b) in enumerate(((cos_ref, cos_hbm), (sin_ref, sin_hbm))):
-        copy = pltpu.make_async_copy(a, b, wave_sems.at[number])
+    send(cos_ref, cos_hbm, wave_sems.at[0])
+    send(sin_ref, sin_hbm, wave_sems.at[1])
+    copies[3].wait()
+    copies[4].wait()
+    for kv in range(kv_heads):
+        cols = slice(kv * HEAD, (kv + 1) * HEAD)
+        send(v_ref.at[:, pl.ds(kv * HEAD, HEAD)], out_hbm.at[kv, pl.ds(start + rows, rows), :], v_sems.at[kv])
+        u = k_ref[:, cols].astype(f32)
+        packed_k[kv] = (u * cosine + swap_halves(u) * signed).astype(bf16)
+        send(packed_k.at[kv], out_hbm.at[kv, pl.ds(start, rows), :], k_sems.at[kv])
+    for copy in sent:
+        copy.wait()
+
+
+def second_kernel(held_hbm, cos_hbm, sin_hbm, q_hbm, prior_hbm, do_hbm, out_hbm,
+                  cos_ref, sin_ref, q_ref, prior_ref, do_ref, packed_q, in_sems, do_sems, q_sems):
+    rows, width = q_ref.shape
+    heads = width // HEAD
+    group = heads // out_hbm.shape[0]
+    copies = [pltpu.make_async_copy(cos_hbm, cos_ref, in_sems.at[0]), pltpu.make_async_copy(sin_hbm, sin_ref, in_sems.at[1])]
+    for kv in range(heads // group):
+        cols = pl.ds(kv * group * HEAD, group * HEAD)
+        for a, b in ((q_hbm, q_ref), (prior_hbm, prior_ref), (do_hbm, do_ref)):
+            copies.append(pltpu.make_async_copy(a.at[:, cols], b.at[:, cols], in_sems.at[len(copies)]))
+    for copy in copies:
+        copy.start()
+    sent = []
+
+    def send(source, head, part, sem):
+        to = out_hbm.at[head // group, pl.ds((part * group + head % group) * rows, rows), :]
+        copy = pltpu.make_async_copy(source, to, sem)
         copy.start()
         sent.append(copy)
-    copies[6].wait()
-    copies[7].wait()
-    for head in range(heads):
-        send(do_ref.at[:, pl.ds(head * HEAD, HEAD)], head // group, group + head % group, do_sems.at[head])
-    for kv in range(heads // group):
-        send(v_ref.at[:, pl.ds(kv * HEAD, HEAD)], kv, 2 * group + 1, v_sems.at[kv])
-    copies[3].wait()
-    for kv in range(heads // group):
-        u = k_ref[:, kv * HEAD:(kv + 1) * HEAD].astype(f32)
-        packed_k[kv] = (u * cosine + swap_halves(u) * signed).astype(bf16)
-        send(packed_k.at[kv], kv, 2 * group, k_sems.at[kv])
-    copies[4].wait()
-    copies[5].wait()
+
+    for copy in copies[:2]:
+        copy.wait()
+    cosine, signed = cos_ref[...], sin_ref[...]
     for head in range(heads):
         cols = slice(head * HEAD, (head + 1) * HEAD)
+        if head % group == 0:
+            for copy in copies[2 + 3 * (head // group):5 + 3 * (head // group)]:
+                copy.wait()
         u = q_ref[:, cols].astype(f32) + prior_ref[:, cols].astype(f32)
         packed_q[head] = (u * cosine + swap_halves(u) * signed).astype(bf16)
-        send(packed_q.at[head], head // group, head % group, q_sems.at[head])
+        send(packed_q.at[head], head, 0, q_sems.at[head])
+        send(do_ref.at[:, pl.ds(head * HEAD, HEAD)], head, 1, do_sems.at[head])
     for copy in sent:
         copy.wait()
 
@@ -319,30 +342,44 @@
                  for core in range(pipe) for rank in range(RING) for column in range(RING)]
         return lax.ppermute(value, both, pairs)
 
+    payload = shape(RING, 2 * (group + 1) * rows, HEAD)
+    wave = shape(rows, HEAD, dtype=f32)
+    wide = pltpu.CompilerParams(vmem_limit_bytes=56 * 2**20)
+    wave_buffer = pltpu.VMEM((rows, HEAD), f32)
+    kv_buffer = pltpu.VMEM((rows, kv_width), bf16)
+    buffer = pltpu.VMEM((rows, width), bf16)
     sent, cosine, sine = pl.pallas_call(
-        before_kernel,
-        out_shape=(shape(RING, 2 * (group + 1) * rows, HEAD), shape(rows, HEAD, dtype=f32), shape(rows, HEAD, dtype=f32)),
-        in_specs=[HBM] * 8,
+        first_kernel,
+        out_shape=(payload, wave, wave),
+        in_specs=[HBM] * 5,
         out_specs=[HBM] * 3,
         scratch_shapes=[
             pltpu.SMEM(order.shape, jnp.int32),
             pltpu.SMEM(table.shape, f32),
             pltpu.VMEM(index.shape, jnp.int32),
-            pltpu.VMEM((rows, width), bf16),
-            pltpu.VMEM((rows, kv_width), bf16),
-            pltpu.VMEM((rows, width), bf16),
-            pltpu.VMEM((rows, width), bf16),
-            pltpu.VMEM((rows, kv_width), bf16),
-            pltpu.VMEM((heads, rows, HEAD), bf16),
-            pltpu.VMEM((kv_width // HEAD, rows, HEAD), bf16),
-            pltpu.VMEM((rows, HEAD), f32),
-            pltpu.VMEM((rows, HEAD), f32),
-            pltpu.SemaphoreType.DMA((8,)),
-        ]
-        + [pltpu.SemaphoreType.DMA((heads,))] * 4
-        + [pltpu.SemaphoreType.DMA((2,))],
-        compiler_params=pltpu.CompilerParams(vmem_limit_bytes=56 * 2**20),
-    )(order, table, index, queries[0, 0], key_rows[0, 0], values[0, 0], arriving[0, 0], returning[0, 0])
+            kv_buffer,
+            kv_buffer,
+            pltpu.VMEM((RING, rows, HEAD), bf16),
+            wave_buffer,
+            wave_buffer,
+            pltpu.SemaphoreType.DMA((5,)),
+            pltpu.SemaphoreType.DMA((RING,)),
+            pltpu.SemaphoreType.DMA((RING,)),
+            pltpu.SemaphoreType.DMA((2,)),
+        ],
+        compiler_params=wide,
+        cost_estimate=pl.CostEstimate(flops=10**7, bytes_accessed=4 * 10**6, transcendentals=0),
+    )(order, table, index, key_rows[0, 0], values[0, 0])
+    sent = pl.pallas_call(
+        second_kernel,
+        out_shape=payload,
+        in_specs=[HBM] * 6,
+        out_specs=HBM,
+        scratch_shapes=[wave_buffer, wave_buffer, buffer, buffer, buffer, pltpu.VMEM((heads, rows, HEAD), bf16)]
+        + [pltpu.SemaphoreType.DMA((2 + 3 * RING,))] + [pltpu.SemaphoreType.DMA((heads,))] * 2,
+        input_output_aliases={0: 0},
+        compiler_params=wide,
+    )(sent, cosine, sine, queries[0, 0], arriving[0, 0], returning[0, 0])
 
     held = lax.all_to_all(sent, both, 0, 0, axis_index_groups=heads_over)
     own = held[:, 2 * group * rows:, :]

time: 88.9 us -> 89 us (level); the launches traced: 88 us -> 89.7 us
  Pallas kernels: 17.4 us -> 21.6 us
  starting transfers between devices: 15.7 us -> 14.1 us
  waiting for transfers between devices: 20.8 us -> 19.8 us
    pallas_call x1, Pallas kernels: 12.6 us -> 15.4 us  [on_device(): pl.pallas_call(main_kernel, out_shape=[shape(RING, 2 * (group + 1) * rows...]
    ppermute x6, starting transfers between devices: 9.43 us -> 7.81 us  [moved(): return lax.ppermute(value, both, pairs)]
    ppermute x1, waiting for transfers between devices: 1.61 us -> 0.01 us  [on_device(): lax.ppermute(prior, 'pipe', [(i, (i + 1) % pipe) for i in range(pipe)])]
    pallas_call x1 -> x2, Pallas kernels: 3.18 us -> 4.66 us  [the longest x1 2.76 us: on_device(): pl.pallas_call(second_kernel, out_shape=payload, in_specs=[HBM] * 6, out_...]
    ppermute x6, waiting for transfers between devices: 16.5 us -> 17.4 us  [moved(): return lax.ppermute(value, both, pairs)]
  transfers between devices with their start and end apart: 11 -> 11, of which waited for: 9 -> 8; matrix products, arithmetic and copies ran while one was open for 0% -> 0% of each run, Pallas kernels for 2% -> 4%
where the time goes in v5:
time: 89 us; the launch traced here: 89.7 us
  blocking collectives  31.8 us (36%)
  Pallas kernels  21.6 us (24%)
  waiting for transfers between devices  19.8 us (22%)
  starting transfers between devices  14.1 us (16%)
    ppermute x6, waiting for transfers between devices, moved(): return lax.ppermute(value, both, pairs)  17.4 us
    all_to_all x1, blocking collectives, on_device(): held = lax.all_to_all(sent, both, 0, 0, axis_index_groups=heads_over)  16.9 us
    pallas_call x1, Pallas kernels, on_device(): pl.pallas_call(main_kernel, out_shape=[shape(RING, 2 * (group + 1) * rows...  15.4 us
    all_to_all x1, blocking collectives, on_device(): back = lax.all_to_all(done, both, 0, 0, axis_index_groups=heads_over)  14.9 us
    ppermute x6, starting transfers between devices, moved(): return lax.ppermute(value, both, pairs)  7.81 us
    ppermute x3, starting transfers between devices, on_device(): lax.ppermute(line, 'dp', [(i, i ^ s) for i in range(dp)])  5.66 us
    pallas_call x1, Pallas kernels, on_device(): pl.pallas_call(second_kernel, out_shape=payload, in_specs=[HBM] * 6, out_...  2.76 us
    ppermute x3, waiting for transfers between devices, on_device(): lax.ppermute(line, 'dp', [(i, i ^ s) for i in range(dp)])  1.96 us
  transfers between devices with their start and end apart: 11, of which 8 were waited for; matrix products, arithmetic and copies ran while one was open for 0% of the time, Pallas kernels for 4%

profile of v5, /device:TPU:0, one launch (start us, length us, event | category | flops | bytes accessed | tf_op | source)
XLA Modules:
  0.0 89.7 jit_solution(11319480137840397414)
XLA Ops:
  0.6 0.1 collective-permute-start
  0.7 0.5 collective-permute-start.1
  1.2 1.9 %shard_map.119 = (bf16[4,1280,128]{2,1,0:T(8,128)(2,1)}, f32[128,128]{1,0:T(8,128)}, f32[128,128]{1,0:T(8,128)}) custom-call(s32[32]{0:T(128)} %order_ref.1, f32[1,16]{1,0:T(1,128)} %table_hbm.1, s32[1,64]{1,0:T(1,128)} %index_hbm.1, bf16[128,512]{1,0:T(8,128)(2,1)} %bitcast.16, bf16[128,512]{1,0:T(8,128)(2,1)} %bitcast.17), custom_call_target="tpu_custom_call" | custom-call | flops 10000000 | bytes 4000000 | tf_op jit(solution)/shard_map/pallas_call | solution.py:351
  3.1 0.0 collective-permute-done
  3.1 0.0 copy-start.3
  3.2 0.4 collective-permute-done.1
  3.6 0.0 copy-start.4
  3.6 0.4 copy-done.3
  3.9 0.4 copy-done.4
  4.4 2.8 %shard_map.120 = bf16[4,1280,128]{2,1,0:T(8,128)(2,1)} custom-call(bf16[4,1280,128]{2,1,0:T(8,128)(2,1)} %get-tuple-element.17.held_hbm, f32[128,128]{1,0:T(8,128)} %get-tuple-element.18.cos_hbm.cos_ref, f32[128,128]{1,0:T(8,128)} %get-tuple-element.19.sin_hbm.sin_ref, bf16[128,2048]{1,0:T(8,128)(2,1)} %bitcast.13, ...), custom_call_target="tpu_custom_call", output_to_operand_aliasing={{}: (0, {})} | custom-call | tf_op jit(solution)/shard_map/pallas_call | solution.py:373
  7.1 0.0 copy-start.2
  7.2 16.9 %all_to_all.10.in_ref = bf16[4,1280,128]{2,1,0:T(8,128)(2,1)S(1)} all-to-all(bf16[4,1280,128]{2,1,0:T(8,128)(2,1)} %shard_map.120), channel_id=1, replica_groups={{0,16,32,48},{4,20,36,52},{8,24,40,56},{12,28,44,60},{64,68,72,76},{80,..., dimensions={0} | all-to-all | bytes 2621440 | tf_op jit(solution)/shard_map/all_to_all | solution.py:384
  24.0 2.8 %collective-permute-start.2 = (bf16[4,256,128]{2,1,0:T(8,128)(2,1)S(1)}, bf16[4,256,128]{2,1,0:T(8,128)(2,1)S(1)}, u32[]{:S(2)}, u32[]{:S(2)}) collective-permute-start(bf16[4,256,128]{2,1,0:T(8,128)(2,1)S(1)} %slice.16.own_ref), channel_id=1, source_target_pairs={{0,12},{4,0},{8,4},{12,8},{16,28},{20,16},{24,20},{28,24},{32,44},... | collective-permute-start | bytes 786440 | tf_op jit(solution)/shard_map/ppermute | solution.py:343
  26.9 0.8 collective-permute-start.3
  27.7 0.9 collective-permute-start.4
  28.5 5.0 %collective-permute-done.2.next_ref = bf16[4,256,128]{2,1,0:T(8,128)(2,1)S(1)} collective-permute-done((bf16[4,256,128]{2,1,0:T(8,128)(2,1)S(1)}, bf16[4,256,128]{2,1,0:T(8,128)(2,1)S(1)}, u32[]{:S(2)}, u32[]{:S(2)}) %collective-permute-start.2) | collective-permute-done | bytes 262176 | tf_op jit(solution)/shard_map/ppermute | solution.py:343
  33.6 1.2 %collective-permute-done.3.far_ref = bf16[4,256,128]{2,1,0:T(8,128)(2,1)S(1)} collective-permute-done((bf16[4,256,128]{2,1,0:T(8,128)(2,1)S(1)}, bf16[4,256,128]{2,1,0:T(8,128)(2,1)S(1)}, u32[]{:S(2)}, u32[]{:S(2)}) %collective-permute-start.3) | collective-permute-done | bytes 262176 | tf_op jit(solution)/shard_map/ppermute | solution.py:343
  34.8 2.7 %collective-permute-done.4.last_ref = bf16[4,256,128]{2,1,0:T(8,128)(2,1)S(1)} collective-permute-done((bf16[4,256,128]{2,1,0:T(8,128)(2,1)S(1)}, bf16[4,256,128]{2,1,0:T(8,128)(2,1)S(1)}, u32[]{:S(2)}, u32[]{:S(2)}) %collective-permute-start.4) | collective-permute-done | bytes 262176 | tf_op jit(solution)/shard_map/ppermute | solution.py:343
  37.5 0.0 copy-done.2
  37.5 15.4 %shard_map.121 = (bf16[4,1296,128]{2,1,0:T(8,128)(2,1)S(1)}, bf16[4,272,128]{2,1,0:T(8,128)(2,1)S(1)}, bf16[4,272,128]{2,1,0:T(8,128)(2,1)S(1)}, bf16[4,272,128]...) custom-call(s32[32]{0:T(128)S(1)} %copy-done.2, bf16[4,1280,128]{2,1,0:T(8,128)(2,1)S(1)} %all_to_all.10.in_ref, ...), custom_call_target="tpu_custom_call" | custom-call | tf_op jit(solution)/shard_map/pallas_call | solution.py:389
  52.9 0.1 collective-permute-start.5
  53.0 0.1 collective-permute-start.6
  53.1 3.1 %collective-permute-start.7 = (bf16[4,272,128]{2,1,0:T(8,128)(2,1)S(1)}, bf16[4,272,128]{2,1,0:T(8,128)(2,1)S(1)}, u32[]{:S(2)}, u32[]{:S(2)}) collective-permute-start(bf16[4,272,128]{2,1,0:T(8,128)(2,1)S(1)} %get-tuple-element.24), channel_id=1, source_target_pairs={{0,12},{4,0},{8,4},{12,8},{16,28},{20,16},{24,20},{28,24},{32,44},... | collective-permute-start | bytes 835592 | tf_op jit(solution)/shard_map/ppermute | solution.py:343
  56.2 7.5 %collective-permute-done.5.next_ref = bf16[4,272,128]{2,1,0:T(8,128)(2,1)S(1)} collective-permute-done((bf16[4,272,128]{2,1,0:T(8,128)(2,1)S(1)}, bf16[4,272,128]{2,1,0:T(8,128)(2,1)S(1)}, u32[]{:S(2)}, u32[]{:S(2)}) %collective-permute-start.5) | collective-permute-done | bytes 278560 | tf_op jit(solution)/shard_map/ppermute | solution.py:343
  63.7 0.0 collective-permute-done.6.far_ref
  63.8 0.9 %collective-permute-done.7.last_ref = bf16[4,272,128]{2,1,0:T(8,128)(2,1)S(1)} collective-permute-done((bf16[4,272,128]{2,1,0:T(8,128)(2,1)S(1)}, bf16[4,272,128]{2,1,0:T(8,128)(2,1)S(1)}, u32[]{:S(2)}, u32[]{:S(2)}) %collective-permute-start.7) | collective-permute-done | bytes 278560 | tf_op jit(solution)/shard_map/ppermute | solution.py:343
  64.6 0.2 shard_map.122
  64.8 0.0 copy-start.5
  64.8 0.0 copy-start.6
  64.8 0.0 copy-start
  64.8 0.0 copy-start.1
  64.8 14.9 %all_to_all.11.in_ref = bf16[4,1296,128]{2,1,0:T(8,128)(2,1)S(1)} all-to-all(bf16[4,1296,128]{2,1,0:T(8,128)(2,1)S(1)} %shard_map.122), channel_id=1, replica_groups={{0,16,32,48},{4,20,36,52},{8,24,40,56},{12,28,44,60},{64,68,72,76},{80,..., dimensions={0} | all-to-all | bytes 2654208 | tf_op jit(solution)/shard_map/all_to_all | solution.py:412
  79.8 4.1 %collective-permute-start.10 = (f32[128]{0:T(128)S(1)}, f32[128]{0:T(128)S(1)}, u32[]{:S(2)}, u32[]{:S(2)}) collective-permute-start(f32[128]{0:T(128)S(1)} %convert_reduce_fusion), channel_id=1, source_target_pairs={{0,3},{1,2},{2,1},{3,0},{4,7},{5,6},{6,5},{7,4},{8,11},{9,10},{10,... | collective-permute-start | bytes 1544 | tf_op jit(solution)/shard_map/ppermute | solution.py:416
  83.9 0.0 collective-permute-start.8
  83.9 1.6 %collective-permute-start.9 = (f32[128]{0:T(128)S(1)}, f32[128]{0:T(128)S(1)}, u32[]{:S(2)}, u32[]{:S(2)}) collective-permute-start(f32[128]{0:T(128)S(1)} %convert_reduce_fusion), channel_id=1, source_target_pairs={{0,2},{1,3},{2,0},{3,1},{4,6},{5,7},{6,4},{7,5},{8,10},{9,11},{10,... | collective-permute-start | bytes 1544 | tf_op jit(solution)/shard_map/ppermute | solution.py:416
  85.5 0.0 copy-done.5
  85.5 0.0 copy-done.6
  85.5 0.1 select_reduce_fusion.1
  85.5 0.0 copy-done
  85.5 0.0 copy-done.1
  85.6 1.4 %shard_map.123 = (bf16[128,2048]{1,0:T(8,128)(2,1)}, bf16[128,2048]{1,0:T(8,128)(2,1)}, bf16[128,512]{1,0:T(8,128)(2,1)}, bf16[128,512]{1,0:T(8,128)(2,1)}) custom-call(bf16[4,1296,128]{2,1,0:T(8,128)(2,1)S(1)} %all_to_all.11.in_ref, f32[128,128]{1,0:T(8,128)S(1)} %copy-done, f32[128,128]{1,0:T(8,128)S(1)} %copy-done.1), custom_call_target="tpu_custom_call" | custom-call | tf_op jit(solution)/shard_map/pallas_call | solution.py:418
  87.0 0.0 collective-permute-done.10
  87.0 0.4 collective-permute-done.8
  87.4 1.5 %collective-permute-done.9 = f32[128]{0:T(128)S(1)} collective-permute-done((f32[128]{0:T(128)S(1)}, f32[128]{0:T(128)S(1)}, u32[]{:S(2)}, u32[]{:S(2)}) %collective-permute-start.9) | collective-permute-done | bytes 544 | tf_op jit(solution)/shard_map/ppermute | solution.py:416
  88.9 0.1 exponential_multiply_fusion
  89.0 0.1 select_reduce_fusion
  89.1 0.5 multiply_bitcast_fusion
  (3 shorter events, 0.0 us)
Async XLA Ops:
  0.6 2.5 %collective-permute-start = (bf16[1,1,128,2048]{3,2,1,0:T(8,128)(2,1)}, bf16[1,1,128,2048]{3,2,1,0:T(8,128)(2,1)S(1)}, u32[]{:S(2)}, u32[]{:S(2)}) collective-permute-start(bf16[1,1,128,2048]{3,2,1,0:T(8,128)(2,1)} %param.11), channel_id=1, source_target_pairs={{0,64},{64,0},{1,65},{65,1},{2,66},{66,2},{3,67},{67,3},{4,68},{68... | collective-permute-start | bytes 1572872 | tf_op jit(solution)/shard_map/ppermute | solution.py:329
  0.7 2.9 %collective-permute-start.1 = (bf16[1,1,128,2048]{3,2,1,0:T(8,128)(2,1)}, bf16[1,1,128,2048]{3,2,1,0:T(8,128)(2,1)S(1)}, u32[]{:S(2)}, u32[]{:S(2)}) collective-permute-start(bf16[1,1,128,2048]{3,2,1,0:T(8,128)(2,1)} %param.12), channel_id=1, source_target_pairs={{0,64},{64,0},{1,65},{65,1},{2,66},{66,2},{3,67},{67,3},{4,68},{68... | collective-permute-start | bytes 1572872 | tf_op jit(solution)/shard_map/ppermute | solution.py:330
  3.1 0.8 copy-start.3
  3.6 0.8 copy-start.4
  7.1 30.4 %copy-start.2 = (s32[32]{0:T(128)S(1)}, s32[32]{0:T(128)}, u32[]{:S(2)}) copy-start(s32[32]{0:T(128)} %order_ref.1) | copy-start | bytes 388
  24.0 9.6 %collective-permute-start.2 = (bf16[4,256,128]{2,1,0:T(8,128)(2,1)S(1)}, bf16[4,256,128]{2,1,0:T(8,128)(2,1)S(1)}, u32[]{:S(2)}, u32[]{:S(2)}) collective-permute-start(bf16[4,256,128]{2,1,0:T(8,128)(2,1)S(1)} %slice.16.own_ref), channel_id=1, source_target_pairs={{0,12},{4,0},{8,4},{12,8},{16,28},{20,16},{24,20},{28,24},{32,44},... | collective-permute-start | bytes 786440 | tf_op jit(solution)/shard_map/ppermute | solution.py:343
  26.9 8.0 %collective-permute-start.3 = (bf16[4,256,128]{2,1,0:T(8,128)(2,1)S(1)}, bf16[4,256,128]{2,1,0:T(8,128)(2,1)S(1)}, u32[]{:S(2)}, u32[]{:S(2)}) collective-permute-start(bf16[4,256,128]{2,1,0:T(8,128)(2,1)S(1)} %slice.16.own_ref), channel_id=1, source_target_pairs={{0,8},{4,12},{8,0},{12,4},{16,24},{20,28},{24,16},{28,20},{32,40},... | collective-permute-start | bytes 786440 | tf_op jit(solution)/shard_map/ppermute | solution.py:343
  27.7 9.9 %collective-permute-start.4 = (bf16[4,256,128]{2,1,0:T(8,128)(2,1)S(1)}, bf16[4,256,128]{2,1,0:T(8,128)(2,1)S(1)}, u32[]{:S(2)}, u32[]{:S(2)}) collective-permute-start(bf16[4,256,128]{2,1,0:T(8,128)(2,1)S(1)} %slice.16.own_ref), channel_id=1, source_target_pairs={{0,4},{4,8},{8,12},{12,0},{16,20},{20,24},{24,28},{28,16},{32,36},... | collective-permute-start | bytes 786440 | tf_op jit(solution)/shard_map/ppermute | solution.py:343
  52.9 10.8 %collective-permute-start.5 = (bf16[4,272,128]{2,1,0:T(8,128)(2,1)S(1)}, bf16[4,272,128]{2,1,0:T(8,128)(2,1)S(1)}, u32[]{:S(2)}, u32[]{:S(2)}) collective-permute-start(bf16[4,272,128]{2,1,0:T(8,128)(2,1)S(1)} %get-tuple-element.22), channel_id=1, source_target_pairs={{0,4},{4,8},{8,12},{12,0},{16,20},{20,24},{24,28},{28,16},{32,36},... | collective-permute-start | bytes 835592 | tf_op jit(solution)/shard_map/ppermute | solution.py:343
  53.0 10.7 %collective-permute-start.6 = (bf16[4,272,128]{2,1,0:T(8,128)(2,1)S(1)}, bf16[4,272,128]{2,1,0:T(8,128)(2,1)S(1)}, u32[]{:S(2)}, u32[]{:S(2)}) collective-permute-start(bf16[4,272,128]{2,1,0:T(8,128)(2,1)S(1)} %get-tuple-element.23), channel_id=1, source_target_pairs={{0,8},{4,12},{8,0},{12,4},{16,24},{20,28},{24,16},{28,20},{32,40},... | collective-permute-start | bytes 835592 | tf_op jit(solution)/shard_map/ppermute | solution.py:343
  53.1 11.5 %collective-permute-start.7 = (bf16[4,272,128]{2,1,0:T(8,128)(2,1)S(1)}, bf16[4,272,128]{2,1,0:T(8,128)(2,1)S(1)}, u32[]{:S(2)}, u32[]{:S(2)}) collective-permute-start(bf16[4,272,128]{2,1,0:T(8,128)(2,1)S(1)} %get-tuple-element.24), channel_id=1, source_target_pairs={{0,12},{4,0},{8,4},{12,8},{16,28},{20,16},{24,20},{28,24},{32,44},... | collective-permute-start | bytes 835592 | tf_op jit(solution)/shard_map/ppermute | solution.py:343
  64.8 20.7 %copy-start.5 = (f32[1,16]{1,0:T(1,128)S(1)}, f32[1,16]{1,0:T(1,128)}, u32[]{:S(2)}) copy-start(f32[1,16]{1,0:T(1,128)} %table_hbm.1) | copy-start | bytes 196
  64.8 20.6 %copy-start.6 = (s32[1,64]{1,0:T(1,128)S(1)}, s32[1,64]{1,0:T(1,128)}, u32[]{:S(2)}) copy-start(s32[1,64]{1,0:T(1,128)} %index_hbm.1) | copy-start | bytes 772
  64.8 20.7 %copy-start = (f32[128,128]{1,0:T(8,128)S(1)}, f32[128,128]{1,0:T(8,128)}, u32[]{:S(2)}) copy-start(f32[128,128]{1,0:T(8,128)} %get-tuple-element.18.cos_hbm.cos_ref) | copy-start | bytes 196612
  64.8 20.7 %copy-start.1 = (f32[128,128]{1,0:T(8,128)S(1)}, f32[128,128]{1,0:T(8,128)}, u32[]{:S(2)}) copy-start(f32[128,128]{1,0:T(8,128)} %get-tuple-element.19.sin_hbm.sin_ref) | copy-start | bytes 196612
  79.8 7.2 %collective-permute-start.10 = (f32[128]{0:T(128)S(1)}, f32[128]{0:T(128)S(1)}, u32[]{:S(2)}, u32[]{:S(2)}) collective-permute-start(f32[128]{0:T(128)S(1)} %convert_reduce_fusion), channel_id=1, source_target_pairs={{0,3},{1,2},{2,1},{3,0},{4,7},{5,6},{6,5},{7,4},{8,11},{9,10},{10,... | collective-permute-start | bytes 1544 | tf_op jit(solution)/shard_map/ppermute | solution.py:416
  83.9 3.5 %collective-permute-start.8 = (f32[128]{0:T(128)S(1)}, f32[128]{0:T(128)S(1)}, u32[]{:S(2)}, u32[]{:S(2)}) collective-permute-start(f32[128]{0:T(128)S(1)} %convert_reduce_fusion), channel_id=1, source_target_pairs={{0,1},{1,0},{2,3},{3,2},{4,5},{5,4},{6,7},{7,6},{8,9},{9,8},{10,11... | collective-permute-start | bytes 1544 | tf_op jit(solution)/shard_map/ppermute | solution.py:416
  83.9 5.0 %collective-permute-start.9 = (f32[128]{0:T(128)S(1)}, f32[128]{0:T(128)S(1)}, u32[]{:S(2)}, u32[]{:S(2)}) collective-permute-start(f32[128]{0:T(128)S(1)} %convert_reduce_fusion), channel_id=1, source_target_pairs={{0,2},{1,3},{2,0},{3,1},{4,6},{5,7},{6,4},{7,5},{8,10},{9,11},{10,... | collective-permute-start | bytes 1544 | tf_op jit(solution)/shard_map/ppermute | solution.py:416
